TPU v7x, 128 devices: a whole 4x4x4 slice. The times are simulated.
128 devices in a mesh: seg: 4 (over x), doc: 32 (over y, z, core).
Axes of the slice: x: 4, y: 4, z: 4, core: 2. Of those that a mesh axis runs over, the one named last changes fastest.
Arguments:
- tokens: bfloat16 [64, 512, 512], P('doc', 'seg'), may hold values from -6 to 6
- memory_start: bfloat16 [64, 64, 512], P('doc'), may hold values from -6 to 6
- doc_lengths: int32 [64, 8], P('doc'), may hold values from 1 to 448, 480 in all within a row
- attn_weights: bfloat16 [3, 4, 512, 512], replicated, as said below
- ffn_in: bfloat16 [512, 2048], replicated, may hold values from -0.25 to 0.25
- ffn_out: bfloat16 [2048, 512], replicated, may hold values from -0.125 to 0.125
- gains: float32 [5, 512], replicated, may hold values from 0.5 to 1.5
- forget_w: float32 [512], replicated, may hold values from -0.25 to 0.25
- forget_bias: float32 [64], replicated, may hold values from 1 to 3
- out_cotangent: bfloat16 [64, 512, 512], P('doc', 'seg'), may hold values from -6 to 6
- memory_cotangent: bfloat16 [64, 256, 512], P('doc', 'seg'), may hold values from -6 to 6
Outputs:
- activations: bfloat16 [64, 512, 512], P('doc', 'seg')
- memories: bfloat16 [64, 256, 512], P('doc', 'seg')
- grad_tokens: float32 [64, 512, 512], P('doc', 'seg')
- grad_memory: float32 [64, 256, 512], P('doc', 'seg')
- grad_attn: float32 [3, 4, 512, 512], replicated
- grad_ffn_in: float32 [512, 2048], replicated
- grad_ffn_out: float32 [2048, 512], replicated
- grad_gains: float32 [5, 512], replicated
- grad_forget_w: float32 [512], replicated
- grad_forget_bias: float32 [64], replicated
Inputs may be any that keep to these rules, and one draw needn't show every extreme that they name: `doc_lengths`: each row sums to 480 and holds one document of 448 tokens. `attn_weights`: independent entries of scale 512 ** -0.5, the output projections four times that.
All inputs are finite; a program needn't handle non-finite values.
Results may differ from a plain program's by a relative error of at most 0.025.
Values may be sent and summed in bfloat16 or wider, within the bound.
A program may use at most 384 MiB of HBM per device.

v0:
```python
import math

import jax
import jax.numpy as jnp
from jax import lax
from jax.sharding import PartitionSpec as P

HEADS = 8
NDOC = 8


def shifted(value, axis, steps):
    count = lax.axis_size(axis)
    first, last = (max(0, -steps), min(count, count - steps))
    return lax.ppermute(value, axis, [(source, source + steps) for source in range(first, last)])


def make_layer():

    def round_value(v):
        return lax.optimization_barrier(v.astype(jnp.bfloat16)).astype(jnp.float32)

    low = jax.custom_vjp(round_value)

    def low_keep(v):
        return (low(v), None)

    def low_pass(kept, grad):
        return (grad,)

    low.defvjp(low_keep, low_pass)

    def keep_value(v):
        return v

    low_back = jax.custom_vjp(keep_value)

    def back_keep(v):
        return (v, None)

    def back_low(kept, grad):
        return (low(grad),)

    low_back.defvjp(back_keep, back_low)

    def plain_dot(left, right):
        return jnp.dot(
            left.astype(jnp.bfloat16),
            right.astype(jnp.bfloat16),
            preferred_element_type=jnp.float32,
        )

    narrow_dot = jax.custom_vjp(plain_dot)

    def narrow_keep(left, right):
        left_low = left.astype(jnp.bfloat16)
        right_low = right.astype(jnp.bfloat16)
        return (
            jnp.dot(left_low, right_low, preferred_element_type=jnp.float32),
            (left_low, right_low),
        )

    def narrow_pass(kept, grad):
        left_low, right_low = kept
        grad_low = grad.astype(jnp.bfloat16)
        grad_left = jnp.dot(grad_low, right_low.T, preferred_element_type=jnp.float32)
        grad_right = jnp.dot(left_low.T, grad_low, preferred_element_type=jnp.float32)
        return (grad_left, grad_right)

    narrow_dot.defvjp(narrow_keep, narrow_pass)

    def plain_scores(q_heads, k_heads):
        scale = 1.0 / math.sqrt(q_heads.shape[-1])
        return (
            jnp.einsum(
                "qhd,khd->hqk",
                q_heads.astype(jnp.bfloat16),
                k_heads.astype(jnp.bfloat16),
                preferred_element_type=jnp.float32,
            )
            * scale
        )

    score_product = jax.custom_vjp(plain_scores)

    def score_keep(q_heads, k_heads):
        q_low = q_heads.astype(jnp.bfloat16)
        k_low = k_heads.astype(jnp.bfloat16)
        scale = 1.0 / math.sqrt(q_heads.shape[-1])
        return (
            jnp.einsum("qhd,khd->hqk", q_low, k_low, preferred_element_type=jnp.float32) * scale,
            (q_low, k_low),
        )

    def score_pass(kept, grad):
        q_low, k_low = kept
        scale = 1.0 / math.sqrt(q_low.shape[-1])
        grad_low = grad.astype(jnp.bfloat16)
        grad_q = (
            jnp.einsum("hqk,khd->qhd", grad_low, k_low, preferred_element_type=jnp.float32) * scale
        )
        grad_k = (
            jnp.einsum("hqk,qhd->khd", grad_low, q_low, preferred_element_type=jnp.float32) * scale
        )
        return (grad_q, grad_k)

    score_product.defvjp(score_keep, score_pass)

    def plain_mix(probs, v_heads):
        return jnp.einsum(
            "hqk,khd->qhd",
            probs.astype(jnp.bfloat16),
            v_heads.astype(jnp.bfloat16),
            preferred_element_type=jnp.float32,
        )

    mix_product = jax.custom_vjp(plain_mix)

    def mix_keep(probs, v_heads):
        p_low = probs.astype(jnp.bfloat16)
        v_low = v_heads.astype(jnp.bfloat16)
        return (
            jnp.einsum("hqk,khd->qhd", p_low, v_low, preferred_element_type=jnp.float32),
            (p_low, v_low),
        )

    def mix_pass(kept, grad):
        p_low, v_low = kept
        grad_low = grad.astype(jnp.bfloat16)
        grad_p = jnp.einsum("qhd,khd->hqk", grad_low, v_low, preferred_element_type=jnp.float32)
        grad_v = jnp.einsum("hqk,qhd->khd", p_low, grad_low, preferred_element_type=jnp.float32)
        return (grad_p, grad_v)

    mix_product.defvjp(mix_keep, mix_pass)

    def layer_norm(values, gain):
        row_mean = jnp.mean(values, -1, keepdims=True)
        centered = values - row_mean
        spread = jnp.mean(centered * centered, -1, keepdims=True)
        return centered * lax.rsqrt(spread + 1e-05) * gain

    def project(low_in, weight):
        return low_back(narrow_dot(low_in, weight))

    def attend(query, key_rows, value_rows, allowed):
        row_count, model_width = query.shape
        head_size = model_width // HEADS
        q_heads = low(query).reshape(row_count, HEADS, head_size)
        k_heads = low(key_rows).reshape(-1, HEADS, head_size)
        v_heads = low(value_rows).reshape(-1, HEADS, head_size)
        scores = low_back(score_product(q_heads, k_heads))
        scores = jnp.where(allowed[None], scores, -1e30)
        row_max = jnp.max(scores, -1, keepdims=True)
        expd = jnp.exp(scores - row_max)
        probs = expd / jnp.sum(expd, -1, keepdims=True)
        mixed = mix_product(low(probs), v_heads)
        return low_back(mixed.reshape(row_count, model_width))

    def layer_one(
        seg_tokens, memory_in, doc_ids, attn, w_first, w_second, gain_rows, gate_w, gate_bias
    ):
        seg_count = seg_tokens.shape[0]
        slot_count = memory_in.shape[0]
        memory = low_back(memory_in)
        normed_one = low(layer_norm(seg_tokens, gain_rows[0]))
        same_doc = doc_ids[:, None] == doc_ids[None, :]
        self_out = attend(
            project(normed_one, attn[0, 0]),
            project(normed_one, attn[0, 1]),
            project(normed_one, attn[0, 2]),
            same_doc,
        )
        residual = seg_tokens + project(low(self_out), attn[0, 3])
        mem_norm = layer_norm(memory, gain_rows[4])
        mem_low = low(mem_norm)
        normed_two = low(layer_norm(residual, gain_rows[1]))
        every_slot = jnp.ones((seg_count, slot_count), dtype=bool)
        cross_out = attend(
            project(normed_two, attn[1, 0]),
            project(mem_low, attn[1, 1]),
            project(mem_low, attn[1, 2]),
            every_slot,
        )
        residual = residual + project(low(cross_out), attn[1, 3])
        normed_three = low(layer_norm(residual, gain_rows[2]))
        hidden = low(jax.nn.gelu(project(normed_three, w_first)))
        outputs = residual + project(hidden, w_second)
        normed_four = low(layer_norm(outputs, gain_rows[3]))
        live_keys = jnp.broadcast_to((doc_ids < NDOC)[None, :], (slot_count, seg_count))
        written = attend(
            project(mem_low, attn[2, 0]),
            project(normed_four, attn[2, 1]),
            project(normed_four, attn[2, 2]),
            live_keys,
        )
        update = project(low(written), attn[2, 3])
        forget = jax.nn.sigmoid(
            jnp.dot(mem_norm, gate_w, preferred_element_type=jnp.float32) + gate_bias
        )[:, None]
        fresh = low(low_back(forget * memory + (1.0 - forget) * update))
        return (outputs, fresh)

    return layer_one


def sum_leading(grad):
    return jnp.sum(grad, 0)


def body(
    tokens,
    memory_start,
    doc_lengths,
    attn_weights,
    ffn_in,
    ffn_out,
    gains,
    forget_w,
    forget_bias,
    out_cotangent,
    memory_cotangent,
):
    layer_one = make_layer()

    def run_one(seg_rows, memory_in, doc_ids, weights):
        return layer_one(seg_rows, memory_in, doc_ids, *weights)

    def pull_one(seg_rows, memory_in, doc_ids, out_grad, mem_grad, weights):

        def primal(rows_in, mem_in, weight_in):
            return layer_one(rows_in, mem_in, doc_ids, *weight_in)

        _, pullback = jax.vjp(primal, seg_rows, memory_in, weights)
        return pullback((out_grad, mem_grad))

    section_index = lax.axis_index("seg")
    section_count = lax.axis_size("seg")
    micro_count, seg_tokens, model_width = tokens.shape
    slot_count = memory_start.shape[1]
    doc_ends = jnp.cumsum(doc_lengths, -1)
    positions = section_index * seg_tokens + jnp.arange(seg_tokens, dtype=jnp.int32)
    doc_ids = jnp.sum((doc_ends[:, None, :] <= positions[None, :, None]).astype(jnp.int32), -1)
    weights = (
        attn_weights.astype(jnp.float32),
        ffn_in.astype(jnp.float32),
        ffn_out.astype(jnp.float32),
        gains,
        forget_w,
        forget_bias,
    )
    first_section = section_index == 0
    outputs = jnp.zeros((micro_count, seg_tokens, model_width), jnp.float32)
    entering = jnp.zeros((micro_count, slot_count, model_width), jnp.float32)
    leaving = jnp.zeros((micro_count, slot_count, model_width), jnp.bfloat16)
    grad_rows = jnp.zeros((micro_count, seg_tokens, model_width), jnp.float32)
    grad_entering = jnp.zeros((micro_count, slot_count, model_width), jnp.float32)
    weight_sums = jax.tree.map(jnp.zeros_like, weights)
    run_many = jax.vmap(run_one, in_axes=(0, 0, 0, None))
    pull_many = jax.vmap(pull_one, in_axes=(0, 0, 0, 0, 0, None))
    sending = jnp.zeros((micro_count, slot_count, model_width), jnp.bfloat16)
    for step_index in range(section_count):
        arrived = shifted(sending, "seg", 1)
        mem_in = jnp.where(first_section, memory_start, arrived).astype(jnp.float32)
        active = section_index == step_index

        def compute_all(mem_all):
            return run_many(tokens.astype(jnp.float32), mem_all, doc_ids, weights)

        def skip_all(mem_all):
            return (
                jnp.zeros((micro_count, seg_tokens, model_width), jnp.float32),
                jnp.zeros_like(mem_all),
            )

        result, fresh = lax.cond(active, compute_all, skip_all, mem_in)
        outputs = jnp.where(active, result, outputs)
        entering = jnp.where(active, mem_in, entering)
        leaving = jnp.where(active, fresh.astype(jnp.bfloat16), leaving)
        sending = fresh.astype(jnp.bfloat16)
    sending = jnp.zeros((micro_count, slot_count, model_width), jnp.bfloat16)
    for step_index in range(section_count):
        arrived = shifted(sending, "seg", -1)
        mem_grad = memory_cotangent.astype(jnp.float32) + arrived.astype(jnp.float32)
        active = section_index == section_count - 1 - step_index

        def pull_all(grad_in):
            tok_grad, mem_back, weight_grad = pull_many(
                tokens.astype(jnp.float32),
                entering,
                doc_ids,
                out_cotangent.astype(jnp.float32),
                grad_in,
                weights,
            )
            return (tok_grad, mem_back, jax.tree.map(sum_leading, weight_grad))

        def skip_pull(grad_in):
            return (
                jnp.zeros_like(grad_rows),
                jnp.zeros_like(grad_in),
                jax.tree.map(jnp.zeros_like, weights),
            )

        tok_grad, mem_back, weight_grad = lax.cond(active, pull_all, skip_pull, mem_grad)
        weight_sums = jax.tree.map(jnp.add, weight_sums, weight_grad)
        grad_rows = jnp.where(active, tok_grad, grad_rows)
        grad_entering = jnp.where(active, mem_back, grad_entering)
        sending = mem_back.astype(jnp.bfloat16)
    attn_sum, first_sum, second_sum, gain_sum, gate_sum, bias_sum = weight_sums
    summed = lax.psum(
        (attn_sum, first_sum, second_sum, gain_sum, gate_sum, bias_sum), ("seg", "doc")
    )
    return (
        outputs.astype(jnp.bfloat16),
        leaving,
        grad_rows,
        grad_entering,
        summed[0],
        summed[1],
        summed[2],
        summed[3],
        summed[4],
        summed[5],
    )


def solution(mesh):
    return jax.shard_map(
        body,
        mesh=mesh,
        in_specs=(
            P("doc", "seg", None),
            P("doc", None, None),
            P("doc", None),
            P(),
            P(),
            P(),
            P(),
            P(),
            P(),
            P("doc", "seg", None),
            P("doc", "seg", None),
        ),
        out_specs=(
            P("doc", "seg", None),
            P("doc", "seg", None),
            P("doc", "seg", None),
            P("doc", "seg", None),
            P(),
            P(),
            P(),
            P(),
            P(),
            P(),
        ),
        check_vma=False,
    )
```

profile of v0, /device:TPU:1, one launch (start us, length us, event | category | flops | bytes accessed | tf_op | source)
XLA Modules:
  0.0 1048.7 jit_solution(8022341388931181254)
XLA Ops:
  7.2 4.0 collective-permute-start
  14.4 40.4 %conditional.8 = (f32[2,128,512]{2,1,0:T(8,128)}, bf16[2,64,512]{2,1,0:T(8,128)(2,1)S(1)}) conditional(s32[]{:T(128)} %convert_element_type.2554, () %tuple.98, (bf16[2,128,512]{2,1,0:T(8,128)(2,1)}, f32[5,512]{1,0:T(8,128)}, bf16[3,4,512,512]{3,2,1,0:T(8,128)(2,1)}, s32[2,128]{1,0:T(2,128)}, f32[2,64,512]{2,1,0:T(8,128)S(1)}, ...), branch_computations={%region_2.3_spmd, %region_3.20_spmd} | conditional | flops 2565441536 | bytes 58259928 | solution.py:275
  37.8 2.0 fusion.571
  45.4 1.5 fusion.575
  56.0 1.9 collective-permute-done.1
  58.6 2.0 conditional.9
  60.6 43.0 %collective-permute-start.2 = (bf16[2,64,512]{2,1,0:T(8,128)(2,1)}, bf16[2,64,512]{2,1,0:T(8,128)(2,1)S(1)}, u32[]{:S(2)}, u32[]{:S(2)}) collective-permute-start(bf16[2,64,512]{2,1,0:T(8,128)(2,1)} %get-tuple-element.295), channel_id=1, source_target_pairs={{0,32},{32,64},{64,96},{1,33},{33,65},{65,97},{2,34},{34,66},{66,9... | collective-permute-start | bytes 393224 | tf_op jit(solution)/shard_map/ppermute | solution.py:15
  107.5 3.9 collective-permute-start.3
  114.1 18.6 %conditional.12 = (f32[2,128,512]{2,1,0:T(8,128)S(1)}, f32[2,64,512]{2,1,0:T(8,128)S(1)}, f32[3,4,512,512]{3,2,1,0:T(8,128)}, f32[512,2048]{1,0:T(8,128)S(1)}, f...) conditional(s32[]{:T(128)} %convert_element_type.2549, () %tuple.106, ...), branch_computations={%region_74.75_spmd, %region_75.121_spmd} | conditional | flops 7776626176 | bytes 310954240 | solution.py:304
  117.0 6.4 broadcast.1784
  134.1 44.7 %collective-permute-done.5 = bf16[2,64,512]{2,1,0:T(8,128)(2,1)S(1)} collective-permute-done((bf16[2,64,512]{2,1,0:T(8,128)(2,1)S(1)}, bf16[2,64,512]{2,1,0:T(8,128)(2,1)S(1)}, u32[]{:S(2)}, u32[]{:S(2)}) %collective-permute-start.5) | collective-permute-done | bytes 131104 | tf_op jit(solution)/shard_map/ppermute | solution.py:15
  178.8 18.2 %conditional.13 = (f32[2,128,512]{2,1,0:T(8,128)S(1)}, f32[2,64,512]{2,1,0:T(8,128)S(1)}, f32[3,4,512,512]{3,2,1,0:T(8,128)}, f32[512,2048]{1,0:T(8,128)S(1)}, f...) conditional(s32[]{:T(128)} %convert_element_type.2552, () %tuple.105, ...), branch_computations={%region_121.122_spmd, %region_122.168_spmd} | conditional | flops 7776626176 | bytes 310954240 | solution.py:304
  181.7 6.1 broadcast.1848
  198.4 4.8 collective-permute-done.6
  203.3 18.3 %conditional.14 = (f32[2,128,512]{2,1,0:T(8,128)S(1)}, f32[2,64,512]{2,1,0:T(8,128)S(1)}, f32[3,4,512,512]{3,2,1,0:T(8,128)}, f32[512,2048]{1,0:T(8,128)S(1)}, f...) conditional(s32[]{:T(128)} %convert_element_type.2553, () %tuple.104, ...), branch_computations={%region_168.169_spmd, %region_169.215_spmd} | conditional | flops 7776626176 | bytes 310954240 | solution.py:304
  206.2 6.1 broadcast.1912
  222.9 381.9 %collective-permute-done.7 = bf16[2,64,512]{2,1,0:T(8,128)(2,1)S(1)} collective-permute-done((bf16[2,64,512]{2,1,0:T(8,128)(2,1)S(1)}, bf16[2,64,512]{2,1,0:T(8,128)(2,1)S(1)}, u32[]{:S(2)}, u32[]{:S(2)}) %collective-permute-start.7) | collective-permute-done | bytes 131104 | tf_op jit(solution)/shard_map/ppermute | solution.py:15
  604.9 145.5 %conditional.15 = (f32[2,128,512]{2,1,0:T(8,128)S(1)}, f32[2,64,512]{2,1,0:T(8,128)S(1)}, f32[3,4,512,512]{3,2,1,0:T(8,128)}, f32[512,2048]{1,0:T(8,128)S(1)}, f...) conditional(s32[]{:T(128)} %convert_element_type.2554, () %tuple.103, ...), branch_computations={%region_215.216_spmd, %region_216.262_spmd} | conditional | flops 7776626176 | bytes 308856960 | solution.py:304
  608.5 1.5 fusion.633
  612.5 1.5 fusion.532
  626.6 1.5 fusion.635
  633.0 1.5 fusion.637
  636.8 4.0 multiply_convert_fusion.24
  643.7 2.0 convolution_convert_fusion.107
  645.7 1.8 copy.772
  647.5 2.1 convolution_convert_fusion.109
  649.6 1.8 copy.768
  661.8 2.0 convolution_convert_fusion.119
  663.8 1.8 convert_element_type.2434
  667.0 1.8 multiply_reduce_fusion.69
  668.9 1.8 convert_reduce_fusion.19
  670.7 1.9 select_convert_fusion.7
  673.2 2.4 fusion.511
  677.0 2.1 multiply_reduce_fusion.64
  679.6 1.8 fusion.472
  692.0 1.5 multiply_reduce_fusion.74
  694.8 1.6 multiply_reduce_fusion.62
  697.5 2.1 convolution_convert_fusion.105
  702.9 1.5 multiply_reduce_fusion.61
  707.7 1.5 fusion.510
  711.8 2.1 convolution_bitcast_fusion.48
  713.9 1.7 convolution_bitcast_fusion.51
  715.7 1.8 convolution_bitcast_fusion.55
  717.4 1.8 convolution_bitcast_fusion.44
  719.2 1.8 convolution_bitcast_fusion.45
  721.0 1.8 convolution_bitcast_fusion.46
  722.9 1.9 convolution_bitcast_fusion.49
  724.7 1.8 convolution_bitcast_fusion.50
  726.6 1.8 convolution_bitcast_fusion.52
  728.4 1.8 convolution_bitcast_fusion.53
  730.2 1.8 convolution_bitcast_fusion.54
  732.1 15.5 %add_reduce_fusion.6 = f32[3,4,512,512]{3,2,1,0:T(8,128)} fusion(f32[2,1,1,512,512]{4,3,0,2,1:T(8,128)} %convolution_bitcast_fusion.44, f32[2,1,1,512,512]{4,3,0,2,1:T(8,128)} %convolution_bitcast_fusion.45, f32[2,1,1,512,512]{4,3,0,2,1:T(8,128)} %convolution_bitcast_fusion.46, f32[2,1,1,512,512]{4,3,0,2,1:T(8,128)S(1)} %convolution_bitcast_fusion.47, ...), kind=kLoop, calls=%fused_computation.1101 | loop fusion | flops 72351744 | bytes 37748736 | tf_op jit(solution)/shard_map/cond/branch_1_fun/reduce_sum | solution.py:207
  750.4 1.9 copy-done.53
  753.8 10.2 add_add_fusion.37
  764.0 6.1 add_add_fusion.38
  770.1 22.7 %add_add_fusion.36 = f32[3,4,512,512]{3,2,1,0:T(8,128)} fusion(f32[3,4,512,512]{3,2,1,0:T(8,128)} %get-tuple-element.313, f32[3,4,512,512]{3,2,1,0:T(8,128)} %get-tuple-element.312, f32[3,4,512,512]{3,2,1,0:T(8,128)} %get-tuple-element.310, f32[3,4,512,512]{3,2,1,0:T(8,128)} %get-tuple-element.311), kind=kLoop, calls=%fused_computation.1332 | loop fusion | flops 9437184 | bytes 62914560 | tf_op jit(solution)/shard_map/add | solution.py:305
  796.4 2.0 select_convert_fusion.8
  800.6 73.3 %all-reduce.68 = (f32[5,512]{1,0:T(8,128)}, f32[512]{0:T(512)}, f32[64]{0:T(128)}) all-reduce(f32[5,512]{1,0:T(8,128)S(1)} %add_add_fusion.39, f32[512]{0:T(512)S(1)} %add_add_fusion.40, f32[64]{0:T(128)S(1)} %add_add_fusion.41), channel_id=1, replica_groups=mesh['seg'=4,'doc'=32] {'seg','doc'}, use_global_device_ids=true, to_apply=%region_265.266 | all-reduce | flops 3136 | bytes 25088 | tf_op jit(solution)/shard_map/psum | solution.py:310
  873.9 1.7 select_select_fusion.1
  876.7 148.2 %all-reduce.72.cloned.1.call-done = (f32[3,4,512,512]{3,2,1,0:T(8,128)}, f32[512,2048]{1,0:T(8,128)}, f32[2048,512]{1,0:T(8,128)}) async-done(((f32[3,4,512,512]{3,2,1,0:T(8,128)}, f32[512,2048]{1,0:T(8,128)}, f32[2048,512]{1,0:T(8,128)}), (f32[3,4,512,512]{3,2,1,0:T(8,128)}, f32[512,2048]{1,0:T(8,128)}, f32[2048,512]{1,0:T(8,128)})) %all-reduce.72.cloned.1.call-update) | async-done | bytes 20971536 | tf_op jit(solution)/shard_map/psum | solution.py:310
  1024.9 11.1 %copy.1172 = f32[3,4,512,512]{3,2,1,0:T(8,128)} copy(f32[3,4,512,512]{3,2,1,0:T(8,128)} %get-tuple-element.760) | data formatting | bytes 25165824
  1036.0 2.1 copy.1173
  1038.1 1.6 copy-done.104
  1039.7 2.0 copy.1174
  (582 shorter events, 137.9 us)
Async XLA Ops:
  7.2 1017.7 %all-reduce.72.cloned.1.call-start = ((), (), s32[]{:S(2)}) async-start(), calls=%async_computation | async-start | bytes 41943040 | tf_op jit(solution)/shard_map/psum | solution.py:310
  7.2 7.1 copy-start.381
  7.2 6.1 collective-permute-start
  14.3 43.6 %copy-start.111 = (bf16[2,64,512]{2,1,0:T(8,128)(2,1)S(1)}, bf16[2,64,512]{2,1,0:T(8,128)(2,1)}, u32[]{:S(2)}) copy-start(bf16[2,64,512]{2,1,0:T(8,128)(2,1)} %param.28) | copy-start | bytes 393220
  14.4 14.3 %copy-start.1 = (bf16[2,128,512]{2,1,0:T(8,128)(2,1)S(1)}, bf16[2,128,512]{2,1,0:T(8,128)(2,1)}, u32[]{:S(2)}) copy-start(bf16[2,128,512]{2,1,0:T(8,128)(2,1)} %get-tuple-element.164) | copy-start | bytes 786436 | tf_op jit(solution)/shard_map/cond
  36.0 8.0 copy-start.24
  45.4 7.0 copy-start.361
  45.4 7.0 copy-start.581
  54.7 3.2 collective-permute-start.1
  60.6 45.2 %collective-permute-start.2 = (bf16[2,64,512]{2,1,0:T(8,128)(2,1)}, bf16[2,64,512]{2,1,0:T(8,128)(2,1)S(1)}, u32[]{:S(2)}, u32[]{:S(2)}) collective-permute-start(bf16[2,64,512]{2,1,0:T(8,128)(2,1)} %get-tuple-element.295), channel_id=1, source_target_pairs={{0,32},{32,64},{64,96},{1,33},{33,65},{65,97},{2,34},{34,66},{66,9... | collective-permute-start | bytes 393224 | tf_op jit(solution)/shard_map/ppermute | solution.py:15
  103.6 8.8 collective-permute-start.4
  105.9 7.7 copy-start.55
  107.5 5.9 collective-permute-start.3
  132.7 46.1 %copy-start.266 = (f32[2,128,512]{2,1,0:T(8,128)}, f32[2,128,512]{2,1,0:T(8,128)S(1)}, u32[]{:S(2)}) copy-start(f32[2,128,512]{2,1,0:T(8,128)S(1)} %get-tuple-element.308) | copy-start | bytes 1572868
  132.7 46.1 %copy-start.44 = (f32[2048,512]{1,0:T(8,128)}, f32[2048,512]{1,0:T(8,128)S(1)}, u32[]{:S(2)}) copy-start(f32[2048,512]{1,0:T(8,128)S(1)} %get-tuple-element.318) | copy-start | bytes 12582916
  132.8 46.1 %copy-start.45 = (f32[512,2048]{1,0:T(8,128)}, f32[512,2048]{1,0:T(8,128)S(1)}, u32[]{:S(2)}) copy-start(f32[512,2048]{1,0:T(8,128)S(1)} %get-tuple-element.314) | copy-start | bytes 12582916
  132.8 46.1 %copy-start.196 = (f32[2,64,512]{2,1,0:T(8,128)}, f32[2,64,512]{2,1,0:T(8,128)S(1)}, u32[]{:S(2)}) copy-start(f32[2,64,512]{2,1,0:T(8,128)S(1)} %get-tuple-element.302) | copy-start | bytes 786436
  132.8 46.0 %collective-permute-start.5 = (bf16[2,64,512]{2,1,0:T(8,128)(2,1)S(1)}, bf16[2,64,512]{2,1,0:T(8,128)(2,1)S(1)}, u32[]{:S(2)}, u32[]{:S(2)}) collective-permute-start(bf16[2,64,512]{2,1,0:T(8,128)(2,1)S(1)} %convert_element_type.2564), channel_id=1, source_target_pairs={{32,0},{64,32},{96,64},{33,1},{65,33},{97,65},{34,2},{66,34},{98,6... | collective-permute-start | bytes 393224 | tf_op jit(solution)/shard_map/ppermute | solution.py:15
  197.1 6.1 collective-permute-start.6
  221.6 383.3 %copy-start.50 = (f32[2048,512]{1,0:T(8,128)}, f32[2048,512]{1,0:T(8,128)S(1)}, u32[]{:S(2)}) copy-start(f32[2048,512]{1,0:T(8,128)S(1)} %get-tuple-element.320) | copy-start | bytes 12582916
  221.6 383.3 %copy-start.51 = (f32[512,2048]{1,0:T(8,128)}, f32[512,2048]{1,0:T(8,128)S(1)}, u32[]{:S(2)}) copy-start(f32[512,2048]{1,0:T(8,128)S(1)} %get-tuple-element.316) | copy-start | bytes 12582916
  221.6 383.3 %copy-start.201 = (f32[2,64,512]{2,1,0:T(8,128)}, f32[2,64,512]{2,1,0:T(8,128)S(1)}, u32[]{:S(2)}) copy-start(f32[2,64,512]{2,1,0:T(8,128)S(1)} %get-tuple-element.304) | copy-start | bytes 786436
  221.6 383.3 %copy-start.272 = (f32[2,128,512]{2,1,0:T(8,128)}, f32[2,128,512]{2,1,0:T(8,128)S(1)}, u32[]{:S(2)}) copy-start(f32[2,128,512]{2,1,0:T(8,128)S(1)} %get-tuple-element.306) | copy-start | bytes 1572868
  221.6 383.2 %collective-permute-start.7 = (bf16[2,64,512]{2,1,0:T(8,128)(2,1)S(1)}, bf16[2,64,512]{2,1,0:T(8,128)(2,1)S(1)}, u32[]{:S(2)}, u32[]{:S(2)}) collective-permute-start(bf16[2,64,512]{2,1,0:T(8,128)(2,1)S(1)} %convert_element_type.2568), channel_id=1, source_target_pairs={{32,0},{64,32},{96,64},{33,1},{65,33},{97,65},{34,2},{66,34},{98,6... | collective-permute-start | bytes 393224 | tf_op jit(solution)/shard_map/ppermute | solution.py:15
  604.9 14.6 %copy-start.7 = (bf16[2,128,512]{2,1,0:T(8,128)(2,1)S(1)}, bf16[2,128,512]{2,1,0:T(8,128)(2,1)}, u32[]{:S(2)}) copy-start(bf16[2,128,512]{2,1,0:T(8,128)(2,1)} %get-tuple-element.241) | copy-start | bytes 786436 | tf_op jit(solution)/shard_map/cond
  607.2 15.6 %copy-start.416 = (f32[2,128]{1,0:T(2,128)}, f32[2,128]{1,0:T(2,128)S(1)}, u32[]{:S(2)}) copy-start(f32[2,128]{1,0:T(2,128)S(1)} %broadcast_multiply_fusion.38) | copy-start | bytes 3076 | tf_op jit(solution)/shard_map/cond
  608.4 14.4 %copy-start.469 = (f32[2,128]{1,0:T(2,128)}, f32[2,128]{1,0:T(2,128)S(1)}, u32[]{:S(2)}) copy-start(f32[2,128]{1,0:T(2,128)S(1)} %fusion.545) | copy-start | bytes 3076 | tf_op jit(solution)/shard_map/cond
  608.5 14.3 %copy-start.396 = (f32[2,64]{1,0:T(2,128)}, f32[2,64]{1,0:T(2,128)S(1)}, u32[]{:S(2)}) copy-start(f32[2,64]{1,0:T(2,128)S(1)} %broadcast_multiply_fusion.39) | copy-start | bytes 1540 | tf_op jit(solution)/shard_map/cond
  610.0 12.8 %copy-start.388 = (f32[1,512]{1,0:T(1,128)}, f32[1,512]{1,0:T(1,128)S(1)}, u32[]{:S(2)}) copy-start(f32[1,512]{1,0:T(1,128)S(1)} %get-tuple-element.647) | copy-start | bytes 6148 | tf_op jit(solution)/shard_map/cond
  610.0 12.8 %copy-start.408 = (f32[1,512]{1,0:T(1,128)}, f32[1,512]{1,0:T(1,128)S(1)}, u32[]{:S(2)}) copy-start(f32[1,512]{1,0:T(1,128)S(1)} %get-tuple-element.646) | copy-start | bytes 6148 | tf_op jit(solution)/shard_map/cond
  610.0 18.4 %copy-start.461 = (f32[1,512]{1,0:T(1,128)}, f32[1,512]{1,0:T(1,128)S(1)}, u32[]{:S(2)}) copy-start(f32[1,512]{1,0:T(1,128)S(1)} %get-tuple-element.645) | copy-start | bytes 6148 | tf_op jit(solution)/shard_map/cond
  610.8 13.8 %copy-start.359 = (pred[2,128,128]{1,2,0:T(8,128)(4,1)}, pred[2,128,128]{1,2,0:T(8,128)(4,1)S(1)}, u32[]{:S(2)}) copy-start(pred[2,128,128]{1,2,0:T(8,128)(4,1)S(1)} %broadcast_compare_fusion.26) | copy-start | bytes 98308 | tf_op jit(solution)/shard_map/cond
  612.5 11.9 %copy-start.526 = (f32[2,64]{1,0:T(2,128)}, f32[2,64]{1,0:T(2,128)S(1)}, u32[]{:S(2)}) copy-start(f32[2,64]{1,0:T(2,128)S(1)} %get-tuple-element.389) | copy-start | bytes 1540 | tf_op jit(solution)/shard_map/cond
  614.2 10.2 copy-start.263
  615.7 15.6 %copy-start.228 = (bf16[2,64,512]{1,2,0:T(8,128)(2,1)}, bf16[2,64,512]{1,2,0:T(8,128)(2,1)S(1)}, u32[]{:S(2)}) copy-start(bf16[2,64,512]{1,2,0:T(8,128)(2,1)S(1)} %copy.984) | copy-start | bytes 393220 | tf_op jit(solution)/shard_map/cond
  617.3 15.5 %copy-start.169 = (bf16[2,64,8,64]{3,2,1,0:T(8,128)(2,1)}, bf16[2,64,8,64]{3,2,1,0:T(8,128)(2,1)S(1)}, u32[]{:S(2)}) copy-start(bf16[2,64,8,64]{3,2,1,0:T(8,128)(2,1)S(1)} %convert_element_type.2457) | copy-start | bytes 393220 | tf_op jit(solution)/shard_map/cond
  652.9 8.1 copy-start.347
  653.3 7.7 copy-start.380
  665.6 7.3 copy-start.240
  667.0 12.2 %copy-start.135 = (bf16[2,8,64,128]{3,2,1,0:T(8,128)(2,1)}, bf16[2,8,64,128]{3,2,1,0:T(8,128)(2,1)S(1)}, u32[]{:S(2)}) copy-start(bf16[2,8,64,128]{3,2,1,0:T(8,128)(2,1)S(1)} %convolution_convert_fusion.108) | copy-start | bytes 786436 | tf_op jit(solution)/shard_map/cond
  667.0 10.0 copy-start.71
  667.0 10.0 copy-start.446
  667.0 10.0 copy-start.454
  667.0 10.0 copy-start.486
  670.7 8.4 copy-start.551
  684.2 7.6 copy-start.229
  686.1 7.5 copy-start.527
  686.1 7.5 copy-start.425
  693.6 7.2 copy-start.89
  694.8 8.1 copy-start.23
  694.8 8.1 copy-start.437
  696.7 7.7 copy-start.372
  732.1 15.5 %copy-start.110 = (bf16[2,128,2048]{2,1,0:T(8,128)(2,1)S(1)}, bf16[2,128,2048]{2,1,0:T(8,128)(2,1)}, u32[]{:S(2)}) copy-start(bf16[2,128,2048]{2,1,0:T(8,128)(2,1)} %copy-done.109) | copy-start | bytes 3145732 | tf_op jit(solution)/shard_map/cond
  732.1 15.5 %copy-start.284 = (bf16[2,128,512]{2,1,0:T(8,128)(2,1)S(1)}, bf16[2,128,512]{2,1,0:T(8,128)(2,1)}, u32[]{:S(2)}) copy-start(bf16[2,128,512]{2,1,0:T(8,128)(2,1)} %copy-done.283) | copy-start | bytes 786436 | tf_op jit(solution)/shard_map/cond
  750.4 13.6 %copy-start.310 = (f32[2,64,512]{2,1,0:T(8,128)}, f32[2,64,512]{2,1,0:T(8,128)S(1)}, u32[]{:S(2)}) copy-start(f32[2,64,512]{2,1,0:T(8,128)S(1)} %get-tuple-element.309) | copy-start | bytes 786436
  753.8 10.2 copy-start.46
  753.8 10.2 copy-start.49
  753.8 10.2 copy-start.52
  794.6 79.3 %copy-start.197 = (f32[2,64,512]{2,1,0:T(8,128)S(1)}, f32[2,64,512]{2,1,0:T(8,128)}, u32[]{:S(2)}) copy-start(f32[2,64,512]{2,1,0:T(8,128)} %copy-done.196) | copy-start | bytes 786436
  795.7 80.0 %copy-start.267 = (f32[2,128,512]{2,1,0:T(8,128)S(1)}, f32[2,128,512]{2,1,0:T(8,128)}, u32[]{:S(2)}) copy-start(f32[2,128,512]{2,1,0:T(8,128)} %copy-done.266) | copy-start | bytes 1572868
  795.7 80.0 %copy-start.270 = (f32[2,128,512]{2,1,0:T(8,128)S(1)}, f32[2,128,512]{2,1,0:T(8,128)}, u32[]{:S(2)}) copy-start(f32[2,128,512]{2,1,0:T(8,128)} %copy-done.269) | copy-start | bytes 1572868
  795.7 80.0 %copy-start.273 = (f32[2,128,512]{2,1,0:T(8,128)S(1)}, f32[2,128,512]{2,1,0:T(8,128)}, u32[]{:S(2)}) copy-start(f32[2,128,512]{2,1,0:T(8,128)} %copy-done.272) | copy-start | bytes 1572868
  795.7 80.0 %copy-start.276 = (f32[2,128,512]{2,1,0:T(8,128)S(1)}, f32[2,128,512]{2,1,0:T(8,128)}, u32[]{:S(2)}) copy-start(f32[2,128,512]{2,1,0:T(8,128)} %copy-done.275) | copy-start | bytes 1572868
  1024.9 11.1 %copy-start.105 = (f32[512,2048]{1,0:T(8,128)S(1)}, f32[512,2048]{1,0:T(8,128)}, u32[]{:S(2)}) copy-start(f32[512,2048]{1,0:T(8,128)} %get-tuple-element.761) | copy-start | bytes 12582916
  (121 other events, 399.6 us)
Sparse Core Ops, SparseCore 0:
  793.0 231.8 all-reduce.71
where the time goes:
time: 1060 us; the launch traced here: 1050 us
  waiting for transfers between devices  583 us (55%)
  matrix products  108 us (10%)
  other arithmetic  102 us (10%)
  local copies, waits for them, and re-layouts  78.5 us (7%)
  blocking collectives  73.3 us (7%)
  starting transfers between devices  57.4 us (5%)
  loops' own time  31.5 us (3%)
  between operations  14.9 us (1%)
    ppermute x8, waiting for transfers between devices, shifted(): lax.ppermute(value, axis, [(source, source + steps) for source in range(f...  435 us
    psum x1, waiting for transfers between devices, body(): lax.psum((attn_sum, first_sum, second_sum, gain_sum, gate_sum, bias_sum),...  148 us
    psum x1, blocking collectives, body(): lax.psum((attn_sum, first_sum, second_sum, gain_sum, gate_sum, bias_sum),...  73.3 us
    ppermute x8, starting transfers between devices, shifted(): lax.ppermute(value, axis, [(source, source + steps) for source in range(f...  57.3 us
    dot_general x28, matrix products, project(): return low_back(narrow_dot(low_in, weight))  44.9 us
    add x6, other arithmetic, body(): weight_sums = jax.tree.map(jnp.add, weight_sums, weight_grad)  41.1 us
    another operation x31, local copies, waits for them, and re-layouts  30.4 us
    another operation x4, loops' own time, body(): lax.cond(active, pull_all, skip_pull, mem_grad)  30.3 us
  transfers between devices with their start and end apart: 9, of which 7 were waited for; matrix products, arithmetic and copies ran while one was open for 1% of the time, Pallas kernels for 0%

commit v1 on v0

v1 whole, which is shorter than its diff:
```python
import functools

import jax
import jax.numpy as jnp
from jax import lax
from jax.experimental import pallas as pl
from jax.experimental.pallas import tpu as pltpu
from jax.sharding import PartitionSpec as P

HEADS = 8
NDOC = 8
D = 512
FF = 2048
SLOTS = 64
SEG = 128
NSEG = 4
ROWS = NSEG * SEG
MROWS = NSEG * SLOTS
PAIRS = 4
PAIR = 128
FCHUNK = 512
BLOCK = 256
NBLOCKS = 20

f32 = jnp.float32
bf16 = jnp.bfloat16


def dot(a, b):
    return lax.dot_general(a, b, (((1,), (0,)), ((), ())), preferred_element_type=f32)


def dot_nt(a, b):
    return lax.dot_general(a, b, (((1,), (1,)), ((), ())), preferred_element_type=f32)


def dot_tn(a, b):
    return lax.dot_general(a, b, (((0,), (0,)), ((), ())), preferred_element_type=f32)


def norm_stats(values):
    centered = values - jnp.mean(values, -1, keepdims=True)
    rstd = lax.rsqrt(jnp.mean(centered * centered, -1, keepdims=True) + 1e-05)
    return centered * rstd, rstd


def norm_back(grad, gain, xhat, rstd):
    scaled = grad * gain
    mean_one = jnp.mean(scaled, -1, keepdims=True)
    mean_two = jnp.mean(scaled * xhat, -1, keepdims=True)
    return rstd * (scaled - mean_one - xhat * mean_two)


def head_halves(values):
    low_half = lax.broadcasted_iota(jnp.int32, values.shape, 1) % PAIR < PAIR // 2
    return jnp.where(low_half, values, 0.0).astype(bf16), jnp.where(low_half, 0.0, values).astype(bf16)


def join_halves(stacked):
    rows = stacked.shape[0] // 2
    low_half = lax.broadcasted_iota(jnp.int32, (rows, PAIR), 1) < PAIR // 2
    return jnp.where(low_half, stacked[:rows], stacked[rows:])


def softmax_rows(scores):
    expd = jnp.exp(scores - jnp.max(scores, -1, keepdims=True))
    return expd * (1.0 / jnp.sum(expd, -1, keepdims=True))


def softmax_back(probs, grad):
    return probs * (grad - jnp.sum(probs * grad, -1, keepdims=True))


def gelu_both(u):
    square = u * u
    tanh = jnp.tanh(0.7978845608028654 * u * (1.0 + 0.044715 * square))
    half = 0.5 + 0.5 * tanh
    slope = half + u * half * (1.0 - tanh) * (0.7978845608028654 + 0.1070322243 * square)
    return u * half, slope


def layer_kernel(
    ends_ref, half_ref,
    tok_ref, mem_ref, ocot_ref, mcot_ref, attn_ref, win_ref, wout_ref, gains_ref, fw_ref, fb_ref,
    act_ref, mout_ref, gtok_ref, gmem_ref, dw_ref, small_ref,
    h_s, q_s, k_s, v_s, p_s, o_s, xh0_s, rs0_s,
    res_s, n1_s, xh1_s, rs1_s, cq_s, ck_s, cv_s, cp_s, co_s,
    n2_s, xh2_s, rs2_s, hid_s, gd_s,
    t_s, xh3_s, rs3_s, m_s, xh4_s, rs4_s, mlow_s, gate_s, upd_s, mprev_s,
    wq_s, wk_s, wv_s, wp_s, wo_s,
    gup_s, dwq_s, dwk_s, dwv_s, gyl_s, gul_s, gbl_s, dcq_s, dck_s, dcv_s,
    gb_s, gal_s, dq_s, dk_s, dv_s, gain_s, gm_s,
):
    gain = [gains_ref[i : i + 1, :] for i in range(5)]

    def doc_ids(shape, dim, base):
        pos = lax.broadcasted_iota(jnp.int32, shape, dim) + base
        ids = jnp.zeros(shape, jnp.int32)
        for j in range(NDOC):
            ids += (ends_ref[j] <= pos).astype(jnp.int32)
        return ids

    xhat, rstd = norm_stats(tok_ref[...].astype(f32))
    xh0_s[...] = xhat
    rs0_s[...] = rstd
    h = (xhat * gain[0]).astype(bf16)
    h_s[...] = h
    q_s[0], q_s[1] = head_halves(dot(h, attn_ref[0]) * 0.125)
    k_s[...] = dot(h, attn_ref[1]).astype(bf16)
    v_s[...] = dot(h, attn_ref[2]).astype(bf16)

    def self_forward(seg, carry):
        rows = pl.ds(pl.multiple_of(seg * SEG, SEG), SEG)
        same = doc_ids((SEG, SEG), 0, seg * SEG) == doc_ids((SEG, SEG), 1, seg * SEG)
        same = jnp.concatenate([same.astype(jnp.int32)] * 2, 0) > 0
        for pair in range(PAIRS):
            lanes = slice(pair * PAIR, (pair + 1) * PAIR)
            q_both = jnp.concatenate([q_s[0, rows, lanes], q_s[1, rows, lanes]], 0)
            scores = jnp.where(same, dot_nt(q_both, k_s[rows, lanes]), -1e30)
            probs = softmax_rows(scores).astype(bf16)
            p_s[seg, pair] = probs
            o_s[rows, lanes] = join_halves(dot(probs, v_s[rows, lanes])).astype(bf16)
        return carry

    lax.fori_loop(0, NSEG, self_forward, 0)
    res = tok_ref[...].astype(f32) + dot(o_s[...], attn_ref[3])
    res_s[...] = res
    xhat, rstd = norm_stats(res)
    xh1_s[...] = xhat
    rs1_s[...] = rstd
    n1 = (xhat * gain[1]).astype(bf16)
    n1_s[...] = n1
    cq_s[0], cq_s[1] = head_halves(dot(n1, attn_ref[4]) * 0.125)

    mprev_s[...] = mem_ref[...].astype(f32)

    def forward(seg, carry):
        rows = pl.ds(pl.multiple_of(seg * SEG, SEG), SEG)
        slots = pl.ds(pl.multiple_of(seg * SLOTS, SLOTS), SLOTS)
        mem = mprev_s[...]
        xhat, rstd = norm_stats(mem)
        xh4_s[slots, :] = xhat
        rs4_s[slots, :] = rstd
        m = xhat * gain[4]
        mlow = m.astype(bf16)
        mlow_s[slots, :] = mlow
        gate = jax.nn.sigmoid(jnp.sum(m * fw_ref[...], -1, keepdims=True) + fb_ref[...])
        gate_s[slots, :] = gate
        ck = dot(mlow, attn_ref[5]).astype(bf16)
        cv = dot(mlow, attn_ref[6]).astype(bf16)
        ck_s[slots, :] = ck
        cv_s[slots, :] = cv
        wq0, wq1 = head_halves(dot(mlow, attn_ref[8]) * 0.125)
        wq_s[0, slots, :] = wq0
        wq_s[1, slots, :] = wq1
        for pair in range(PAIRS):
            lanes = slice(pair * PAIR, (pair + 1) * PAIR)
            q_both = jnp.concatenate([cq_s[0, rows, lanes], cq_s[1, rows, lanes]], 0)
            probs = softmax_rows(dot_nt(q_both, ck[:, lanes])).astype(bf16)
            cp_s[seg, pair] = probs
            co_s[rows, lanes] = join_halves(dot(probs, cv[:, lanes])).astype(bf16)
        res = res_s[rows, :] + dot(co_s[rows, :], attn_ref[7])
        xhat, rstd = norm_stats(res)
        xh2_s[rows, :] = xhat
        rs2_s[rows, :] = rstd
        n2 = (xhat * gain[2]).astype(bf16)
        n2_s[rows, :] = n2
        for c in range(0, FF, FCHUNK):
            hid, slope = gelu_both(dot(n2, win_ref[:, c : c + FCHUNK]))
            hid = hid.astype(bf16)
            hid_s[rows, c : c + FCHUNK] = hid
            gd_s[rows, c : c + FCHUNK] = slope.astype(bf16)
            res = res + dot(hid, wout_ref[c : c + FCHUNK, :])
        act_ref[rows, :] = res.astype(bf16)
        xhat, rstd = norm_stats(res)
        xh3_s[rows, :] = xhat
        rs3_s[rows, :] = rstd
        t = (xhat * gain[3]).astype(bf16)
        t_s[rows, :] = t
        wk = dot(t, attn_ref[9]).astype(bf16)
        wv = dot(t, attn_ref[10]).astype(bf16)
        wk_s[rows, :] = wk
        wv_s[rows, :] = wv
        live = doc_ids((2 * SLOTS, SEG), 1, seg * SEG) < NDOC
        for pair in range(PAIRS):
            lanes = slice(pair * PAIR, (pair + 1) * PAIR)
            q_both = jnp.concatenate([wq0[:, lanes], wq1[:, lanes]], 0)
            scores = jnp.where(live, dot_nt(q_both, wk[:, lanes]), -1e30)
            probs = softmax_rows(scores).astype(bf16)
            wp_s[seg, pair] = probs
            wo_s[slots, lanes] = join_halves(dot(probs, wv[:, lanes])).astype(bf16)
        update = dot(wo_s[slots, :], attn_ref[11])
        upd_s[slots, :] = mem - update
        fresh = (update + gate * (mem - update)).astype(bf16)
        mout_ref[slots, :] = fresh
        mprev_s[...] = fresh.astype(f32)
        return carry

    lax.fori_loop(0, NSEG, forward, 0)

    gm_s[...] = jnp.zeros_like(gm_s)
    gain_s[...] = jnp.zeros_like(gain_s)
    small_ref[...] = jnp.zeros_like(small_ref)

    def backward(step, carry):
        seg = NSEG - 1 - step
        rows = pl.ds(pl.multiple_of(seg * SEG, SEG), SEG)
        slots = pl.ds(pl.multiple_of(seg * SLOTS, SLOTS), SLOTS)
        gz = (mcot_ref[slots, :].astype(f32) + gm_s[...]).astype(bf16).astype(f32)
        gate = gate_s[slots, :]
        dgate = jnp.sum(gz * upd_s[slots, :], -1, keepdims=True) * gate * (1.0 - gate)
        gup = ((1.0 - gate) * gz).astype(bf16)
        gup_s[slots, :] = gup
        xh4 = xh4_s[slots, :]
        small_ref[0:1, :] += jnp.sum(dgate * (xh4 * gain[4]), 0, keepdims=True)
        small_ref[8:72, 0:128] += jnp.broadcast_to(dgate, (SLOTS, 128))
        gm = dgate * fw_ref[...]
        g_o0, g_o1 = head_halves(dot_nt(gup, attn_ref[11]))
        for pair in range(PAIRS):
            lanes = slice(pair * PAIR, (pair + 1) * PAIR)
            probs = wp_s[seg, pair]
            g_both = jnp.concatenate([g_o0[:, lanes], g_o1[:, lanes]], 0)
            q_both = jnp.concatenate([wq_s[0, slots, lanes], wq_s[1, slots, lanes]], 0)
            ds = softmax_back(probs.astype(f32), dot_nt(g_both, wv_s[rows, lanes])).astype(bf16)
            dwv_s[rows, lanes] = dot_tn(probs, g_both).astype(bf16)
            dwk_s[rows, lanes] = dot_tn(ds, q_both).astype(bf16)
            dwq_s[slots, lanes] = (join_halves(dot(ds, wk_s[rows, lanes])) * 0.125).astype(bf16)
        gm = gm + dot_nt(dwq_s[slots, :], attn_ref[8])
        gt = dot_nt(dwk_s[rows, :], attn_ref[9]) + dot_nt(dwv_s[rows, :], attn_ref[10])
        xhat = xh3_s[rows, :]
        gain_s[3:4, :] += jnp.sum(gt * xhat, 0, keepdims=True)
        gy = ocot_ref[rows, :].astype(f32) + norm_back(gt, gain[3], xhat, rs3_s[rows, :])
        gyl = gy.astype(bf16)
        gyl_s[rows, :] = gyl
        gn2 = jnp.zeros((SEG, D), f32)
        for c in range(0, FF, FCHUNK):
            ghid = dot_nt(gyl, wout_ref[c : c + FCHUNK, :])
            gul = (ghid * gd_s[rows, c : c + FCHUNK].astype(f32)).astype(bf16)
            gul_s[rows, c : c + FCHUNK] = gul
            gn2 = gn2 + dot_nt(gul, win_ref[:, c : c + FCHUNK])
        xhat = xh2_s[rows, :]
        gain_s[2:3, :] += jnp.sum(gn2 * xhat, 0, keepdims=True)
        gb = gy + norm_back(gn2, gain[2], xhat, rs2_s[rows, :])
        gb_s[rows, :] = gb
        gbl = gb.astype(bf16)
        gbl_s[rows, :] = gbl
        g_o0, g_o1 = head_halves(dot_nt(gbl, attn_ref[7]))
        for pair in range(PAIRS):
            lanes = slice(pair * PAIR, (pair + 1) * PAIR)
            probs = cp_s[seg, pair]
            g_both = jnp.concatenate([g_o0[:, lanes], g_o1[:, lanes]], 0)
            q_both = jnp.concatenate([cq_s[0, rows, lanes], cq_s[1, rows, lanes]], 0)
            ds = softmax_back(probs.astype(f32), dot_nt(g_both, cv_s[slots, lanes])).astype(bf16)
            dcv_s[slots, lanes] = dot_tn(probs, g_both).astype(bf16)
            dck_s[slots, lanes] = dot_tn(ds, q_both).astype(bf16)
            dcq_s[rows, lanes] = (join_halves(dot(ds, ck_s[slots, lanes])) * 0.125).astype(bf16)
        gm = gm + dot_nt(dck_s[slots, :], attn_ref[5]) + dot_nt(dcv_s[slots, :], attn_ref[6])
        gain_s[4:5, :] += jnp.sum(gm * xh4, 0, keepdims=True)
        gmem = gate * gz + norm_back(gm, gain[4], xh4, rs4_s[slots, :])
        gmem = gmem.astype(bf16)
        gmem_ref[slots, :] = gmem
        gm_s[...] = gmem.astype(f32)
        return carry

    lax.fori_loop(0, NSEG, backward, 0)

    gn1 = dot_nt(dcq_s[...], attn_ref[4])
    xhat = xh1_s[...]
    gain_s[1:2, :] = jnp.sum(gn1 * xhat, 0, keepdims=True)
    ga = gb_s[...] + norm_back(gn1, gain[1], xhat, rs1_s[...])
    gb_s[...] = ga
    gal = ga.astype(bf16)
    gal_s[...] = gal
    g0, g1 = head_halves(dot_nt(gal, attn_ref[3]))
    cq_s[0] = g0
    cq_s[1] = g1

    def self_backward(seg, carry):
        rows = pl.ds(pl.multiple_of(seg * SEG, SEG), SEG)
        for pair in range(PAIRS):
            lanes = slice(pair * PAIR, (pair + 1) * PAIR)
            probs = p_s[seg, pair]
            g_both = jnp.concatenate([cq_s[0, rows, lanes], cq_s[1, rows, lanes]], 0)
            q_both = jnp.concatenate([q_s[0, rows, lanes], q_s[1, rows, lanes]], 0)
            ds = softmax_back(probs.astype(f32), dot_nt(g_both, v_s[rows, lanes])).astype(bf16)
            dv_s[rows, lanes] = dot_tn(probs, g_both).astype(bf16)
            dk_s[rows, lanes] = dot_tn(ds, q_both).astype(bf16)
            dq_s[rows, lanes] = (join_halves(dot(ds, k_s[rows, lanes])) * 0.125).astype(bf16)
        return carry

    lax.fori_loop(0, NSEG, self_backward, 0)
    gh = dot_nt(dq_s[...], attn_ref[0]) + dot_nt(dk_s[...], attn_ref[1]) + dot_nt(dv_s[...], attn_ref[2])
    xhat = xh0_s[...]
    gain_s[0:1, :] = jnp.sum(gh * xhat, 0, keepdims=True)
    gtok_ref[...] = (gb_s[...] + norm_back(gh, gain[0], xhat, rs0_s[...])).astype(bf16)
    small_ref[1:6, :] = gain_s[0:5, :]

    half = half_ref[0]
    cut = pl.ds(pl.multiple_of(half * BLOCK, BLOCK), BLOCK)
    pairs = [
        (h_s, dq_s), (h_s, dk_s), (h_s, dv_s), (o_s, gal_s),
        (n1_s, dcq_s), (mlow_s, dck_s), (mlow_s, dcv_s), (co_s, gbl_s),
        (mlow_s, dwq_s), (t_s, dwk_s), (t_s, dwv_s), (wo_s, gup_s),
    ]
    for i, (left, right) in enumerate(pairs):
        dw_ref[i] = dot_tn(left[:, cut], right[...]).astype(bf16)
    for i in range(4):
        dw_ref[12 + i] = dot_tn(n2_s[:, cut], gul_s[:, i * D : (i + 1) * D]).astype(bf16)
    for i in range(4):
        cut_i = pl.ds(pl.multiple_of(half * 4 * BLOCK + i * BLOCK, BLOCK), BLOCK)
        dw_ref[16 + i] = dot_tn(hid_s[:, cut_i], gyl_s[...]).astype(bf16)


def run_layer(ends, half, tok, mem, ocot, mcot, attn, win, wout, gains, fw, fb):
    def rows(dtype=bf16, width=D):
        return pltpu.VMEM((ROWS, width), dtype)

    def slots(dtype=bf16, width=D):
        return pltpu.VMEM((MROWS, width), dtype)

    def two(count):
        return pltpu.VMEM((2, count, D), bf16)

    scratch = [
        rows(), two(ROWS), rows(), rows(), pltpu.VMEM((NSEG, PAIRS, 2 * SEG, SEG), bf16), rows(),
        rows(f32), rows(f32, 1),
        rows(f32), rows(), rows(f32), rows(f32, 1), two(ROWS), slots(), slots(),
        pltpu.VMEM((NSEG, PAIRS, 2 * SEG, SLOTS), bf16), rows(),
        rows(), rows(f32), rows(f32, 1), rows(bf16, FF), rows(bf16, FF),
        rows(), rows(f32), rows(f32, 1), slots(f32), slots(f32), slots(f32, 1), slots(), slots(f32, 1),
        slots(f32), pltpu.VMEM((SLOTS, D), f32),
        two(MROWS), rows(), rows(), pltpu.VMEM((NSEG, PAIRS, 2 * SLOTS, SEG), bf16), slots(),
        slots(), slots(), rows(), rows(), rows(), rows(bf16, FF), rows(), rows(), slots(), slots(),
        rows(f32), rows(), rows(), rows(), rows(), pltpu.VMEM((8, D), f32), pltpu.VMEM((SLOTS, D), f32),
    ]
    smem = pl.BlockSpec(memory_space=pltpu.SMEM)
    vmem = pl.BlockSpec(memory_space=pltpu.VMEM)
    return pl.pallas_call(
        layer_kernel,
        out_shape=(
            jax.ShapeDtypeStruct((ROWS, D), bf16),
            jax.ShapeDtypeStruct((MROWS, D), bf16),
            jax.ShapeDtypeStruct((ROWS, D), bf16),
            jax.ShapeDtypeStruct((MROWS, D), bf16),
            jax.ShapeDtypeStruct((NBLOCKS, BLOCK, D), bf16),
            jax.ShapeDtypeStruct((72, D), f32),
        ),
        in_specs=[smem] * 2 + [vmem] * 10,
        out_specs=[vmem] * 6,
        scratch_shapes=scratch,
        compiler_params=pltpu.CompilerParams(vmem_limit_bytes=60 << 20),
        name="layer",
    )(ends, half, tok, mem, ocot, mcot, attn, win, wout, gains, fw, fb)


def body(
    tokens, memory_start, doc_lengths, attn_weights, ffn_in, ffn_out, gains, forget_w, forget_bias,
    out_cotangent, memory_cotangent,
):
    section = lax.axis_index("seg")
    stream, half = section % 2, section // 2

    def one_stream(value):
        gathered = lax.all_gather(value, "seg", axis=0)
        picked = lax.dynamic_index_in_dim(gathered, stream, 1, keepdims=False)
        return picked.reshape(-1, D)

    ends = lax.dynamic_index_in_dim(jnp.cumsum(doc_lengths, -1).astype(jnp.int32), stream, 0, keepdims=False)
    acts, mems, gtok, gmem, dw, small = run_layer(
        ends, half.reshape(1).astype(jnp.int32),
        one_stream(tokens), lax.dynamic_index_in_dim(memory_start, stream, 0, keepdims=False),
        one_stream(out_cotangent), one_stream(memory_cotangent),
        attn_weights.reshape(12, D, D), ffn_in, ffn_out, gains, forget_w.reshape(1, D), forget_bias.reshape(SLOTS, 1),
    )

    def both_streams(value):
        parts = value.reshape(NSEG, -1, D)
        return lax.all_to_all(parts, "seg", 0, 0)[:2]

    acts, mems, gtok, gmem = (both_streams(v) for v in (acts, mems, gtok, gmem))
    whole = jnp.stack([jnp.where(half == i, dw, 0) for i in range(2)], 1)
    whole, small = lax.psum((whole, jnp.where(half == 0, small, 0)), ("seg", "doc"))
    whole = whole.astype(f32)
    grad_attn = whole[:12].reshape(3, 4, D, D)
    grad_in = whole[12:16].transpose(1, 2, 0, 3).reshape(D, FF)
    grad_out = whole[16:20].transpose(1, 0, 2, 3).reshape(FF, D)
    return (
        acts, mems, gtok.astype(f32), gmem.astype(f32), grad_attn, grad_in, grad_out,
        small[1:6], small[0], small[8:72, 0],
    )


def solution(mesh):
    return jax.shard_map(
        body,
        mesh=mesh,
        in_specs=(
            P("doc", "seg", None), P("doc", None, None), P("doc", None), P(), P(), P(), P(), P(), P(),
            P("doc", "seg", None), P("doc", "seg", None),
        ),
        out_specs=(
            P("doc", "seg", None), P("doc", "seg", None), P("doc", "seg", None), P("doc", "seg", None),
            P(), P(), P(), P(), P(), P(),
        ),
        check_vma=False,
    )
```

time: 1060 us -> 493 us (0.47); the launches traced: 1050 us -> 492 us
  waiting for transfers between devices: 583 us -> 295 us
  matrix products: 108 us -> 0 us
  other arithmetic: 102 us -> 34.1 us
  Pallas kernels: 0 us -> 63.7 us
  starting transfers between devices: 57.4 us -> 3.63 us
  blocking collectives: 73.3 us -> 37.7 us
  local copies, waits for them, and re-layouts: 78.5 us -> 44.9 us
  loops' own time: 31.5 us -> 0 us
    ppermute x8 -> x0, waiting for transfers between devices: 435 us -> none  [shifted(): lax.ppermute(value, axis, [(source, source + steps) for source in range(f...]
    psum x1 -> x2, waiting for transfers between devices: 148 us -> 258 us  [body(): lax.psum((whole, jnp.where(half == 0, small, 0)), ('seg', 'doc'))]
    dot_general x80 -> x0, matrix products: 105 us -> none  [the longest x28 44.9 us: project(): return low_back(narrow_dot(low_in, weight))]
    psum x1 -> x0, blocking collectives: 73.3 us -> none  [body(): lax.psum((attn_sum, first_sum, second_sum, gain_sum, gate_sum, bias_sum),...]
    pallas_call x0 -> x1, Pallas kernels: none -> 63.7 us  [run_layer(): pl.pallas_call(layer_kernel, out_shape=(jax.ShapeDtypeStruct((ROWS, D), b...]
    ppermute x8 -> x0, starting transfers between devices: 57.3 us -> none  [shifted(): lax.ppermute(value, axis, [(source, source + steps) for source in range(f...]
    add x7 -> x0, other arithmetic: 41.1 us -> none  [the longest x6 41.1 us: body(): weight_sums = jax.tree.map(jnp.add, weight_sums, weight_grad)]
    all_gather x0 -> x2, waiting for transfers between devices: none -> 35.3 us  [one_stream(): gathered = lax.all_gather(value, 'seg', axis=0)]
  transfers between devices with their start and end apart: 9 -> 5, of which waited for: 7 -> 4; matrix products, arithmetic and copies ran while one was open for 1% -> 6% of each run, Pallas kernels for 0% -> 0%
where the time goes in v1:
time: 493 us; the launch traced here: 492 us
  waiting for transfers between devices  295 us (60%)
  Pallas kernels  63.7 us (13%)
  local copies, waits for them, and re-layouts  44.9 us (9%)
  blocking collectives  37.7 us (8%)
  other arithmetic  34.1 us (7%)
  between operations  13.9 us (3%)
    psum x2, waiting for transfers between devices, body(): lax.psum((whole, jnp.where(half == 0, small, 0)), ('seg', 'doc'))  258 us
    pallas_call x1, Pallas kernels, run_layer(): pl.pallas_call(layer_kernel, out_shape=(jax.ShapeDtypeStruct((ROWS, D), b...  63.7 us
    all_gather x2, waiting for transfers between devices, one_stream(): gathered = lax.all_gather(value, 'seg', axis=0)  35.3 us
    all_to_all x3, blocking collectives, both_streams(): return lax.all_to_all(parts, 'seg', 0, 0)[:2]  25.2 us
    slice x2, local copies, waits for them, and re-layouts, body(): grad_attn = whole[:12].reshape(3, 4, D, D)  17.9 us
    another operation x2, other arithmetic, body(): whole = jnp.stack([jnp.where(half == i, dw, 0) for i in range(2)], 1)  16.3 us
    convert_element_type x1, other arithmetic, body(): whole = whole.astype(f32)  13.8 us
    all_gather x1, blocking collectives, one_stream(): gathered = lax.all_gather(value, 'seg', axis=0)  12.5 us
  transfers between devices with their start and end apart: 5, of which 4 were waited for; matrix products, arithmetic and copies ran while one was open for 6% of the time, Pallas kernels for 0%

profile of v1, /device:TPU:1, one launch (start us, length us, event | category | flops | bytes accessed | tf_op | source)
XLA Modules:
  0.0 492.5 jit_solution(517417538706482456)
XLA Ops:
  7.2 0.0 copy-start
  7.2 0.0 all-gather.6.cloned.1.call-start
  7.2 0.7 all-gather.6.cloned.1.call-update
  7.9 0.0 all-gather.8.cloned.1.call-start
  8.0 0.7 all-gather.8.cloned.1.call-update
  8.7 0.0 all-reduce.5.cloned.1.call-start
  8.8 0.9 reduce_window_sum.11
  9.6 1.3 copy.34.fb_ref
  11.0 0.5 fusion.ends_ref
  11.5 0.0 copy-done
  11.5 0.6 dynamic-slice_bitcast_fusion.mem_ref
  12.1 12.5 %all-gather.2 = bf16[8,64,512]{2,1,0:T(8,128)(2,1)S(1)} all-gather(bf16[2,64,512]{2,1,0:T(8,128)(2,1)} %param.21), channel_id=4, replica_groups=mesh['seg'=4,'doc'=32] {'seg'}, dimensions={0}, use_global_device_ids=true | all-gather | bytes 655360 | tf_op jit(solution)/shard_map/all_gather | solution.py:364
  24.6 0.7 constant_dynamic-slice_fusion
  25.4 10.6 %all-gather.6.cloned.1.call-done = bf16[8,128,512]{2,1,0:T(8,128)(2,1)} async-done(((bf16[2,128,512]{2,1,0:T(8,128)(2,1)}), bf16[8,128,512]{2,1,0:T(8,128)(2,1)}) %all-gather.6.cloned.1.call-update) | async-done | bytes 1048592 | tf_op jit(solution)/shard_map/all_gather | solution.py:364
  36.0 1.9 constant_dynamic-slice_fusion.2
  37.8 24.7 %all-gather.8.cloned.1.call-done = bf16[8,128,512]{2,1,0:T(8,128)(2,1)} async-done(((bf16[2,128,512]{2,1,0:T(8,128)(2,1)}), bf16[8,128,512]{2,1,0:T(8,128)(2,1)}) %all-gather.8.cloned.1.call-update) | async-done | bytes 1048592 | tf_op jit(solution)/shard_map/all_gather | solution.py:364
  62.5 1.9 constant_dynamic-slice_fusion.1
  64.4 63.7 %layer.1 = (bf16[512,512]{1,0:T(8,128)(2,1)}, bf16[256,512]{1,0:T(8,128)(2,1)}, bf16[512,512]{1,0:T(8,128)(2,1)}, bf16[256,512]{1,0:T(8,128)(2,1)}, bf16[20,256,512]{2,1,0:T(8,128)(2,1)}, /*index=5*/f32[72,512]{1,0:T(8,128)}) custom-call(s32[8]{0:T(128)} %fusion.ends_ref, s32[1]{0:T(128)} %bitcast.1.half_ref, bf16[512,512]{1,0:T(8,128)(2,1)} %bitcast.45, ...), custom_call_target="tpu_custom_call" | custom-call | tf_op jit(solution)/shard_map/layer/pallas_call | solution.py:338
  128.1 1.6 broadcast_select_fusion
  129.7 0.0 all-reduce.5.cloned.1.call-update
  129.7 0.0 all-reduce.3.cloned.1.call-start
  129.7 7.1 %select_bitcast_fusion.1 = (bf16[20,1,256,512]{3,2,0,1:T(8,128)(2,1)}, bf16[20,1,256,512]{3,2,0,1:T(8,128)(2,1)}) fusion(bf16[20,256,512]{2,1,0:T(8,128)(2,1)} %get-tuple-element.20, pred[]{:T(512)S(6)} %eq.9, pred[]{:T(512)S(6)} %eq.10), kind=kLoop, calls=%fused_computation.2 | loop fusion | flops 5242880 | bytes 15728642 | tf_op jit(solution)/shard_map/stack | solution.py:381
  136.9 9.1 %pad_maximum_fusion = bf16[20,2,256,512]{3,2,0,1:T(8,128)(2,1)} fusion(bf16[20,1,256,512]{3,2,0,1:T(8,128)(2,1)} %get-tuple-element.23, bf16[20,1,256,512]{3,2,0,1:T(8,128)(2,1)} %get-tuple-element.22), kind=kLoop, calls=%fused_computation | loop fusion | flops 5242880 | bytes 20971520 | tf_op jit(solution)/shard_map/stack | solution.py:381
  146.0 0.0 copy-start.4
  146.0 0.0 copy-start.3
  146.0 0.0 copy-start.2
  146.0 0.0 all-reduce.3.cloned.1.call-update
  146.1 0.9 copy-done.4
  147.0 7.9 %all_to_all.20 = bf16[4,64,512]{2,1,0:T(8,128)(2,1)S(1)} all-to-all(bf16[4,64,512]{2,1,0:T(8,128)(2,1)S(1)} %bitcast.51), channel_id=1, replica_groups=mesh['seg'=4,'doc'=32] {'seg'}, dimensions={0} | all-to-all | bytes 524288 | tf_op jit(solution)/shard_map/all_to_all | solution.py:378
  154.9 0.0 copy-done.3
  154.9 7.9 %all_to_all.21 = bf16[4,64,512]{2,1,0:T(8,128)(2,1)S(1)} all-to-all(bf16[4,64,512]{2,1,0:T(8,128)(2,1)S(1)} %bitcast.50), channel_id=1, replica_groups=mesh['seg'=4,'doc'=32] {'seg'}, dimensions={0} | all-to-all | bytes 524288 | tf_op jit(solution)/shard_map/all_to_all | solution.py:378
  162.8 0.0 copy-done.2
  162.8 9.4 %all_to_all.22 = bf16[4,128,512]{2,1,0:T(8,128)(2,1)S(1)} all-to-all(bf16[4,128,512]{2,1,0:T(8,128)(2,1)S(1)} %bitcast.49), channel_id=1, replica_groups=mesh['seg'=4,'doc'=32] {'seg'}, dimensions={0} | all-to-all | bytes 1048576 | tf_op jit(solution)/shard_map/all_to_all | solution.py:378
  172.2 3.5 all-to-all-start.2
  175.7 94.9 %all-reduce.5.cloned.1.call-done = f32[72,512]{1,0:T(8,128)} async-done(((f32[72,512]{1,0:T(8,128)}), f32[72,512]{1,0:T(8,128)}) %all-reduce.5.cloned.1.call-update) | async-done | bytes 147472 | tf_op jit(solution)/shard_map/psum | solution.py:382
  270.6 1.3 slice.47
  271.9 1.3 slice.48
  273.2 1.4 slice_reduce_fusion
  274.6 0.7 slice.41
  275.2 0.7 slice_convert_fusion.1
  276.0 0.7 slice.40
  276.7 0.0 all-to-all-done.2
  276.7 0.9 slice_convert_fusion
  277.5 162.9 %all-reduce.3.cloned.1.call-done = bf16[20,2,256,512]{3,2,0,1:T(8,128)(2,1)} async-done(((bf16[20,2,256,512]{3,2,0,1:T(8,128)(2,1)}), bf16[20,2,256,512]{3,2,0,1:T(8,128)(2,1)}) %all-reduce.3.cloned.1.call-update) | async-done | bytes 10485776 | tf_op jit(solution)/shard_map/psum | solution.py:382
  440.5 13.8 %convert_element_type.16 = f32[20,2,256,512]{3,2,0,1:T(8,128)} convert(bf16[20,2,256,512]{3,2,0,1:T(8,128)(2,1)} %all-reduce.3.cloned.1.call-done) | non-fusion elementwise | flops 5242880 | bytes 31457280 | tf_op jit(solution)/shard_map/convert_element_type | solution.py:383
  454.3 0.0 slice-start
  454.3 2.8 slice_bitcast_fusion
  457.1 0.0 slice-start.1
  457.1 2.7 copy.36
  459.8 0.0 slice-start.2
  459.8 4.0 copy.40
  463.8 0.0 slice-done
  463.8 0.0 slice-done.1
  463.8 0.0 slice-done.2
  463.8 6.2 %slice.44 = f32[12,2,256,512]{3,2,0,1:T(8,128)} slice(bf16[20,2,256,512]{3,2,0,1:T(8,128)(2,1)S(1)} %bitcast.39), slice={[0:12], [0:2], [0:256], [0:512]} | slice | bytes 25165824 | tf_op jit(solution)/shard_map/slice | solution.py:384
  470.1 0.0 copy-start.1
  470.1 11.7 %copy.35 = f32[12,2,256,512]{3,2,1,0:T(8,128)} copy(f32[12,2,256,512]{3,2,0,1:T(8,128)} %slice.44) | data formatting | bytes 25165824 | tf_op jit(solution)/shard_map/slice | solution.py:384
  481.8 4.2 slice.46
  485.9 0.0 copy-done.1
  (1 shorter events, 0.0 us)
Async XLA Ops:
  7.2 4.3 copy-start
  7.2 28.8 %all-gather.6.cloned.1.call-start = ((), (), s32[]{:S(2)}) async-start(), calls=%async_computation.6 | async-start | bytes 1310720 | tf_op jit(solution)/shard_map/all_gather | solution.py:364
  7.9 54.6 %all-gather.8.cloned.1.call-start = ((), (), s32[]{:S(2)}) async-start(), calls=%async_computation.7 | async-start | bytes 1310720 | tf_op jit(solution)/shard_map/all_gather | solution.py:364
  8.7 261.9 %all-reduce.5.cloned.1.call-start = ((), (), s32[]{:S(2)}) async-start(), calls=%async_computation.5 | async-start | bytes 294912 | tf_op jit(solution)/shard_map/psum | solution.py:382
  129.7 310.8 %all-reduce.3.cloned.1.call-start = ((), (), s32[]{:S(2)}) async-start(), calls=%async_computation.4 | async-start | bytes 20971520 | tf_op jit(solution)/shard_map/psum | solution.py:382
  146.0 0.9 copy-start.4
  146.0 8.9 %copy-start.3 = (bf16[256,512]{1,0:T(8,128)(2,1)S(1)}, bf16[256,512]{1,0:T(8,128)(2,1)}, u32[]{:S(2)}) copy-start(bf16[256,512]{1,0:T(8,128)(2,1)} %get-tuple-element.17) | copy-start | bytes 786436
  146.0 16.8 %copy-start.2 = (bf16[512,512]{1,0:T(8,128)(2,1)S(1)}, bf16[512,512]{1,0:T(8,128)(2,1)}, u32[]{:S(2)}) copy-start(bf16[512,512]{1,0:T(8,128)(2,1)} %get-tuple-element.16) | copy-start | bytes 1572868
  172.2 104.5 %all-to-all-start.2 = ((bf16[4,128,512]{2,1,0:T(8,128)(2,1)}), bf16[4,128,512]{2,1,0:T(8,128)(2,1)S(1)}, u32[]{:S(2)}, u32[]{:S(2)}) async-start(bf16[4,128,512]{2,1,0:T(8,128)(2,1)} %bitcast.14), calls=%async_computation.2 | async-start | bytes 1048576 | tf_op jit(solution)/shard_map/all_to_all | solution.py:378
  454.3 9.5 %slice-start = ((s8[10485760]{0:T(1024)(128)(4,1)}), s8[4194304]{0:T(1024)(128)(4,1)S(1)}, s32[]{:S(2)}) async-start(s8[10485760]{0:T(1024)(128)(4,1)} %bitcast.38), calls=%async_computation.8 | async-start | bytes 8388608
  457.1 6.7 %slice-start.1 = ((s8[10485760]{0:T(1024)(128)(4,1)}), s8[4194304]{0:T(1024)(128)(4,1)S(1)}, s32[]{:S(2)}) async-start(s8[10485760]{0:T(1024)(128)(4,1)} %bitcast.38), calls=%async_computation.9 | async-start | bytes 8388608
  459.8 4.0 slice-start.2
  470.1 15.9 %copy-start.1 = (bf16[2,64,512]{2,1,0:T(8,128)(2,1)S(1)}, bf16[2,64,512]{2,1,0:T(8,128)(2,1)}, u32[]{:S(2)}) copy-start(bf16[2,64,512]{2,1,0:T(8,128)(2,1)} %param.12) | copy-start | bytes 393220
Sparse Core Ops, SparseCore 0:
  9.7 26.2 all-gather.5
  37.6 24.8 all-gather.7
  129.8 140.6 all-reduce.4
  276.9 163.4 all-reduce.2

commit v2 on v1

--- a/solution.py
+++ b/solution.py
@@ -21,6 +21,10 @@
 FCHUNK = 512
 BLOCK = 256
 NBLOCKS = 20
+LANES = 128
+LANE_CUTS = D // LANES
+FLAT = NBLOCKS * BLOCK * LANE_CUTS
+MESH = pl.DeviceIdType.MESH
 
 f32 = jnp.float32
 bf16 = jnp.bfloat16
@@ -80,7 +84,7 @@
 
 
 def layer_kernel(
-    ends_ref, half_ref,
+    half_ref, len_ref,
     tok_ref, mem_ref, ocot_ref, mcot_ref, attn_ref, win_ref, wout_ref, gains_ref, fw_ref, fb_ref,
     act_ref, mout_ref, gtok_ref, gmem_ref, dw_ref, small_ref,
     h_s, q_s, k_s, v_s, p_s, o_s, xh0_s, rs0_s,
@@ -89,15 +93,17 @@
     t_s, xh3_s, rs3_s, m_s, xh4_s, rs4_s, mlow_s, gate_s, upd_s, mprev_s,
     wq_s, wk_s, wv_s, wp_s, wo_s,
     gup_s, dwq_s, dwk_s, dwv_s, gyl_s, gul_s, gbl_s, dcq_s, dck_s, dcv_s,
-    gb_s, gal_s, dq_s, dk_s, dv_s, gain_s, gm_s,
+    gb_s, gal_s, dq_s, dk_s, dv_s, gain_s, gm_s, bias_s,
 ):
     gain = [gains_ref[i : i + 1, :] for i in range(5)]
 
     def doc_ids(shape, dim, base):
         pos = lax.broadcasted_iota(jnp.int32, shape, dim) + base
         ids = jnp.zeros(shape, jnp.int32)
+        end = jnp.zeros((1, 1), jnp.int32)
         for j in range(NDOC):
-            ids += (ends_ref[j] <= pos).astype(jnp.int32)
+            end += len_ref[0:1, j : j + 1]
+            ids += (end <= pos).astype(jnp.int32)
         return ids
 
     xhat, rstd = norm_stats(tok_ref[...].astype(f32))
@@ -201,6 +207,7 @@
     gm_s[...] = jnp.zeros_like(gm_s)
     gain_s[...] = jnp.zeros_like(gain_s)
     small_ref[...] = jnp.zeros_like(small_ref)
+    bias_s[...] = jnp.zeros_like(bias_s)
 
     def backward(step, carry):
         seg = NSEG - 1 - step
@@ -213,7 +220,7 @@
         gup_s[slots, :] = gup
         xh4 = xh4_s[slots, :]
         small_ref[0:1, :] += jnp.sum(dgate * (xh4 * gain[4]), 0, keepdims=True)
-        small_ref[8:72, 0:128] += jnp.broadcast_to(dgate, (SLOTS, 128))
+        bias_s[...] += jnp.broadcast_to(dgate, (SLOTS, LANES))
         gm = dgate * fw_ref[...]
         g_o0, g_o1 = head_halves(dot_nt(gup, attn_ref[11]))
         for pair in range(PAIRS):
@@ -294,6 +301,7 @@
     gain_s[0:1, :] = jnp.sum(gh * xhat, 0, keepdims=True)
     gtok_ref[...] = (gb_s[...] + norm_back(gh, gain[0], xhat, rs0_s[...])).astype(bf16)
     small_ref[1:6, :] = gain_s[0:5, :]
+    small_ref[6:7, 0:SLOTS] = jnp.transpose(bias_s[...])[0:1, :]
 
     half = half_ref[0]
     cut = pl.ds(pl.multiple_of(half * BLOCK, BLOCK), BLOCK)
@@ -302,16 +310,22 @@
         (n1_s, dcq_s), (mlow_s, dck_s), (mlow_s, dcv_s), (co_s, gbl_s),
         (mlow_s, dwq_s), (t_s, dwk_s), (t_s, dwv_s), (wo_s, gup_s),
     ]
+
+    def put(i, value):
+        value = value.astype(bf16)
+        for j in range(LANE_CUTS):
+            dw_ref[i, j] = value[:, j * LANES : (j + 1) * LANES]
+
     for i, (left, right) in enumerate(pairs):
-        dw_ref[i] = dot_tn(left[:, cut], right[...]).astype(bf16)
+        put(i, dot_tn(left[:, cut], right[...]))
     for i in range(4):
-        dw_ref[12 + i] = dot_tn(n2_s[:, cut], gul_s[:, i * D : (i + 1) * D]).astype(bf16)
+        put(12 + i, dot_tn(n2_s[:, cut], gul_s[:, i * D : (i + 1) * D]))
     for i in range(4):
         cut_i = pl.ds(pl.multiple_of(half * 4 * BLOCK + i * BLOCK, BLOCK), BLOCK)
-        dw_ref[16 + i] = dot_tn(hid_s[:, cut_i], gyl_s[...]).astype(bf16)
-
-
-def run_layer(ends, half, tok, mem, ocot, mcot, attn, win, wout, gains, fw, fb):
+        put(16 + i, dot_tn(hid_s[:, cut_i], gyl_s[...]))
+
+
+def run_layer(half, lens, tok, mem, ocot, mcot, attn, win, wout, gains, fw, fb):
     def rows(dtype=bf16, width=D):
         return pltpu.VMEM((ROWS, width), dtype)
 
@@ -332,6 +346,7 @@
         two(MROWS), rows(), rows(), pltpu.VMEM((NSEG, PAIRS, 2 * SLOTS, SEG), bf16), slots(),
         slots(), slots(), rows(), rows(), rows(), rows(bf16, FF), rows(), rows(), slots(), slots(),
         rows(f32), rows(), rows(), rows(), rows(), pltpu.VMEM((8, D), f32), pltpu.VMEM((SLOTS, D), f32),
+        pltpu.VMEM((SLOTS, LANES), f32),
     ]
     smem = pl.BlockSpec(memory_space=pltpu.SMEM)
     vmem = pl.BlockSpec(memory_space=pltpu.VMEM)
@@ -342,51 +357,472 @@
             jax.ShapeDtypeStruct((MROWS, D), bf16),
             jax.ShapeDtypeStruct((ROWS, D), bf16),
             jax.ShapeDtypeStruct((MROWS, D), bf16),
-            jax.ShapeDtypeStruct((NBLOCKS, BLOCK, D), bf16),
-            jax.ShapeDtypeStruct((72, D), f32),
+            jax.ShapeDtypeStruct((NBLOCKS, LANE_CUTS, BLOCK, LANES), bf16),
+            jax.ShapeDtypeStruct((8, D), f32),
         ),
-        in_specs=[smem] * 2 + [vmem] * 10,
+        in_specs=[smem] + [vmem] * 11,
         out_specs=[vmem] * 6,
         scratch_shapes=scratch,
         compiler_params=pltpu.CompilerParams(vmem_limit_bytes=60 << 20),
         name="layer",
-    )(ends, half, tok, mem, ocot, mcot, attn, win, wout, gains, fw, fb)
+    )(half, lens, tok, mem, ocot, mcot, attn, win, wout, gains, fw, fb)
+
+
+def my_place():
+    doc = lax.axis_index("doc")
+    return lax.axis_index("seg"), doc // 8, (doc // 2) % 4, doc % 2
+
+
+def device_at(x, y, z, core):
+    return (x, y * 8 + z * 2 + core)
+
+
+def remote(src, dst, send_sem, recv_sem, device):
+    return pltpu.make_async_remote_copy(
+        src_ref=src, dst_ref=dst, send_sem=send_sem, recv_sem=recv_sem, device_id=device, device_id_type=MESH
+    )
+
+
+def signal(sem, device):
+    pl.semaphore_signal(sem, inc=1, device_id=device, device_id_type=MESH)
+
+
+def gather_kernel(
+    tok_ref, ocot_ref, mcot_ref, mem_ref, len_ref,
+    tok_out, ocot_out, mcot_out, mem_out, len_out,
+    send_sem, recv_sem, local_sem,
+):
+    x, y, z, core = my_place()
+    owner, stream = x // 2, x % 2
+    barrier = pltpu.get_barrier_semaphore()
+    own = (owner == core).astype(jnp.int32)
+    for src in range(NSEG):
+
+        @pl.when(jnp.logical_or(src != x, owner != core))
+        def _():
+            signal(barrier, device_at(src, y, z, owner))
+
+    pl.semaphore_wait(barrier, 4 - own)
+
+    def copies(src_stream, seg):
+        return [
+            (tok_ref.at[src_stream], tok_out.at[seg]),
+            (ocot_ref.at[src_stream], ocot_out.at[seg]),
+            (mcot_ref.at[src_stream], mcot_out.at[seg]),
+        ]
+
+    for s in range(2):
+        for to_core in range(2):
+            chip = 2 * core + s
+            here = jnp.logical_and(chip == x, core == to_core)
+            for i, (src, dst) in enumerate(copies(s, x)):
+
+                @pl.when(jnp.logical_not(here))
+                def _():
+                    remote(src, dst, send_sem.at[s, to_core, i], recv_sem.at[x, i], device_at(chip, y, z, to_core)).start()
+
+                @pl.when(here)
+                def _():
+                    pltpu.make_async_copy(src, dst, local_sem.at[i]).start()
+
+    for i, (src, dst) in enumerate([(mem_ref, mem_out), (len_ref, len_out)]):
+
+        @pl.when(owner == core)
+        def _():
+            copy = remote(src.at[stream], dst, send_sem.at[2, 0, i], recv_sem.at[4, i], device_at(x, y, z, 1 - core))
+            copy.start()
+            local = pltpu.make_async_copy(src.at[stream], dst, local_sem.at[3 + i])
+            local.start()
+            local.wait()
+            copy.wait_send()
+
+        @pl.when(owner != core)
+        def _():
+            remote(src.at[stream], dst, send_sem.at[2, 0, i], recv_sem.at[4, i], device_at(x, y, z, 1 - core)).wait_recv()
+
+    for s in range(2):
+        for to_core in range(2):
+            chip = 2 * core + s
+            here = jnp.logical_and(chip == x, core == to_core)
+            for i, (src, dst) in enumerate(copies(s, x)):
+
+                @pl.when(jnp.logical_not(here))
+                def _():
+                    remote(src, dst, send_sem.at[s, to_core, i], recv_sem.at[x, i], device_at(chip, y, z, to_core)).wait_send()
+
+                @pl.when(here)
+                def _():
+                    pltpu.make_async_copy(src, dst, local_sem.at[i]).wait()
+
+    for seg in range(NSEG):
+        for i, (src, dst) in enumerate(copies(0, seg)):
+
+            @pl.when(jnp.logical_or(seg != x, owner != core))
+            def _():
+                remote(src, dst, send_sem.at[0, 0, i], recv_sem.at[seg, i], device_at(seg, y, z, owner)).wait_recv()
+
+
+def run_gather(tok, ocot, mcot, mem, lens):
+    hbm = pl.BlockSpec(memory_space=pl.ANY)
+    return pl.pallas_call(
+        gather_kernel,
+        out_shape=(
+            jax.ShapeDtypeStruct((NSEG, SEG, D), bf16),
+            jax.ShapeDtypeStruct((NSEG, SEG, D), bf16),
+            jax.ShapeDtypeStruct((NSEG, SLOTS, D), bf16),
+            jax.ShapeDtypeStruct((SLOTS, D), bf16),
+            jax.ShapeDtypeStruct((8, LANES), jnp.int32),
+        ),
+        in_specs=[hbm] * 5,
+        out_specs=[hbm] * 5,
+        scratch_shapes=[
+            pltpu.SemaphoreType.DMA((3, 2, 3)),
+            pltpu.SemaphoreType.DMA((5, 3)),
+            pltpu.SemaphoreType.DMA((5,)),
+        ],
+        compiler_params=pltpu.CompilerParams(collective_id=1, has_side_effects=True),
+        name="gather_stream",
+    )(tok, ocot, mcot, mem, lens)
+
+
+CHUNKS = ((3, 4, 3), (3, 3, 4))
+UNIT = 16
+
+
+def reduce_kernel(
+    dw_ref, act_ref, mout_ref, gtok_ref, gmem_ref, small_ref,
+    full_ref, act_out, mout_out, gtok_out, gmem_out, small_out,
+    near_s, far_s, e_s, f_s, sums_s,
+    send_sem, recv_sem, out_send, out_recv, small_send, small_recv, local_sem,
+):
+    place = my_place()
+    x, y, z, core = place
+    owner, stream = x // 2, x % 2
+    sibling = device_at(x, y, z, 1 - core)
+    barrier = pltpu.get_barrier_semaphore()
+
+    def along(axis, coordinate):
+        there = list(place)
+        there[axis] = coordinate
+        return device_at(*there)
+
+    for axis in range(3):
+        for step in range(1, 4):
+            signal(barrier, along(axis, (place[axis] + step) % 4))
+    signal(barrier, sibling)
+    for k in range(2):
+
+        @pl.when(jnp.logical_or(2 * core + k != x, owner != core))
+        def _():
+            signal(barrier, device_at(2 * core + k, y, z, owner))
+
+    pl.semaphore_wait(barrier, 12 - (owner == core).astype(jnp.int32))
+
+    def rows(start, count):
+        return pl.ds(pl.multiple_of(start, UNIT), count)
+
+    def result_copies(k):
+        seg = 2 * core + k
+        return [
+            (act_ref.at[rows(seg * SEG, SEG)], act_out),
+            (mout_ref.at[rows(seg * SLOTS, SLOTS)], mout_out),
+            (gtok_ref.at[rows(seg * SEG, SEG)], gtok_out),
+            (gmem_ref.at[rows(seg * SLOTS, SLOTS)], gmem_out),
+        ]
+
+    def results(do):
+        for k in range(2):
+            here = jnp.logical_and(2 * core + k == x, owner == core)
+            peer = device_at(2 * core + k, y, z, owner)
+            for i, (src, dst) in enumerate(result_copies(k)):
+
+                @pl.when(jnp.logical_not(here))
+                def _():
+                    do(
+                        remote(src, dst.at[stream], out_send.at[k, i], out_recv.at[stream, i], peer),
+                        remote(src, dst.at[k], out_send.at[k, i], out_recv.at[k, i], peer),
+                    )
+
+                @pl.when(here)
+                def _():
+                    do(pltpu.make_async_copy(src, dst.at[stream], local_sem.at[i]), None)
+
+    def small_copies(axis):
+        src = small_ref if axis == 0 else sums_s.at[axis - 1, 4]
+        here = place[axis]
+        return [
+            remote(
+                src, sums_s.at[axis, here], small_send.at[axis, step - 1], small_recv.at[axis, step - 1],
+                along(axis, (here + step) % 4),
+            )
+            for step in range(1, 4)
+        ]
+
+    def small_start(axis):
+        sums_s[axis, place[axis]] = small_ref[...] if axis == 0 else sums_s[axis - 1, 4]
+        for copy in small_copies(axis):
+            copy.start()
+
+    def small_finish(axis):
+        for copy in small_copies(axis):
+            copy.wait()
+        total = (sums_s[axis, 0] + sums_s[axis, 1]) + (sums_s[axis, 2] + sums_s[axis, 3])
+        sums_s[axis, 4] = total
+        if axis == 2:
+            small_out[...] = total
+
+    def part_steps(chunk, part):
+        r = CHUNKS[chunk][part] * UNIT
+        base = 64 * UNIT * (sum(sum(c) for c in CHUNKS[:chunk]) + sum(CHUNKS[chunk][:part]))
+        axes = [(part + i) % 3 for i in range(3)]
+        i1, i2, i3 = (place[a] for a in axes)
+        right, left = along(axes[0], (i1 + 1) % 4), along(axes[0], (i1 + 3) % 4)
+        sems = iter(range(40))
+        near, far, mid, low_ = near_s[chunk][part], far_s[chunk][part], e_s[chunk][part], f_s[chunk][part]
+
+        def copy(src, dst, device):
+            i = next(sems)
+            return remote(src, dst, send_sem.at[chunk, part, i], recv_sem.at[chunk, part, i], device)
+
+        def block(b, first=0, count=16):
+            return rows(base + (b % 4) * 16 * r + first * r, count * r)
+
+        def add(refs):
+            total = refs[0][...].astype(f32)
+            for ref in refs[1:]:
+                total += ref[...].astype(f32)
+            return total.astype(bf16)
+
+        half0, half1 = pl.ds(0, 8 * r), pl.ds(8 * r, 8 * r)
+        a = copy(dw_ref.at[block(i1 + 2, 0, 8)], near.at[0], right)
+        b = copy(dw_ref.at[block(i1 + 2, 8, 8)], near.at[1], left)
+        c1 = copy(dw_ref.at[block(i1 + 1, 8, 8)], far.at[0, half1], right)
+        d0 = copy(dw_ref.at[block(i1 + 3, 0, 8)], far.at[1, half0], left)
+        for one in (a, b, c1, d0):
+            one.start()
+        yield
+        a.wait()
+        near[0] = add([near.at[0], dw_ref.at[block(i1 + 1, 0, 8)]])
+        c0 = copy(near.at[0], far.at[0, half0], right)
+        c0.start()
+        b.wait()
+        near[1] = add([near.at[1], dw_ref.at[block(i1 + 3, 8, 8)]])
+        d1 = copy(near.at[1], far.at[1, half1], left)
+        d1.start()
+        yield
+        for one in (c1, d0, c0, d1):
+            one.wait()
+        far[0] = add([far.at[0], far.at[1], dw_ref.at[block(i1)]])
+        two = [
+            copy(far.at[0, rows((i2 + s) % 4 * 4 * r, 4 * r)], mid.at[s - 1], along(axes[1], (i2 + s) % 4))
+            for s in range(1, 4)
+        ]
+        for one in two:
+            one.start()
+        yield
+        for one in two:
+            one.wait()
+        mid[0] = add([mid.at[0], mid.at[1], mid.at[2], far.at[0, rows(i2 * 4 * r, 4 * r)]])
+        three = [
+            copy(mid.at[0, rows((i3 + s) % 4 * r, r)], low_.at[s - 1], along(axes[2], (i3 + s) % 4))
+            for s in range(1, 4)
+        ]
+        for one in three:
+            one.start()
+        yield
+        for one in three:
+            one.wait()
+        mine = full_ref.at[core]
+        home = block(i1, i2 * 4 + i3, 1)
+        mine[home, :] = add([low_.at[0], low_.at[1], low_.at[2], mid.at[0, rows(i3 * r, r)]])
+        back = [copy(mine.at[home], mine.at[home], along(axes[2], (i3 + s) % 4)) for s in range(1, 4)]
+        for one in back:
+            one.start()
+        yield
+        for one in back:
+            one.wait()
+        home = block(i1, i2 * 4, 4)
+        back = [copy(mine.at[home], mine.at[home], along(axes[1], (i2 + s) % 4)) for s in range(1, 4)]
+        for one in back:
+            one.start()
+        yield
+        for one in back:
+            one.wait()
+        home = block(i1)
+        to_right = copy(mine.at[home], mine.at[home], right)
+        to_left = copy(mine.at[home], mine.at[home], left)
+        over = [copy(mine.at[home], mine.at[home], sibling)]
+        for one in (to_right, to_left, over[0]):
+            one.start()
+        yield
+        to_right.wait()
+        from_left = block(i1 + 3)
+        on_right = copy(mine.at[block(i1 + 3, 0, 8)], mine.at[block(i1 + 3, 0, 8)], right)
+        on_right.start()
+        over.append(copy(mine.at[from_left], mine.at[from_left], sibling))
+        over[-1].start()
+        to_left.wait()
+        from_right = block(i1 + 1)
+        on_left = copy(mine.at[block(i1 + 1, 8, 8)], mine.at[block(i1 + 1, 8, 8)], left)
+        on_left.start()
+        over.append(copy(mine.at[from_right], mine.at[from_right], sibling))
+        over[-1].start()
+        yield
+        on_right.wait()
+        on_left.wait()
+        opposite = block(i1 + 2)
+        over.append(copy(mine.at[opposite], mine.at[opposite], sibling))
+        over[-1].start()
+        yield
+        for one in over:
+            one.wait()
+        yield
+
+    def chunk_steps(chunk):
+        parts = [part_steps(chunk, part) for part in range(3)]
+        for _ in range(10):
+            for part in parts:
+                next(part)
+            yield
+
+    first, second = chunk_steps(0), chunk_steps(1)
+    next(first)
+    results(lambda copy, back: copy.start())
+    small_start(0)
+    next(first)
+    next(second)
+    next(first)
+    small_finish(0)
+    small_start(1)
+    next(second)
+    next(first)
+    small_finish(1)
+    small_start(2)
+    next(second)
+    next(first)
+    small_finish(2)
+    for _ in range(5):
+        next(second)
+        next(first)
+    next(second)
+    next(second)
+
+    def finish(copy, back):
+        if back is None:
+            copy.wait()
+        else:
+            copy.wait_send()
+            back.wait_recv()
+
+    results(finish)
+
+
+def run_reduce(dw, acts, mems, gtok, gmem, small):
+    vmem = pl.BlockSpec(memory_space=pltpu.VMEM)
+    hbm = pl.BlockSpec(memory_space=pl.ANY)
+
+    def buffers(*shape_of):
+        return [[pltpu.VMEM(shape_of[0](count * UNIT), bf16) for count in chunk] for chunk in CHUNKS]
+
+    return pl.pallas_call(
+        reduce_kernel,
+        out_shape=(
+            jax.ShapeDtypeStruct((2, FLAT, LANES), bf16),
+            jax.ShapeDtypeStruct((2, SEG, D), bf16),
+            jax.ShapeDtypeStruct((2, SLOTS, D), bf16),
+            jax.ShapeDtypeStruct((2, SEG, D), bf16),
+            jax.ShapeDtypeStruct((2, SLOTS, D), bf16),
+            jax.ShapeDtypeStruct((8, D), f32),
+        ),
+        in_specs=[vmem] + [hbm] * 4 + [vmem],
+        out_specs=[vmem] + [hbm] * 4 + [vmem],
+        scratch_shapes=[
+            buffers(lambda r: (2, 8 * r, LANES)),
+            buffers(lambda r: (2, 16 * r, LANES)),
+            buffers(lambda r: (3, 4 * r, LANES)),
+            buffers(lambda r: (3, r, LANES)),
+            pltpu.VMEM((3, 5, 8, D), f32),
+            pltpu.SemaphoreType.DMA((2, 3, 32)),
+            pltpu.SemaphoreType.DMA((2, 3, 32)),
+            pltpu.SemaphoreType.DMA((2, 4)),
+            pltpu.SemaphoreType.DMA((2, 4)),
+            pltpu.SemaphoreType.DMA((3, 3)),
+            pltpu.SemaphoreType.DMA((3, 3)),
+            pltpu.SemaphoreType.DMA((4,)),
+        ],
+        compiler_params=pltpu.CompilerParams(collective_id=2, has_side_effects=True, vmem_limit_bytes=60 << 20),
+        name="reduce_gradients",
+    )(dw, acts, mems, gtok, gmem, small)
+
+
+def widen_kernel(full_ref, attn_ref, in_ref, out_ref, full_s, wide_s, load_sem, store_sem):
+    def load(i):
+        return [
+            pltpu.make_async_copy(full_ref.at[half, i], full_s.at[i, half], load_sem.at[i, half]) for half in range(2)
+        ]
+
+    def target(i, half):
+        if i < 12:
+            return attn_ref.at[i, pl.ds(half * BLOCK, BLOCK), :]
+        if i < 16:
+            return in_ref.at[pl.ds(half * BLOCK, BLOCK), pl.ds((i - 12) * D, D)]
+        return out_ref.at[pl.ds(half * 4 * BLOCK + (i - 16) * BLOCK, BLOCK), :]
+
+    def store(i, half):
+        return pltpu.make_async_copy(wide_s.at[i, half], target(i, half), store_sem.at[i, half])
+
+    for i in range(NBLOCKS):
+        for copy in load(i):
+            copy.start()
+    for i in range(NBLOCKS):
+        for half, copy in enumerate(load(i)):
+            copy.wait()
+            for j in range(LANE_CUTS):
+                wide_s[i, half, :, j * LANES : (j + 1) * LANES] = full_s[i, half, j].astype(f32)
+            store(i, half).start()
+    for i in range(NBLOCKS):
+        for half in range(2):
+            store(i, half).wait()
+
+
+def run_widen(full):
+    hbm = pl.BlockSpec(memory_space=pl.ANY)
+    return pl.pallas_call(
+        widen_kernel,
+        out_shape=(
+            jax.ShapeDtypeStruct((12, D, D), f32),
+            jax.ShapeDtypeStruct((D, FF), f32),
+            jax.ShapeDtypeStruct((FF, D), f32),
+        ),
+        in_specs=[hbm],
+        out_specs=[hbm] * 3,
+        scratch_shapes=[
+            pltpu.VMEM((NBLOCKS, 2, LANE_CUTS, BLOCK, LANES), bf16),
+            pltpu.VMEM((NBLOCKS, 2, BLOCK, D), f32),
+            pltpu.SemaphoreType.DMA((NBLOCKS, 2)),
+            pltpu.SemaphoreType.DMA((NBLOCKS, 2)),
+        ],
+        compiler_params=pltpu.CompilerParams(vmem_limit_bytes=60 << 20),
+        name="widen_gradients",
+    )(full)
 
 
 def body(
     tokens, memory_start, doc_lengths, attn_weights, ffn_in, ffn_out, gains, forget_w, forget_bias,
     out_cotangent, memory_cotangent,
 ):
-    section = lax.axis_index("seg")
-    stream, half = section % 2, section // 2
-
-    def one_stream(value):
-        gathered = lax.all_gather(value, "seg", axis=0)
-        picked = lax.dynamic_index_in_dim(gathered, stream, 1, keepdims=False)
-        return picked.reshape(-1, D)
-
-    ends = lax.dynamic_index_in_dim(jnp.cumsum(doc_lengths, -1).astype(jnp.int32), stream, 0, keepdims=False)
+    lens = jnp.broadcast_to(jnp.pad(doc_lengths, ((0, 0), (0, LANES - NDOC)))[:, None, :], (2, 8, LANES))
+    tok, ocot, mcot, mem, lens = run_gather(tokens, out_cotangent, memory_cotangent, memory_start, lens)
+    half = (lax.axis_index("doc") % 2).reshape(1).astype(jnp.int32)
     acts, mems, gtok, gmem, dw, small = run_layer(
-        ends, half.reshape(1).astype(jnp.int32),
-        one_stream(tokens), lax.dynamic_index_in_dim(memory_start, stream, 0, keepdims=False),
-        one_stream(out_cotangent), one_stream(memory_cotangent),
+        half, lens, tok.reshape(ROWS, D), mem, ocot.reshape(ROWS, D), mcot.reshape(MROWS, D),
         attn_weights.reshape(12, D, D), ffn_in, ffn_out, gains, forget_w.reshape(1, D), forget_bias.reshape(SLOTS, 1),
     )
-
-    def both_streams(value):
-        parts = value.reshape(NSEG, -1, D)
-        return lax.all_to_all(parts, "seg", 0, 0)[:2]
-
-    acts, mems, gtok, gmem = (both_streams(v) for v in (acts, mems, gtok, gmem))
-    whole = jnp.stack([jnp.where(half == i, dw, 0) for i in range(2)], 1)
-    whole, small = lax.psum((whole, jnp.where(half == 0, small, 0)), ("seg", "doc"))
-    whole = whole.astype(f32)
-    grad_attn = whole[:12].reshape(3, 4, D, D)
-    grad_in = whole[12:16].transpose(1, 2, 0, 3).reshape(D, FF)
-    grad_out = whole[16:20].transpose(1, 0, 2, 3).reshape(FF, D)
+    full, acts, mems, gtok, gmem, small = run_reduce(dw.reshape(FLAT, LANES), acts, mems, gtok, gmem, small)
+    grad_attn, grad_in, grad_out = run_widen(full.reshape(2, NBLOCKS, LANE_CUTS, BLOCK, LANES))
     return (
-        acts, mems, gtok.astype(f32), gmem.astype(f32), grad_attn, grad_in, grad_out,
-        small[1:6], small[0], small[8:72, 0],
+        acts, mems, gtok.astype(f32), gmem.astype(f32), grad_attn.reshape(3, 4, D, D), grad_in, grad_out,
+        small[1:6], small[0], small[6, :SLOTS],
     )
 
 

time: 493 us -> 180 us (0.37)
  waiting for transfers between devices: 295 us -> 0 us
  Pallas kernels: 63.7 us -> 172 us
  local copies, waits for them, and re-layouts: 44.9 us -> 5.73 us
  blocking collectives: 37.7 us -> 0 us
  other arithmetic: 34.1 us -> 1.58 us
  between operations: 13.9 us -> 0.73 us
    psum x2 -> x0, waiting for transfers between devices: 258 us -> none  [body(): lax.psum((whole, jnp.where(half == 0, small, 0)), ('seg', 'doc'))]
    pallas_call x0 -> x3, Pallas kernels: none -> 108 us  [the longest x1 76.6 us: run_reduce(): pl.pallas_call(reduce_kernel, out_shape=(jax.ShapeDtypeStruct((2, FLAT, L...]
    all_gather x2 -> x0, waiting for transfers between devices: 35.3 us -> none  [one_stream(): gathered = lax.all_gather(value, 'seg', axis=0)]
    all_to_all x3 -> x0, blocking collectives: 25.2 us -> none  [both_streams(): return lax.all_to_all(parts, 'seg', 0, 0)[:2]]
    slice x6 -> x0, local copies, waits for them, and re-layouts: 24.9 us -> none  [the longest x2 17.9 us: body(): grad_attn = whole[:12].reshape(3, 4, D, D)]
    another operation x3 -> x0, other arithmetic: 17.1 us -> none  [the longest x2 16.3 us: body(): whole = jnp.stack([jnp.where(half == i, dw, 0) for i in range(2)], 1)]
    convert_element_type x1 -> x0, other arithmetic: 13.8 us -> none  [body(): whole = whole.astype(f32)]
    all_gather x1 -> x0, blocking collectives: 12.5 us -> none  [one_stream(): gathered = lax.all_gather(value, 'seg', axis=0)]
  transfers between devices with their start and end apart: 5 -> 0, of which waited for: 4 -> 0; matrix products, arithmetic and copies ran while one was open for 6% -> 0% of each run, Pallas kernels for 0% -> 0%
where the time goes in v2:
time: 180 us
  Pallas kernels  172 us (96%)
  local copies, waits for them, and re-layouts  5.73 us (3%)
    pallas_call x1, Pallas kernels, run_reduce(): pl.pallas_call(reduce_kernel, out_shape=(jax.ShapeDtypeStruct((2, FLAT, L...  76.6 us
    pallas_call x1, Pallas kernels, run_layer(): pl.pallas_call(layer_kernel, out_shape=(jax.ShapeDtypeStruct((ROWS, D), b...  63.7 us
    pallas_call x1, Pallas kernels, run_gather(): pl.pallas_call(gather_kernel, out_shape=(jax.ShapeDtypeStruct((NSEG, SEG,...  20.9 us
    pallas_call x1, Pallas kernels, run_widen(): pl.pallas_call(widen_kernel, out_shape=(jax.ShapeDtypeStruct((12, D, D),...  10.9 us

profile of v2, /device:TPU:1, one launch (start us, length us, event | category | flops | bytes accessed | tf_op | source)
XLA Modules:
  0.0 180.1 jit_solution(14681297754650855637)
XLA Ops:
  0.7 0.7 pad.4
  1.3 0.6 broadcast_in_dim.2.len_ref
  1.9 20.9 %gather_stream.1 = (bf16[4,128,512]{2,1,0:T(8,128)(2,1)}, bf16[4,128,512]{2,1,0:T(8,128)(2,1)}, bf16[4,64,512]{2,1,0:T(8,128)(2,1)}, bf16[64,512]{1,0:T(8,128)(2,1)}, s32[8,128]{1,0:T(8,128)}) custom-call(bf16[2,128,512]{2,1,0:T(8,128)(2,1)} %tok_ref.1, bf16[2,128,512]{2,1,0:T(8,128)(2,1)} %ocot_ref.1, bf16[2,64,512]{2,1,0:T(8,128)(2,1)} %mcot_ref.1, ...), custom_call_target="tpu_custom_call" | custom-call | tf_op jit(solution)/shard_map/gather_stream/pallas_call | solution.py:467
  22.8 1.4 copy.21.fb_ref
  24.2 63.7 %layer.1 = (bf16[512,512]{1,0:T(8,128)(2,1)}, bf16[256,512]{1,0:T(8,128)(2,1)}, bf16[512,512]{1,0:T(8,128)(2,1)}, bf16[256,512]{1,0:T(8,128)(2,1)}, bf16[20,4,256,128]{3,2,1,0:T(8,128)(2,1)}, /*index=5*/f32[8,512]{1,0:T(8,128)}) custom-call(s32[1]{0:T(128)} %bitcast.half_ref, s32[8,128]{1,0:T(8,128)} %get-tuple-element.30.len_ref, ...), custom_call_target="tpu_custom_call" | custom-call | tf_op jit(solution)/shard_map/layer/pallas_call | solution.py:353
  87.8 76.6 %reduce_gradients.1 = (bf16[2,20480,128]{2,1,0:T(8,128)(2,1)}, bf16[2,128,512]{2,1,0:T(8,128)(2,1)}, bf16[2,64,512]{2,1,0:T(8,128)(2,1)}, bf16[2,128,512]{2,1,0:...) custom-call(bf16[20480,128]{1,0:T(8,128)(2,1)} %bitcast.15, bf16[512,512]{1,0:T(8,128)(2,1)} %get-tuple-element.36.act_ref, ...), custom_call_target="tpu_custom_call" | custom-call | tf_op jit(solution)/shard_map/reduce_gradients/pallas_call | solution.py:727
  164.5 0.0 copy-start
  164.5 0.0 copy-start.2
  164.5 0.0 copy-start.4
  164.5 0.0 copy-start.1
  164.5 0.0 copy-start.3
  164.5 10.9 %widen_gradients.1 = (f32[12,512,512]{2,1,0:T(8,128)}, f32[512,2048]{1,0:T(8,128)}, f32[2048,512]{1,0:T(8,128)}) custom-call(bf16[2,20,4,256,128]{4,3,2,1,0:T(8,128)(2,1)} %bitcast.13), custom_call_target="tpu_custom_call" | custom-call | tf_op jit(solution)/shard_map/widen_gradients/pallas_call | solution.py:790
  175.4 0.0 copy-done
  175.4 0.9 convert_element_type.6
  176.3 0.0 copy-done.2
  176.3 0.7 convert_element_type.7
  177.0 0.0 copy-done.4
  177.0 0.6 slice.9
  177.6 0.6 slice.10
  178.2 0.5 slice_bitcast_fusion
  178.7 0.0 copy-done.1
  178.7 0.7 copy.24
  179.4 0.0 copy-done.3
  179.4 0.7 copy.25
Async XLA Ops:
  164.5 11.0 %copy-start = (bf16[2,128,512]{2,1,0:T(8,128)(2,1)S(1)}, bf16[2,128,512]{2,1,0:T(8,128)(2,1)}, u32[]{:S(2)}) copy-start(bf16[2,128,512]{2,1,0:T(8,128)(2,1)} %get-tuple-element.43) | copy-start | bytes 786436
  164.5 11.8 %copy-start.2 = (bf16[2,64,512]{2,1,0:T(8,128)(2,1)S(1)}, bf16[2,64,512]{2,1,0:T(8,128)(2,1)}, u32[]{:S(2)}) copy-start(bf16[2,64,512]{2,1,0:T(8,128)(2,1)} %get-tuple-element.44) | copy-start | bytes 393220
  164.5 12.5 %copy-start.4 = (f32[8,512]{1,0:T(8,128)S(1)}, f32[8,512]{1,0:T(8,128)}, u32[]{:S(2)}) copy-start(f32[8,512]{1,0:T(8,128)} %get-tuple-element.49) | copy-start | bytes 49156
  164.5 14.2 %copy-start.1 = (bf16[2,128,512]{2,1,0:T(8,128)(2,1)S(1)}, bf16[2,128,512]{2,1,0:T(8,128)(2,1)}, u32[]{:S(2)}) copy-start(bf16[2,128,512]{2,1,0:T(8,128)(2,1)} %get-tuple-element.60) | copy-start | bytes 786436
  164.5 14.9 %copy-start.3 = (bf16[2,64,512]{2,1,0:T(8,128)(2,1)S(1)}, bf16[2,64,512]{2,1,0:T(8,128)(2,1)}, u32[]{:S(2)}) copy-start(bf16[2,64,512]{2,1,0:T(8,128)(2,1)} %get-tuple-element.61) | copy-start | bytes 393220

commit v3 on v1

v3 whole, which is shorter than its diff:
```python
import functools

import jax
import jax.numpy as jnp
from jax import lax
from jax.experimental import pallas as pl
from jax.experimental.pallas import tpu as pltpu
from jax.sharding import PartitionSpec as P

HEADS = 8
NDOC = 8
D = 512
FF = 2048
SLOTS = 64
SEG = 128
NSEG = 4
ROWS = NSEG * SEG
MROWS = NSEG * SLOTS
PAIRS = 4
PAIR = 128
FCHUNK = 512
BLOCK = 256
NBLOCKS = 20
LANES = 128
LANE_CUTS = D // LANES
FLAT = NBLOCKS * BLOCK * LANE_CUTS
MESH = pl.DeviceIdType.MESH
SCALE = 0.125

f32 = jnp.float32
bf16 = jnp.bfloat16


def dot(a, b):
    return lax.dot_general(a, b, (((1,), (0,)), ((), ())), preferred_element_type=f32)


def dot_nt(a, b):
    return lax.dot_general(a, b, (((1,), (1,)), ((), ())), preferred_element_type=f32)


def dot_tn(a, b):
    return lax.dot_general(a, b, (((0,), (0,)), ((), ())), preferred_element_type=f32)


def norm_stats(values):
    centered = values - jnp.mean(values, -1, keepdims=True)
    rstd = lax.rsqrt(jnp.mean(centered * centered, -1, keepdims=True) + 1e-05)
    return centered * rstd, rstd


def norm_back(grad, gain, xhat, rstd):
    scaled = grad * gain
    mean_one = jnp.mean(scaled, -1, keepdims=True)
    mean_two = jnp.mean(scaled * xhat, -1, keepdims=True)
    return rstd * (scaled - mean_one - xhat * mean_two)


def head_halves(values):
    low_half = lax.broadcasted_iota(jnp.int32, values.shape, 1) % PAIR < PAIR // 2
    return jnp.where(low_half, values, 0.0).astype(bf16), jnp.where(low_half, 0.0, values).astype(bf16)


def join_halves(stacked):
    rows = stacked.shape[0] // 2
    low_half = lax.broadcasted_iota(jnp.int32, (rows, PAIR), 1) < PAIR // 2
    return jnp.where(low_half, stacked[:rows], stacked[rows:])


def softmax_rows(scores):
    expd = jnp.exp(scores - jnp.max(scores, -1, keepdims=True))
    return expd * (1.0 / jnp.sum(expd, -1, keepdims=True))


def softmax_back(probs, grad):
    return probs * (grad - jnp.sum(probs * grad, -1, keepdims=True))


def gelu_both(u):
    square = u * u
    tanh = jnp.tanh(0.7978845608028654 * u * (1.0 + 0.044715 * square))
    half = 0.5 + 0.5 * tanh
    slope = half + u * half * (1.0 - tanh) * (0.7978845608028654 + 0.1070322243 * square)
    return u * half, slope


CHUNKS = ((4, 4, 4), (2, 3, 3))
UNIT = 16

TURNED = (5, 6, 7, 8, 9, 10, 11)


def scratch_buffers():
    def rows(dtype=bf16, width=D):
        return pltpu.VMEM((ROWS, width), dtype)

    def slots(dtype=bf16, width=D):
        return pltpu.VMEM((MROWS, width), dtype)

    def two(count):
        return pltpu.VMEM((2, count, D), bf16)

    def parts(shape_of):
        return [[pltpu.VMEM(shape_of(count * UNIT), bf16) for count in chunk] for chunk in CHUNKS]

    dma = pltpu.SemaphoreType.DMA
    return dict(
        attn=pltpu.VMEM((12, D, D), bf16), win=pltpu.VMEM((D, FF), bf16), wout=pltpu.VMEM((FF, D), bf16),
        attn_t=pltpu.VMEM((len(TURNED), D, D), bf16), win_t=pltpu.VMEM((FF, D), bf16), wout_t=pltpu.VMEM((D, FF), bf16),
        tok=rows(), ocot=rows(), mcot=slots(), mem=pltpu.VMEM((SLOTS, D), bf16),
        lens_own=pltpu.VMEM((8, LANES), jnp.int32), lens=pltpu.VMEM((8, LANES), jnp.int32),
        act=rows(), mout=slots(), gtok=rows(), gmem=slots(),
        h=rows(), q=two(ROWS), k=rows(), v=rows(), p=pltpu.VMEM((NSEG, PAIRS, 2 * SEG, SEG), bf16), o=rows(),
        xh0=rows(), rs0=rows(f32, 1),
        res=rows(f32), n1=rows(), xh1=rows(), rs1=rows(f32, 1), cq=two(ROWS), ck=slots(), cv=slots(),
        cp=pltpu.VMEM((NSEG, PAIRS, 2 * SEG, SLOTS), bf16), co=rows(),
        n2=rows(), xh2=rows(), rs2=rows(f32, 1), hid=rows(bf16, FF), gd=rows(bf16, FF),
        t=rows(), xh3=rows(), rs3=rows(f32, 1),
        xh4=slots(f32), rs4=slots(f32, 1), mlow=slots(), gate=slots(f32, 1), upd=slots(f32),
        mprev=pltpu.VMEM((SLOTS, D), f32),
        wq=two(MROWS), wk=rows(), wv=rows(), wp=pltpu.VMEM((NSEG, PAIRS, 2 * SLOTS, SEG), bf16), wo=slots(),
        gup=slots(), dwq=slots(), dwk=rows(), dwv=rows(), gyl=rows(), gul=rows(bf16, FF), gbl=rows(),
        dcq=rows(), dck=slots(), dcv=slots(),
        gal=rows(), dq=rows(),
        gain=pltpu.VMEM((8, D), f32), gm=pltpu.VMEM((SLOTS, D), f32), bias=pltpu.VMEM((SLOTS, LANES), f32),
        dw=pltpu.VMEM((FLAT, LANES), bf16),
        near=parts(lambda r: (2, 8 * r, LANES)), far=parts(lambda r: (2, 16 * r, LANES)),
        mid=parts(lambda r: (3, 4 * r, LANES)), last=parts(lambda r: (3, r, LANES)),
        small=pltpu.VMEM((3, 5, 8, D), f32),
        in_send=dma((3, 2, 3)), in_recv=dma((5, 3)), in_local=dma((8,)), load=dma((4,)),
        send=dma((2, 3, 32)), recv=dma((2, 3, 32)), own=dma((2, 3)),
        out_send=dma((2, 4)), out_recv=dma((2, 4)), out_local=dma((4,)),
        small_send=dma((3, 3)), small_recv=dma((3, 3)),
    )


def my_place():
    doc = lax.axis_index("doc")
    return lax.axis_index("seg"), doc // 8, (doc // 2) % 4, doc % 2


def device_at(x, y, z, core):
    return (x, y * 8 + z * 2 + core)


def remote(src, dst, send_sem, recv_sem, device):
    return pltpu.make_async_remote_copy(
        src_ref=src, dst_ref=dst, send_sem=send_sem, recv_sem=recv_sem, device_id=device, device_id_type=MESH
    )


def signal(sem, device):
    pl.semaphore_signal(sem, inc=1, device_id=device, device_id_type=MESH)


def fused_kernel(
    tok_ref, ocot_ref, mcot_ref, mem_ref, len_ref, attn_ref, win_ref, wout_ref, gains_ref, fw_ref, fb_ref,
    full_ref, act_out, mout_out, gtok_out, gmem_out, small_out,
    s,
):
    place = my_place()
    x, y, z, core = place
    owner, stream = x // 2, x % 2
    mine_here = owner == core
    sibling = device_at(x, y, z, 1 - core)

    def along(axis, coordinate):
        there = list(place)
        there[axis] = coordinate
        return device_at(*there)

    loads = [
        pltpu.make_async_copy(attn_ref.at[pl.ds(0, 4)], s["attn"].at[pl.ds(0, 4)], s["load"].at[0]),
        pltpu.make_async_copy(attn_ref.at[pl.ds(4, 8)], s["attn"].at[pl.ds(4, 8)], s["load"].at[1]),
        pltpu.make_async_copy(win_ref, s["win"], s["load"].at[2]),
        pltpu.make_async_copy(wout_ref, s["wout"], s["load"].at[3]),
    ]
    for i in (1, 2, 3, 0):
        loads[i].start()

    barrier = pltpu.get_barrier_semaphore()
    for src in range(NSEG):

        @pl.when(jnp.logical_or(src != x, owner != core))
        def _():
            signal(barrier, device_at(src, y, z, owner))

    for axis in range(3):
        for step in range(1, 4):
            signal(barrier, along(axis, (place[axis] + step) % 4))
    signal(barrier, sibling)
    for k in range(2):

        @pl.when(jnp.logical_or(2 * core + k != x, owner != core))
        def _():
            signal(barrier, device_at(2 * core + k, y, z, owner))

    s["lens_own"][...] = jnp.zeros_like(s["lens_own"])
    s["lens_own"][0:2, 0:NDOC] = len_ref[...]
    pl.semaphore_wait(barrier, 16 - 2 * mine_here.astype(jnp.int32))

    arrays = [(tok_ref, s["tok"], SEG), (ocot_ref, s["ocot"], SEG), (mcot_ref, s["mcot"], SLOTS)]

    def gather_sends(i, do):
        src, dst, count = arrays[i]
        for st in range(2):
            chip = 2 * core + st
            for to_core in range(2):
                here = jnp.logical_and(chip == x, core == to_core)
                target = dst.at[pl.ds(pl.multiple_of(x * count, count), count)]

                @pl.when(jnp.logical_not(here))
                def _():
                    do(remote(
                        src.at[st], target, s["in_send"].at[st, to_core, i], s["in_recv"].at[x, i],
                        device_at(chip, y, z, to_core),
                    ))

                @pl.when(here)
                def _():
                    copy = pltpu.make_async_copy(src.at[st], target, s["in_local"].at[i])
                    if do is start:
                        copy.start()
                    else:
                        copy.wait()

    def gather_arrivals(i):
        src, dst, count = arrays[i]
        for seg in range(NSEG):

            @pl.when(jnp.logical_or(seg != x, owner != core))
            def _():
                remote(
                    src.at[0], dst.at[pl.ds(seg * count, count)], s["in_send"].at[0, 0, i], s["in_recv"].at[seg, i],
                    device_at(seg, y, z, owner),
                ).wait_recv()

    def start(copy):
        copy.start()

    def sent(copy):
        copy.wait_send()

    gather_sends(0, start)

    firsts = [(mem_ref.at[stream], s["mem"]), (s["lens_own"], s["lens"])]
    for i, (src, dst) in enumerate(firsts):

        @pl.when(mine_here)
        def _():
            remote(src, dst, s["in_send"].at[2, 0, i], s["in_recv"].at[4, i], sibling).start()
            pltpu.make_async_copy(src, dst, s["in_local"].at[3 + i]).start()

    for load in loads[1:]:
        load.wait()
    for i, index in enumerate(TURNED):
        s["attn_t"][i] = jnp.transpose(s["attn"][index])
    for c in range(0, FF, D):
        s["win_t"][c : c + D, :] = jnp.transpose(s["win"][:, c : c + D])
        s["wout_t"][:, c : c + D] = jnp.transpose(s["wout"][c : c + D, :])
    loads[0].wait()

    for i, (src, dst) in enumerate(firsts):

        @pl.when(mine_here)
        def _():
            remote(src, dst, s["in_send"].at[2, 0, i], s["in_recv"].at[4, i], sibling).wait_send()
            pltpu.make_async_copy(src, dst, s["in_local"].at[3 + i]).wait()

        @pl.when(jnp.logical_not(mine_here))
        def _():
            remote(src, dst, s["in_send"].at[2, 0, i], s["in_recv"].at[4, i], sibling).wait_recv()

    gather_sends(0, sent)
    gather_arrivals(0)
    gather_sends(1, start)
    gather_sends(2, start)

    attn, win, wout = s["attn"], s["win"], s["wout"]
    attn_t = {index: s["attn_t"].at[i] for i, index in enumerate(TURNED)}
    win_t, wout_t = s["win_t"], s["wout_t"]
    gain = [gains_ref[i : i + 1, :] for i in range(5)]
    forget_w = fw_ref[...]
    square = (SLOTS, SLOTS)
    diagonal = lax.broadcasted_iota(jnp.int32, square, 0) == lax.broadcasted_iota(jnp.int32, square, 1)
    forget_bias = jnp.sum(jnp.where(diagonal, jnp.broadcast_to(fb_ref[...], square), 0.0), -1, keepdims=True)

    def doc_ids(shape, dim, base):
        pos = lax.broadcasted_iota(jnp.int32, shape, dim) + base
        ids = jnp.zeros(shape, jnp.int32)
        end = jnp.zeros((1, 1), jnp.int32)
        for j in range(NDOC):
            end += s["lens"][pl.ds(stream, 1), j : j + 1]
            ids += (end <= pos).astype(jnp.int32)
        return ids

    xhat, rstd = norm_stats(s["tok"][...].astype(f32))
    s["xh0"][...] = xhat.astype(bf16)
    s["rs0"][...] = rstd
    h = (xhat * gain[0]).astype(bf16)
    s["h"][...] = h
    s["q"][0], s["q"][1] = head_halves(dot(h, attn[0]) * SCALE)
    s["k"][...] = dot(h, attn[1]).astype(bf16)
    s["v"][...] = dot(h, attn[2]).astype(bf16)

    def self_forward(seg, carry):
        rows = pl.ds(pl.multiple_of(seg * SEG, SEG), SEG)
        same = doc_ids((SEG, SEG), 0, seg * SEG) == doc_ids((SEG, SEG), 1, seg * SEG)
        same = jnp.concatenate([same.astype(jnp.int32)] * 2, 0) > 0
        for pair in range(PAIRS):
            lanes = slice(pair * PAIR, (pair + 1) * PAIR)
            q_both = jnp.concatenate([s["q"][0, rows, lanes], s["q"][1, rows, lanes]], 0)
            scores = jnp.where(same, dot_nt(q_both, s["k"][rows, lanes]), -1e30)
            probs = softmax_rows(scores).astype(bf16)
            s["p"][seg, pair] = probs
            s["o"][rows, lanes] = join_halves(dot(probs, s["v"][rows, lanes])).astype(bf16)
        return carry

    lax.fori_loop(0, NSEG, self_forward, 0)
    res = s["tok"][...].astype(f32) + dot(s["o"][...], attn[3])
    s["res"][...] = res
    xhat, rstd = norm_stats(res)
    s["xh1"][...] = xhat.astype(bf16)
    s["rs1"][...] = rstd
    n1 = (xhat * gain[1]).astype(bf16)
    s["n1"][...] = n1
    s["cq"][0], s["cq"][1] = head_halves(dot(n1, attn[4]) * SCALE)

    s["mprev"][...] = s["mem"][...].astype(f32)

    def forward(seg, carry):
        rows = pl.ds(pl.multiple_of(seg * SEG, SEG), SEG)
        slots = pl.ds(pl.multiple_of(seg * SLOTS, SLOTS), SLOTS)
        mem = s["mprev"][...]
        xhat, rstd = norm_stats(mem)
        s["xh4"][slots, :] = xhat
        s["rs4"][slots, :] = rstd
        m = xhat * gain[4]
        mlow = m.astype(bf16)
        s["mlow"][slots, :] = mlow
        gate = jax.nn.sigmoid(jnp.sum(m * forget_w, -1, keepdims=True) + forget_bias)
        s["gate"][slots, :] = gate
        ck = dot(mlow, attn[5]).astype(bf16)
        cv = dot(mlow, attn[6]).astype(bf16)
        s["ck"][slots, :] = ck
        s["cv"][slots, :] = cv
        wq0, wq1 = head_halves(dot(mlow, attn[8]) * SCALE)
        s["wq"][0, slots, :] = wq0
        s["wq"][1, slots, :] = wq1
        for pair in range(PAIRS):
            lanes = slice(pair * PAIR, (pair + 1) * PAIR)
            q_both = jnp.concatenate([s["cq"][0, rows, lanes], s["cq"][1, rows, lanes]], 0)
            probs = softmax_rows(dot_nt(q_both, ck[:, lanes])).astype(bf16)
            s["cp"][seg, pair] = probs
            s["co"][rows, lanes] = join_halves(dot(probs, cv[:, lanes])).astype(bf16)
        res = s["res"][rows, :] + dot(s["co"][rows, :], attn[7])
        xhat, rstd = norm_stats(res)
        s["xh2"][rows, :] = xhat.astype(bf16)
        s["rs2"][rows, :] = rstd
        n2 = (xhat * gain[2]).astype(bf16)
        s["n2"][rows, :] = n2
        for c in range(0, FF, FCHUNK):
            hid, slope = gelu_both(dot(n2, win[:, c : c + FCHUNK]))
            hid = hid.astype(bf16)
            s["hid"][rows, c : c + FCHUNK] = hid
            s["gd"][rows, c : c + FCHUNK] = slope.astype(bf16)
            res = res + dot(hid, wout[c : c + FCHUNK, :])
        s["act"][rows, :] = res.astype(bf16)
        xhat, rstd = norm_stats(res)
        s["xh3"][rows, :] = xhat.astype(bf16)
        s["rs3"][rows, :] = rstd
        t = (xhat * gain[3]).astype(bf16)
        s["t"][rows, :] = t
        wk = dot(t, attn[9]).astype(bf16)
        wv = dot(t, attn[10]).astype(bf16)
        s["wk"][rows, :] = wk
        s["wv"][rows, :] = wv
        live = doc_ids((2 * SLOTS, SEG), 1, seg * SEG) < NDOC
        for pair in range(PAIRS):
            lanes = slice(pair * PAIR, (pair + 1) * PAIR)
            q_both = jnp.concatenate([wq0[:, lanes], wq1[:, lanes]], 0)
            scores = jnp.where(live, dot_nt(q_both, wk[:, lanes]), -1e30)
            probs = softmax_rows(scores).astype(bf16)
            s["wp"][seg, pair] = probs
            s["wo"][slots, lanes] = join_halves(dot(probs, wv[:, lanes])).astype(bf16)
        update = dot(s["wo"][slots, :], attn[11])
        s["upd"][slots, :] = mem - update
        fresh = (update + gate * (mem - update)).astype(bf16)
        s["mout"][slots, :] = fresh
        s["mprev"][...] = fresh.astype(f32)
        return carry

    lax.fori_loop(0, NSEG, forward, 0)

    def rows_at(first, count):
        return pl.ds(pl.multiple_of(first, UNIT), count)

    def results(indices, do):
        for k in range(2):
            seg = 2 * core + k
            here = jnp.logical_and(seg == x, mine_here)
            peer = device_at(seg, y, z, owner)
            sources = [
                (s["act"].at[rows_at(seg * SEG, SEG)], act_out), (s["mout"].at[rows_at(seg * SLOTS, SLOTS)], mout_out),
                (s["gtok"].at[rows_at(seg * SEG, SEG)], gtok_out), (s["gmem"].at[rows_at(seg * SLOTS, SLOTS)], gmem_out),
            ]
            for i in indices:
                src, dst = sources[i]

                @pl.when(jnp.logical_not(here))
                def _():
                    do(
                        remote(src, dst.at[stream], s["out_send"].at[k, i], s["out_recv"].at[stream, i], peer),
                        remote(src, dst.at[k], s["out_send"].at[k, i], s["out_recv"].at[k, i], peer),
                    )

                @pl.when(here)
                def _():
                    do(pltpu.make_async_copy(src, dst.at[stream], s["out_local"].at[i]), None)

    def results_start(copy, back):
        copy.start()

    def results_finish(copy, back):
        if back is None:
            copy.wait()
        else:
            copy.wait_send()
            back.wait_recv()

    results((0, 1), results_start)
    for i in (1, 2):
        gather_sends(i, sent)
        gather_arrivals(i)

    s["gm"][...] = jnp.zeros_like(s["gm"])
    s["gain"][...] = jnp.zeros_like(s["gain"])
    s["bias"][...] = jnp.zeros_like(s["bias"])

    def backward(step, carry):
        seg = NSEG - 1 - step
        rows = pl.ds(pl.multiple_of(seg * SEG, SEG), SEG)
        slots = pl.ds(pl.multiple_of(seg * SLOTS, SLOTS), SLOTS)
        gz = (s["mcot"][slots, :].astype(f32) + s["gm"][...]).astype(bf16).astype(f32)
        gate = s["gate"][slots, :]
        dgate = jnp.sum(gz * s["upd"][slots, :], -1, keepdims=True) * gate * (1.0 - gate)
        gup = ((1.0 - gate) * gz).astype(bf16)
        s["gup"][slots, :] = gup
        xh4 = s["xh4"][slots, :]
        s["gain"][5:6, :] += jnp.sum(dgate * (xh4 * gain[4]), 0, keepdims=True)
        s["bias"][...] += jnp.broadcast_to(dgate, (SLOTS, LANES))
        gm = dgate * forget_w
        g_o0, g_o1 = head_halves(dot(gup, attn_t[11][...]))
        for pair in range(PAIRS):
            lanes = slice(pair * PAIR, (pair + 1) * PAIR)
            probs = s["wp"][seg, pair]
            g_both = jnp.concatenate([g_o0[:, lanes], g_o1[:, lanes]], 0)
            q_both = jnp.concatenate([s["wq"][0, slots, lanes], s["wq"][1, slots, lanes]], 0)
            ds = softmax_back(probs.astype(f32), dot_nt(g_both, s["wv"][rows, lanes])).astype(bf16)
            s["dwv"][rows, lanes] = dot_tn(probs, g_both).astype(bf16)
            s["dwk"][rows, lanes] = dot_tn(ds, q_both).astype(bf16)
            s["dwq"][slots, lanes] = (join_halves(dot(ds, s["wk"][rows, lanes])) * SCALE).astype(bf16)
        gm = gm + dot(s["dwq"][slots, :], attn_t[8][...])
        gt = dot(s["dwk"][rows, :], attn_t[9][...]) + dot(s["dwv"][rows, :], attn_t[10][...])
        xhat = s["xh3"][rows, :].astype(f32)
        s["gain"][3:4, :] += jnp.sum(gt * xhat, 0, keepdims=True)
        gy = s["ocot"][rows, :].astype(f32) + norm_back(gt, gain[3], xhat, s["rs3"][rows, :])
        gyl = gy.astype(bf16)
        s["gyl"][rows, :] = gyl
        gn2 = jnp.zeros((SEG, D), f32)
        for c in range(0, FF, FCHUNK):
            ghid = dot(gyl, wout_t[:, c : c + FCHUNK])
            gul = (ghid * s["gd"][rows, c : c + FCHUNK].astype(f32)).astype(bf16)
            s["gul"][rows, c : c + FCHUNK] = gul
            gn2 = gn2 + dot(gul, win_t[c : c + FCHUNK, :])
        xhat = s["xh2"][rows, :].astype(f32)
        s["gain"][2:3, :] += jnp.sum(gn2 * xhat, 0, keepdims=True)
        gb = gy + norm_back(gn2, gain[2], xhat, s["rs2"][rows, :])
        s["res"][rows, :] = gb
        gbl = gb.astype(bf16)
        s["gbl"][rows, :] = gbl
        g_o0, g_o1 = head_halves(dot(gbl, attn_t[7][...]))
        for pair in range(PAIRS):
            lanes = slice(pair * PAIR, (pair + 1) * PAIR)
            probs = s["cp"][seg, pair]
            g_both = jnp.concatenate([g_o0[:, lanes], g_o1[:, lanes]], 0)
            q_both = jnp.concatenate([s["cq"][0, rows, lanes], s["cq"][1, rows, lanes]], 0)
            ds = softmax_back(probs.astype(f32), dot_nt(g_both, s["cv"][slots, lanes])).astype(bf16)
            s["dcv"][slots, lanes] = dot_tn(probs, g_both).astype(bf16)
            s["dck"][slots, lanes] = dot_tn(ds, q_both).astype(bf16)
            s["dcq"][rows, lanes] = (join_halves(dot(ds, s["ck"][slots, lanes])) * SCALE).astype(bf16)
        gm = gm + dot(s["dck"][slots, :], attn_t[5][...]) + dot(s["dcv"][slots, :], attn_t[6][...])
        s["gain"][4:5, :] += jnp.sum(gm * xh4, 0, keepdims=True)
        gmem = gate * gz + norm_back(gm, gain[4], xh4, s["rs4"][slots, :])
        gmem = gmem.astype(bf16)
        s["gmem"][slots, :] = gmem
        s["gm"][...] = gmem.astype(f32)
        return carry

    lax.fori_loop(0, NSEG, backward, 0)

    cut = pl.ds(pl.multiple_of(core * BLOCK, BLOCK), BLOCK)

    def put(i, value):
        value = value.astype(bf16)
        for j in range(LANE_CUTS):
            s["dw"][(i * LANE_CUTS + j) * BLOCK : (i * LANE_CUTS + j + 1) * BLOCK, :] = value[:, j * LANES : (j + 1) * LANES]

    def put_products(base, names):
        for i, (left, right) in enumerate(names):
            put(base + i, dot_tn(s[left][:, cut], s[right][...]))

    put_products(0, [("mlow", "dwq"), ("t", "dwk"), ("t", "dwv"), ("wo", "gup")])
    for i in range(4):
        put(4 + i, dot_tn(s["n2"][:, cut], s["gul"][:, i * D : (i + 1) * D]))
    for i in range(4):
        cut_i = pl.ds(pl.multiple_of(core * 4 * BLOCK + i * BLOCK, BLOCK), BLOCK)
        put(8 + i, dot_tn(s["hid"][:, cut_i], s["gyl"][...]))

    def small_copies(axis):
        here = place[axis]
        return [
            remote(
                s["small"].at[axis, here], s["small"].at[axis, here], s["small_send"].at[axis, step - 1],
                s["small_recv"].at[axis, step - 1], along(axis, (here + step) % 4),
            )
            for step in range(1, 4)
        ]

    def small_start(axis, value):
        s["small"][axis, place[axis]] = value
        for copy in small_copies(axis):
            copy.start()

    def small_finish(axis):
        for copy in small_copies(axis):
            copy.wait()
        return (s["small"][axis, 0] + s["small"][axis, 1]) + (s["small"][axis, 2] + s["small"][axis, 3])

    def part_steps(chunk, part):
        r = CHUNKS[chunk][part] * UNIT
        base = 64 * UNIT * (sum(sum(c) for c in CHUNKS[:chunk]) + sum(CHUNKS[chunk][:part]))
        axes = [(part + i) % 3 for i in range(3)]
        i1, i2, i3 = (place[a] for a in axes)
        right, left = along(axes[0], (i1 + 1) % 4), along(axes[0], (i1 + 3) % 4)
        sems = iter(range(40))
        near, far, mid, last = (s[name][chunk][part] for name in ("near", "far", "mid", "last"))
        dw = s["dw"]

        def copy(src, dst, device):
            i = next(sems)
            return remote(src, dst, s["send"].at[chunk, part, i], s["recv"].at[chunk, part, i], device)

        def block(b, first=0, count=16):
            return rows_at(base + (b % 4) * 16 * r + first * r, count * r)

        def add(refs):
            total = refs[0][...].astype(f32)
            for ref in refs[1:]:
                total += ref[...].astype(f32)
            return total.astype(bf16)

        half0, half1 = pl.ds(0, 8 * r), pl.ds(8 * r, 8 * r)
        a = copy(dw.at[block(i1 + 2, 0, 8)], near.at[0], right)
        b = copy(dw.at[block(i1 + 2, 8, 8)], near.at[1], left)
        c1 = copy(dw.at[block(i1 + 1, 8, 8)], far.at[0, half1], right)
        d0 = copy(dw.at[block(i1 + 3, 0, 8)], far.at[1, half0], left)
        for one in (a, b, c1, d0):
            one.start()
        yield
        a.wait()
        near[0] = add([near.at[0], dw.at[block(i1 + 1, 0, 8)]])
        c0 = copy(near.at[0], far.at[0, half0], right)
        c0.start()
        b.wait()
        near[1] = add([near.at[1], dw.at[block(i1 + 3, 8, 8)]])
        d1 = copy(near.at[1], far.at[1, half1], left)
        d1.start()
        yield
        for one in (c1, d0, c0, d1):
            one.wait()
        far[0] = add([far.at[0], far.at[1], dw.at[block(i1)]])
        two = [
            copy(far.at[0, rows_at((i2 + step) % 4 * 4 * r, 4 * r)], mid.at[step - 1], along(axes[1], (i2 + step) % 4))
            for step in range(1, 4)
        ]
        for one in two:
            one.start()
        yield
        for one in two:
            one.wait()
        mid[0] = add([mid.at[0], mid.at[1], mid.at[2], far.at[0, rows_at(i2 * 4 * r, 4 * r)]])
        three = [
            copy(mid.at[0, rows_at((i3 + step) % 4 * r, r)], last.at[step - 1], along(axes[2], (i3 + step) % 4))
            for step in range(1, 4)
        ]
        for one in three:
            one.start()
        yield
        for one in three:
            one.wait()
        mine = full_ref.at[core]
        home = block(i1, i2 * 4 + i3, 1)
        last[0] = add([last.at[0], last.at[1], last.at[2], mid.at[0, rows_at(i3 * r, r)]])
        keep = pltpu.make_async_copy(last.at[0], mine.at[home], s["own"].at[chunk, part])
        back = [copy(last.at[0], mine.at[home], along(axes[2], (i3 + step) % 4)) for step in range(1, 4)]
        for one in [keep] + back:
            one.start()
        yield
        for one in [keep] + back:
            one.wait()
        home = block(i1, i2 * 4, 4)
        back = [copy(mine.at[home], mine.at[home], along(axes[1], (i2 + step) % 4)) for step in range(1, 4)]
        for one in back:
            one.start()
        yield
        for one in back:
            one.wait()
        home = block(i1)
        to_right = copy(mine.at[home], mine.at[home], right)
        to_left = copy(mine.at[home], mine.at[home], left)
        over = [copy(mine.at[home], mine.at[home], sibling)]
        for one in (to_right, to_left, over[0]):
            one.start()
        yield
        to_right.wait()
        from_left = block(i1 + 3)
        on_right = copy(mine.at[block(i1 + 3, 0, 8)], mine.at[block(i1 + 3, 0, 8)], right)
        on_right.start()
        over.append(copy(mine.at[from_left], mine.at[from_left], sibling))
        over[-1].start()
        to_left.wait()
        from_right = block(i1 + 1)
        on_left = copy(mine.at[block(i1 + 1, 8, 8)], mine.at[block(i1 + 1, 8, 8)], left)
        on_left.start()
        over.append(copy(mine.at[from_right], mine.at[from_right], sibling))
        over[-1].start()
        yield
        on_right.wait()
        on_left.wait()
        opposite = block(i1 + 2)
        over.append(copy(mine.at[opposite], mine.at[opposite], sibling))
        over[-1].start()
        yield
        for one in over:
            one.wait()
        yield

    def chunk_steps(chunk):
        parts = [part_steps(chunk, part) for part in range(3)]
        for _ in range(10):
            for part in parts:
                next(part)
            yield

    first, second = chunk_steps(0), chunk_steps(1)
    next(first)

    gn1 = dot_nt(s["dcq"][...], attn[4])
    xhat = s["xh1"][...].astype(f32)
    s["gain"][1:2, :] = jnp.sum(gn1 * xhat, 0, keepdims=True)
    ga = s["res"][...] + norm_back(gn1, gain[1], xhat, s["rs1"][...])
    s["res"][...] = ga
    gal = ga.astype(bf16)
    s["gal"][...] = gal
    g0, g1 = head_halves(dot_nt(gal, attn[3]))
    s["cq"][0] = g0
    s["cq"][1] = g1

    def self_backward(seg, carry):
        rows = pl.ds(pl.multiple_of(seg * SEG, SEG), SEG)
        for pair in range(PAIRS):
            lanes = slice(pair * PAIR, (pair + 1) * PAIR)
            probs = s["p"][seg, pair]
            g_both = jnp.concatenate([s["cq"][0, rows, lanes], s["cq"][1, rows, lanes]], 0)
            q_both = jnp.concatenate([s["q"][0, rows, lanes], s["q"][1, rows, lanes]], 0)
            ds = softmax_back(probs.astype(f32), dot_nt(g_both, s["v"][rows, lanes])).astype(bf16)
            s["gyl"][rows, lanes] = dot_tn(probs, g_both).astype(bf16)
            s["t"][rows, lanes] = dot_tn(ds, q_both).astype(bf16)
            s["dq"][rows, lanes] = (join_halves(dot(ds, s["k"][rows, lanes])) * SCALE).astype(bf16)
        return carry

    lax.fori_loop(0, NSEG, self_backward, 0)
    next(first)
    gh = dot_nt(s["dq"][...], attn[0]) + dot_nt(s["t"][...], attn[1]) + dot_nt(s["gyl"][...], attn[2])
    xhat = s["xh0"][...].astype(f32)
    s["gain"][0:1, :] = jnp.sum(gh * xhat, 0, keepdims=True)
    s["gtok"][...] = (s["res"][...] + norm_back(gh, gain[0], xhat, s["rs0"][...])).astype(bf16)
    s["gain"][6:7, 0:SLOTS] = jnp.sum(jnp.where(diagonal, s["bias"][:, 0:SLOTS], 0.0), 0, keepdims=True)
    put_products(12, [("h", "dq"), ("h", "t"), ("h", "gyl"), ("o", "gal")])
    put_products(16, [("n1", "dcq"), ("mlow", "dck"), ("mlow", "dcv"), ("co", "gbl")])

    next(second)
    small_start(0, s["gain"][...])
    next(first)
    results((2, 3), results_start)
    next(second)
    next(first)
    total = small_finish(0)
    small_start(1, total)
    next(second)
    next(first)
    total = small_finish(1)
    small_start(2, total)
    next(second)
    next(first)
    small_out[...] = small_finish(2)
    next(second)
    next(first)
    next(second)
    next(second)
    next(first)
    next(second)
    next(first)
    next(second)
    next(first)
    next(second)
    results((0, 1, 2, 3), results_finish)


def run_fused(tok, ocot, mcot, mem, lens, attn, win, wout, gains, fw, fb):
    vmem = pl.BlockSpec(memory_space=pltpu.VMEM)
    hbm = pl.BlockSpec(memory_space=pl.ANY)
    return pl.pallas_call(
        fused_kernel,
        out_shape=(
            jax.ShapeDtypeStruct((2, FLAT, LANES), bf16),
            jax.ShapeDtypeStruct((2, SEG, D), bf16),
            jax.ShapeDtypeStruct((2, SLOTS, D), bf16),
            jax.ShapeDtypeStruct((2, SEG, D), bf16),
            jax.ShapeDtypeStruct((2, SLOTS, D), bf16),
            jax.ShapeDtypeStruct((8, D), f32),
        ),
        in_specs=[hbm] * 4 + [vmem] + [hbm] * 3 + [vmem] * 3,
        out_specs=[hbm] * 5 + [vmem],
        scratch_shapes=[scratch_buffers()],
        compiler_params=pltpu.CompilerParams(collective_id=1, has_side_effects=True, vmem_limit_bytes=62 << 20),
        name="layer_and_sums",
    )(tok, ocot, mcot, mem, lens, attn, win, wout, gains, fw, fb)


def widen_kernel(
    full_ref, act_ref, mem_ref, gtok_ref, gmem_ref, small_ref,
    attn_ref, in_ref, out_ref, act_out, mem_out, gtok_out, gmem_out, gains_out, fw_out, fb_out,
    full_s, wide_s, load_sem, store_sem,
):
    def load(i):
        return [
            pltpu.make_async_copy(full_ref.at[half, i], full_s.at[i, half], load_sem.at[i, half]) for half in range(2)
        ]

    def target(i, half):
        if i < 4:
            return attn_ref.at[8 + i, pl.ds(half * BLOCK, BLOCK), :]
        if i < 8:
            return in_ref.at[pl.ds(half * BLOCK, BLOCK), pl.ds((i - 4) * D, D)]
        if i < 12:
            return out_ref.at[pl.ds(half * 4 * BLOCK + (i - 8) * BLOCK, BLOCK), :]
        return attn_ref.at[i - 12, pl.ds(half * BLOCK, BLOCK), :]

    def store(i, half):
        return pltpu.make_async_copy(wide_s.at[i, half], target(i, half), store_sem.at[i, half])

    for i in range(NBLOCKS):
        for copy in load(i):
            copy.start()
    act_out[...] = act_ref[...]
    mem_out[...] = mem_ref[...]
    gtok_out[...] = gtok_ref[...].astype(f32)
    gmem_out[...] = gmem_ref[...].astype(f32)
    gains_out[...] = small_ref[0:5, :]
    fw_out[...] = small_ref[5:6, :]
    fb_out[...] = small_ref[6:7, 0:SLOTS]
    for i in range(NBLOCKS):
        for half, copy in enumerate(load(i)):
            copy.wait()
            for j in range(LANE_CUTS):
                wide_s[i, half, :, j * LANES : (j + 1) * LANES] = full_s[i, half, j].astype(f32)
            store(i, half).start()
    for i in range(NBLOCKS):
        for half in range(2):
            store(i, half).wait()


def run_widen(full, *others):
    hbm = pl.BlockSpec(memory_space=pl.ANY)
    vmem = pl.BlockSpec(memory_space=pltpu.VMEM)
    return pl.pallas_call(
        widen_kernel,
        out_shape=(
            jax.ShapeDtypeStruct((12, D, D), f32),
            jax.ShapeDtypeStruct((D, FF), f32),
            jax.ShapeDtypeStruct((FF, D), f32),
            jax.ShapeDtypeStruct((2, SEG, D), bf16),
            jax.ShapeDtypeStruct((2, SLOTS, D), bf16),
            jax.ShapeDtypeStruct((2, SEG, D), f32),
            jax.ShapeDtypeStruct((2, SLOTS, D), f32),
            jax.ShapeDtypeStruct((5, D), f32),
            jax.ShapeDtypeStruct((1, D), f32),
            jax.ShapeDtypeStruct((1, SLOTS), f32),
        ),
        in_specs=[hbm] + [vmem] * 5,
        out_specs=[hbm] * 3 + [vmem] * 7,
        scratch_shapes=[
            pltpu.VMEM((NBLOCKS, 2, LANE_CUTS, BLOCK, LANES), bf16),
            pltpu.VMEM((NBLOCKS, 2, BLOCK, D), f32),
            pltpu.SemaphoreType.DMA((NBLOCKS, 2)),
            pltpu.SemaphoreType.DMA((NBLOCKS, 2)),
        ],
        compiler_params=pltpu.CompilerParams(vmem_limit_bytes=60 << 20),
        name="widen_gradients",
    )(full, *others)


def body(
    tokens, memory_start, doc_lengths, attn_weights, ffn_in, ffn_out, gains, forget_w, forget_bias,
    out_cotangent, memory_cotangent,
):
    full, *others = run_fused(
        tokens, out_cotangent, memory_cotangent, memory_start, doc_lengths,
        attn_weights.reshape(12, D, D), ffn_in, ffn_out, gains, forget_w.reshape(1, D), forget_bias.reshape(1, SLOTS),
    )
    grad_attn, grad_in, grad_out, acts, mems, gtok, gmem, grad_gains, grad_fw, grad_fb = run_widen(
        full.reshape(2, NBLOCKS, LANE_CUTS, BLOCK, LANES), *others
    )
    return (
        acts, mems, gtok, gmem, grad_attn.reshape(3, 4, D, D), grad_in, grad_out,
        grad_gains, grad_fw.reshape(D), grad_fb.reshape(SLOTS),
    )


def solution(mesh):
    return jax.shard_map(
        body,
        mesh=mesh,
        in_specs=(
            P("doc", "seg", None), P("doc", None, None), P("doc", None), P(), P(), P(), P(), P(), P(),
            P("doc", "seg", None), P("doc", "seg", None),
        ),
        out_specs=(
            P("doc", "seg", None), P("doc", "seg", None), P("doc", "seg", None), P("doc", "seg", None),
            P(), P(), P(), P(), P(), P(),
        ),
        check_vma=False,
    )
```

time: 493 us -> 139 us (0.28)
  waiting for transfers between devices: 295 us -> 0 us
  Pallas kernels: 63.7 us -> 138 us
  local copies, waits for them, and re-layouts: 44.9 us -> 0 us
  blocking collectives: 37.7 us -> 0 us
  other arithmetic: 34.1 us -> 0 us
  between operations: 13.9 us -> 0.84 us
    psum x2 -> x0, waiting for transfers between devices: 258 us -> none  [body(): lax.psum((whole, jnp.where(half == 0, small, 0)), ('seg', 'doc'))]
    pallas_call x1 -> x2, Pallas kernels: 63.7 us -> 138 us  [the longest x1 125 us: run_fused(): pl.pallas_call(fused_kernel, out_shape=(jax.ShapeDtypeStruct((2, FLAT, LA...]
    all_gather x2 -> x0, waiting for transfers between devices: 35.3 us -> none  [one_stream(): gathered = lax.all_gather(value, 'seg', axis=0)]
    slice x8 -> x0, local copies, waits for them, and re-layouts: 27.5 us -> none  [the longest x2 17.9 us: body(): grad_attn = whole[:12].reshape(3, 4, D, D)]
    all_to_all x3 -> x0, blocking collectives: 25.2 us -> none  [both_streams(): return lax.all_to_all(parts, 'seg', 0, 0)[:2]]
    another operation x3 -> x0, other arithmetic: 17.1 us -> none  [the longest x2 16.3 us: body(): whole = jnp.stack([jnp.where(half == i, dw, 0) for i in range(2)], 1)]
    convert_element_type x3 -> x0, other arithmetic: 15.4 us -> none  [the longest x1 13.8 us: body(): whole = whole.astype(f32)]
    all_gather x1 -> x0, blocking collectives: 12.5 us -> none  [one_stream(): gathered = lax.all_gather(value, 'seg', axis=0)]
  transfers between devices with their start and end apart: 5 -> 0, of which waited for: 4 -> 0; matrix products, arithmetic and copies ran while one was open for 6% -> 0% of each run, Pallas kernels for 0% -> 0%
where the time goes in v3:
time: 139 us
  Pallas kernels  138 us (99%)
    pallas_call x1, Pallas kernels, run_fused(): pl.pallas_call(fused_kernel, out_shape=(jax.ShapeDtypeStruct((2, FLAT, LA...  125 us
    pallas_call x1, Pallas kernels, run_widen(): pl.pallas_call(widen_kernel, out_shape=(jax.ShapeDtypeStruct((12, D, D),...  12.8 us

profile of v3, /device:TPU:1, one launch (start us, length us, event | category | flops | bytes accessed | tf_op | source)
XLA Modules:
  0.0 139.1 jit_solution(6182337517563459675)
XLA Ops:
  0.6 125.4 %layer_and_sums.1 = (bf16[2,20480,128]{2,1,0:T(8,128)(2,1)}, bf16[2,128,512]{2,1,0:T(8,128)(2,1)}, bf16[2,64,512]{2,1,0:T(8,128)(2,1)}, bf16[2,128,512]{2,1,0:T(...) custom-call(bf16[2,128,512]{2,1,0:T(8,128)(2,1)} %tok_ref.1, bf16[2,128,512]{2,1,0:T(8,128)(2,1)} %ocot_ref.1, ...), custom_call_target="tpu_custom_call" | custom-call | tf_op jit(solution)/shard_map/layer_and_sums/pallas_call | solution.py:724
  126.1 12.8 %widen_gradients.1 = (f32[12,512,512]{2,1,0:T(8,128)}, f32[512,2048]{1,0:T(8,128)}, f32[2048,512]{1,0:T(8,128)}, bf16[2,128,512]{2,1,0:T(8,128)(2,1)}, bf16[2,64...) custom-call(bf16[2,20,4,256,128]{4,3,2,1,0:T(8,128)(2,1)} %bitcast.7, ...), custom_call_target="tpu_custom_call" | custom-call | tf_op jit(solution)/shard_map/widen_gradients/pallas_call | solution.py:788

commit v4 on v3

--- a/solution.py
+++ b/solution.py
@@ -67,13 +67,34 @@
     return jnp.where(low_half, stacked[:rows], stacked[rows:])
 
 
-def softmax_rows(scores):
-    expd = jnp.exp(scores - jnp.max(scores, -1, keepdims=True))
-    return expd * (1.0 / jnp.sum(expd, -1, keepdims=True))
-
-
-def softmax_back(probs, grad):
-    return probs * (grad - jnp.sum(probs * grad, -1, keepdims=True))
+def attend(queries, keys, values, bias):
+    scores = jnp.concatenate([dot_nt(k, q) for k, q in zip(keys, queries)], 1) + bias
+    expd = jnp.exp(scores - jnp.max(scores, 0, keepdims=True))
+    probs = (expd * (1.0 / jnp.sum(expd, 0, keepdims=True))).astype(bf16)
+    width = queries[0].shape[0]
+    mixed = [join_halves(dot_tn(probs[:, i * width : (i + 1) * width], v)) for i, v in enumerate(values)]
+    return probs, jnp.concatenate(mixed, 1).astype(bf16)
+
+
+def attend_back(probs, grads, queries, keys, values):
+    width = queries[0].shape[0]
+    wide = probs.astype(f32)
+    dp = jnp.concatenate([dot_nt(v, g) for v, g in zip(values, grads)], 1)
+    ds = (wide * (dp - jnp.sum(wide * dp, 0, keepdims=True))).astype(bf16)
+    cuts = [slice(i * width, (i + 1) * width) for i in range(PAIRS)]
+    dq = [join_halves(dot_tn(ds[:, cut], k)) for cut, k in zip(cuts, keys)]
+    dk = [dot(ds[:, cut], q) for cut, q in zip(cuts, queries)]
+    dv = [dot(probs[:, cut], g) for cut, g in zip(cuts, grads)]
+    join = lambda parts: jnp.concatenate(parts, 1)
+    return (join(dq) * SCALE).astype(bf16), join(dk).astype(bf16), join(dv).astype(bf16)
+
+
+def pair_lanes(values):
+    return [values[:, i * PAIR : (i + 1) * PAIR] for i in range(PAIRS)]
+
+
+def pair_queries(first, second):
+    return [jnp.concatenate(halves, 0) for halves in zip(pair_lanes(first), pair_lanes(second))]
 
 
 def gelu_both(u):
@@ -84,7 +105,7 @@
     return u * half, slope
 
 
-CHUNKS = ((4, 4, 4), (2, 3, 3))
+CHUNKS = ((5, 6, 5), (1, 1, 2))
 UNIT = 16
 
 TURNED = (5, 6, 7, 8, 9, 10, 11)
@@ -110,24 +131,24 @@
         tok=rows(), ocot=rows(), mcot=slots(), mem=pltpu.VMEM((SLOTS, D), bf16),
         lens_own=pltpu.VMEM((8, LANES), jnp.int32), lens=pltpu.VMEM((8, LANES), jnp.int32),
         act=rows(), mout=slots(), gtok=rows(), gmem=slots(),
-        h=rows(), q=two(ROWS), k=rows(), v=rows(), p=pltpu.VMEM((NSEG, PAIRS, 2 * SEG, SEG), bf16), o=rows(),
+        h=rows(), q=two(ROWS), k=rows(), v=rows(), p=pltpu.VMEM((NSEG, SEG, HEADS * SEG), bf16), o=rows(),
         xh0=rows(), rs0=rows(f32, 1),
         res=rows(f32), n1=rows(), xh1=rows(), rs1=rows(f32, 1), cq=two(ROWS), ck=slots(), cv=slots(),
-        cp=pltpu.VMEM((NSEG, PAIRS, 2 * SEG, SLOTS), bf16), co=rows(),
+        cp=pltpu.VMEM((NSEG, SLOTS, HEADS * SEG), bf16), co=rows(),
         n2=rows(), xh2=rows(), rs2=rows(f32, 1), hid=rows(bf16, FF), gd=rows(bf16, FF),
         t=rows(), xh3=rows(), rs3=rows(f32, 1),
         xh4=slots(f32), rs4=slots(f32, 1), mlow=slots(), gate=slots(f32, 1), upd=slots(f32),
         mprev=pltpu.VMEM((SLOTS, D), f32),
-        wq=two(MROWS), wk=rows(), wv=rows(), wp=pltpu.VMEM((NSEG, PAIRS, 2 * SLOTS, SEG), bf16), wo=slots(),
+        wq=two(MROWS), wk=rows(), wv=rows(), wp=pltpu.VMEM((NSEG, SEG, HEADS * SLOTS), bf16), wo=slots(),
         gup=slots(), dwq=slots(), dwk=rows(), dwv=rows(), gyl=rows(), gul=rows(bf16, FF), gbl=rows(),
         dcq=rows(), dck=slots(), dcv=slots(),
         gal=rows(), dq=rows(),
         gain=pltpu.VMEM((8, D), f32), gm=pltpu.VMEM((SLOTS, D), f32), bias=pltpu.VMEM((SLOTS, LANES), f32),
         dw=pltpu.VMEM((FLAT, LANES), bf16),
-        near=parts(lambda r: (2, 8 * r, LANES)), far=parts(lambda r: (2, 16 * r, LANES)),
+        near=parts(lambda r: (2, 8 * r, LANES)), far=parts(lambda r: (3, 16 * r, LANES)),
         mid=parts(lambda r: (3, 4 * r, LANES)), last=parts(lambda r: (3, r, LANES)),
         small=pltpu.VMEM((3, 5, 8, D), f32),
-        in_send=dma((3, 2, 3)), in_recv=dma((5, 3)), in_local=dma((8,)), load=dma((4,)),
+        in_send=dma((3, 2, 3)), in_recv=dma((5, 3)), pass_send=dma((4, 3)), pass_recv=dma((4, 3)), in_local=dma((8,)), load=dma((4,)),
         send=dma((2, 3, 32)), recv=dma((2, 3, 32)), own=dma((2, 3)),
         out_send=dma((2, 4)), out_recv=dma((2, 4)), out_local=dma((4,)),
         small_send=dma((3, 3)), small_recv=dma((3, 3)),
@@ -169,6 +190,9 @@
         there[axis] = coordinate
         return device_at(*there)
 
+    def rows_at(first, count):
+        return pl.ds(pl.multiple_of(first, UNIT), count)
+
     loads = [
         pltpu.make_async_copy(attn_ref.at[pl.ds(0, 4)], s["attn"].at[pl.ds(0, 4)], s["load"].at[0]),
         pltpu.make_async_copy(attn_ref.at[pl.ds(4, 8)], s["attn"].at[pl.ds(4, 8)], s["load"].at[1]),
@@ -179,12 +203,8 @@
         loads[i].start()
 
     barrier = pltpu.get_barrier_semaphore()
-    for src in range(NSEG):
-
-        @pl.when(jnp.logical_or(src != x, owner != core))
-        def _():
-            signal(barrier, device_at(src, y, z, owner))
-
+    for step in range(1, 4):
+        signal(barrier, device_at((x + step) % 4, y, z, owner))
     for axis in range(3):
         for step in range(1, 4):
             signal(barrier, along(axis, (place[axis] + step) % 4))
@@ -197,51 +217,63 @@
 
     s["lens_own"][...] = jnp.zeros_like(s["lens_own"])
     s["lens_own"][0:2, 0:NDOC] = len_ref[...]
-    pl.semaphore_wait(barrier, 16 - 2 * mine_here.astype(jnp.int32))
+    pl.semaphore_wait(barrier, 16 - 3 * mine_here.astype(jnp.int32))
 
     arrays = [(tok_ref, s["tok"], SEG), (ocot_ref, s["ocot"], SEG), (mcot_ref, s["mcot"], SLOTS)]
 
-    def gather_sends(i, do):
+    def gather_sends(i, start):
         src, dst, count = arrays[i]
+        half = count // 2
         for st in range(2):
             chip = 2 * core + st
-            for to_core in range(2):
-                here = jnp.logical_and(chip == x, core == to_core)
-                target = dst.at[pl.ds(pl.multiple_of(x * count, count), count)]
-
-                @pl.when(jnp.logical_not(here))
-                def _():
-                    do(remote(
-                        src.at[st], target, s["in_send"].at[st, to_core, i], s["in_recv"].at[x, i],
-                        device_at(chip, y, z, to_core),
-                    ))
-
-                @pl.when(here)
-                def _():
-                    copy = pltpu.make_async_copy(src.at[st], target, s["in_local"].at[i])
-                    if do is start:
-                        copy.start()
-                    else:
-                        copy.wait()
-
-    def gather_arrivals(i):
+
+            @pl.when(chip != x)
+            def _():
+                for to_core in range(2):
+                    copy = remote(
+                        src.at[st, pl.ds(to_core * half, half)], dst.at[rows_at(x * count + to_core * half, half)],
+                        s["in_send"].at[st, to_core, i], s["in_recv"].at[x, i], device_at(chip, y, z, to_core),
+                    )
+                    copy.start() if start else copy.wait_send()
+
+            @pl.when(chip == x)
+            def _():
+                target = dst.at[rows_at(x * count, count)]
+                local = pltpu.make_async_copy(src.at[st], target, s["in_local"].at[i])
+                copy = remote(src.at[st], target, s["in_send"].at[st, 0, i], s["in_recv"].at[x, i], sibling)
+                if start:
+                    local.start()
+                    copy.start()
+                else:
+                    local.wait()
+                    copy.wait_send()
+
+    def gather_forward(i):
         src, dst, count = arrays[i]
-        for seg in range(NSEG):
-
-            @pl.when(jnp.logical_or(seg != x, owner != core))
-            def _():
-                remote(
-                    src.at[0], dst.at[pl.ds(seg * count, count)], s["in_send"].at[0, 0, i], s["in_recv"].at[seg, i],
-                    device_at(seg, y, z, owner),
-                ).wait_recv()
-
-    def start(copy):
-        copy.start()
-
-    def sent(copy):
-        copy.wait_send()
-
-    gather_sends(0, start)
+        half = count // 2
+        copies = []
+        for step in (1, 3, 2):
+            seg = (x + step) % 4
+            part = dst.at[rows_at(seg * count + core * half, half)]
+            remote(
+                part, part, s["in_send"].at[0, 0, i], s["in_recv"].at[seg, i], device_at(seg, y, z, owner)
+            ).wait_recv()
+            copies.append(remote(part, part, s["pass_send"].at[step, i], s["pass_recv"].at[step, i], sibling))
+            copies[-1].start()
+        return copies
+
+    def gather_finish(i, copies):
+        src, dst, count = arrays[i]
+        gather_sends(i, False)
+        for copy in copies:
+            copy.wait()
+
+        @pl.when(jnp.logical_not(mine_here))
+        def _():
+            whole = dst.at[rows_at(x * count, count)]
+            remote(whole, whole, s["in_send"].at[0, 0, i], s["in_recv"].at[x, i], sibling).wait_recv()
+
+    gather_sends(0, True)
 
     firsts = [(mem_ref.at[stream], s["mem"]), (s["lens_own"], s["lens"])]
     for i, (src, dst) in enumerate(firsts):
@@ -271,10 +303,9 @@
         def _():
             remote(src, dst, s["in_send"].at[2, 0, i], s["in_recv"].at[4, i], sibling).wait_recv()
 
-    gather_sends(0, sent)
-    gather_arrivals(0)
-    gather_sends(1, start)
-    gather_sends(2, start)
+    gather_finish(0, gather_forward(0))
+    gather_sends(1, True)
+    gather_sends(2, True)
 
     attn, win, wout = s["attn"], s["win"], s["wout"]
     attn_t = {index: s["attn_t"].at[i] for i, index in enumerate(TURNED)}
@@ -285,14 +316,13 @@
     diagonal = lax.broadcasted_iota(jnp.int32, square, 0) == lax.broadcasted_iota(jnp.int32, square, 1)
     forget_bias = jnp.sum(jnp.where(diagonal, jnp.broadcast_to(fb_ref[...], square), 0.0), -1, keepdims=True)
 
+    ends = []
+    for j in range(NDOC):
+        ends.append(s["lens"][pl.ds(stream, 1), j : j + 1] + (ends[-1] if ends else 0))
+
     def doc_ids(shape, dim, base):
         pos = lax.broadcasted_iota(jnp.int32, shape, dim) + base
-        ids = jnp.zeros(shape, jnp.int32)
-        end = jnp.zeros((1, 1), jnp.int32)
-        for j in range(NDOC):
-            end += s["lens"][pl.ds(stream, 1), j : j + 1]
-            ids += (end <= pos).astype(jnp.int32)
-        return ids
+        return sum((end <= pos).astype(jnp.int32) for end in ends)
 
     xhat, rstd = norm_stats(s["tok"][...].astype(f32))
     s["xh0"][...] = xhat.astype(bf16)
@@ -306,14 +336,10 @@
     def self_forward(seg, carry):
         rows = pl.ds(pl.multiple_of(seg * SEG, SEG), SEG)
         same = doc_ids((SEG, SEG), 0, seg * SEG) == doc_ids((SEG, SEG), 1, seg * SEG)
-        same = jnp.concatenate([same.astype(jnp.int32)] * 2, 0) > 0
-        for pair in range(PAIRS):
-            lanes = slice(pair * PAIR, (pair + 1) * PAIR)
-            q_both = jnp.concatenate([s["q"][0, rows, lanes], s["q"][1, rows, lanes]], 0)
-            scores = jnp.where(same, dot_nt(q_both, s["k"][rows, lanes]), -1e30)
-            probs = softmax_rows(scores).astype(bf16)
-            s["p"][seg, pair] = probs
-            s["o"][rows, lanes] = join_halves(dot(probs, s["v"][rows, lanes])).astype(bf16)
+        bias = jnp.concatenate([jnp.where(same, 0.0, -1e30)] * HEADS, 1)
+        s["p"][seg], s["o"][rows, :] = attend(
+            pair_queries(s["q"][0, rows, :], s["q"][1, rows, :]), pair_lanes(s["k"][rows, :]), pair_lanes(s["v"][rows, :]), bias
+        )
         return carry
 
     lax.fori_loop(0, NSEG, self_forward, 0)
@@ -325,6 +351,8 @@
     n1 = (xhat * gain[1]).astype(bf16)
     s["n1"][...] = n1
     s["cq"][0], s["cq"][1] = head_halves(dot(n1, attn[4]) * SCALE)
+
+    passed = [gather_forward(1), gather_forward(2)]
 
     s["mprev"][...] = s["mem"][...].astype(f32)
 
@@ -347,13 +375,11 @@
         wq0, wq1 = head_halves(dot(mlow, attn[8]) * SCALE)
         s["wq"][0, slots, :] = wq0
         s["wq"][1, slots, :] = wq1
-        for pair in range(PAIRS):
-            lanes = slice(pair * PAIR, (pair + 1) * PAIR)
-            q_both = jnp.concatenate([s["cq"][0, rows, lanes], s["cq"][1, rows, lanes]], 0)
-            probs = softmax_rows(dot_nt(q_both, ck[:, lanes])).astype(bf16)
-            s["cp"][seg, pair] = probs
-            s["co"][rows, lanes] = join_halves(dot(probs, cv[:, lanes])).astype(bf16)
-        res = s["res"][rows, :] + dot(s["co"][rows, :], attn[7])
+        s["cp"][seg], co = attend(
+            pair_queries(s["cq"][0, rows, :], s["cq"][1, rows, :]), pair_lanes(ck), pair_lanes(cv), 0.0
+        )
+        s["co"][rows, :] = co
+        res = s["res"][rows, :] + dot(co, attn[7])
         xhat, rstd = norm_stats(res)
         s["xh2"][rows, :] = xhat.astype(bf16)
         s["rs2"][rows, :] = rstd
@@ -375,15 +401,12 @@
         wv = dot(t, attn[10]).astype(bf16)
         s["wk"][rows, :] = wk
         s["wv"][rows, :] = wv
-        live = doc_ids((2 * SLOTS, SEG), 1, seg * SEG) < NDOC
-        for pair in range(PAIRS):
-            lanes = slice(pair * PAIR, (pair + 1) * PAIR)
-            q_both = jnp.concatenate([wq0[:, lanes], wq1[:, lanes]], 0)
-            scores = jnp.where(live, dot_nt(q_both, wk[:, lanes]), -1e30)
-            probs = softmax_rows(scores).astype(bf16)
-            s["wp"][seg, pair] = probs
-            s["wo"][slots, lanes] = join_halves(dot(probs, wv[:, lanes])).astype(bf16)
-        update = dot(s["wo"][slots, :], attn[11])
+        pos = lax.broadcasted_iota(jnp.int32, (SEG, HEADS * SLOTS), 0) + seg * SEG
+        s["wp"][seg], wo = attend(
+            pair_queries(wq0, wq1), pair_lanes(wk), pair_lanes(wv), jnp.where(pos < ends[-1], 0.0, -1e30)
+        )
+        s["wo"][slots, :] = wo
+        update = dot(wo, attn[11])
         s["upd"][slots, :] = mem - update
         fresh = (update + gate * (mem - update)).astype(bf16)
         s["mout"][slots, :] = fresh
@@ -391,9 +414,6 @@
         return carry
 
     lax.fori_loop(0, NSEG, forward, 0)
-
-    def rows_at(first, count):
-        return pl.ds(pl.multiple_of(first, UNIT), count)
 
     def results(indices, do):
         for k in range(2):
@@ -430,8 +450,7 @@
 
     results((0, 1), results_start)
     for i in (1, 2):
-        gather_sends(i, sent)
-        gather_arrivals(i)
+        gather_finish(i, passed[i - 1])
 
     s["gm"][...] = jnp.zeros_like(s["gm"])
     s["gain"][...] = jnp.zeros_like(s["gain"])
@@ -450,18 +469,16 @@
         s["gain"][5:6, :] += jnp.sum(dgate * (xh4 * gain[4]), 0, keepdims=True)
         s["bias"][...] += jnp.broadcast_to(dgate, (SLOTS, LANES))
         gm = dgate * forget_w
-        g_o0, g_o1 = head_halves(dot(gup, attn_t[11][...]))
-        for pair in range(PAIRS):
-            lanes = slice(pair * PAIR, (pair + 1) * PAIR)
-            probs = s["wp"][seg, pair]
-            g_both = jnp.concatenate([g_o0[:, lanes], g_o1[:, lanes]], 0)
-            q_both = jnp.concatenate([s["wq"][0, slots, lanes], s["wq"][1, slots, lanes]], 0)
-            ds = softmax_back(probs.astype(f32), dot_nt(g_both, s["wv"][rows, lanes])).astype(bf16)
-            s["dwv"][rows, lanes] = dot_tn(probs, g_both).astype(bf16)
-            s["dwk"][rows, lanes] = dot_tn(ds, q_both).astype(bf16)
-            s["dwq"][slots, lanes] = (join_halves(dot(ds, s["wk"][rows, lanes])) * SCALE).astype(bf16)
-        gm = gm + dot(s["dwq"][slots, :], attn_t[8][...])
-        gt = dot(s["dwk"][rows, :], attn_t[9][...]) + dot(s["dwv"][rows, :], attn_t[10][...])
+        dwq, dwk, dwv = attend_back(
+            s["wp"][seg], pair_queries(*head_halves(dot(gup, attn_t[11][...]))),
+            pair_queries(s["wq"][0, slots, :], s["wq"][1, slots, :]),
+            pair_lanes(s["wk"][rows, :]), pair_lanes(s["wv"][rows, :]),
+        )
+        s["dwq"][slots, :] = dwq
+        s["dwk"][rows, :] = dwk
+        s["dwv"][rows, :] = dwv
+        gt = dot(dwk, attn_t[9][...]) + dot(dwv, attn_t[10][...])
+        gm = gm + dot(dwq, attn_t[8][...])
         xhat = s["xh3"][rows, :].astype(f32)
         s["gain"][3:4, :] += jnp.sum(gt * xhat, 0, keepdims=True)
         gy = s["ocot"][rows, :].astype(f32) + norm_back(gt, gain[3], xhat, s["rs3"][rows, :])
@@ -479,17 +496,15 @@
         s["res"][rows, :] = gb
         gbl = gb.astype(bf16)
         s["gbl"][rows, :] = gbl
-        g_o0, g_o1 = head_halves(dot(gbl, attn_t[7][...]))
-        for pair in range(PAIRS):
-            lanes = slice(pair * PAIR, (pair + 1) * PAIR)
-            probs = s["cp"][seg, pair]
-            g_both = jnp.concatenate([g_o0[:, lanes], g_o1[:, lanes]], 0)
-            q_both = jnp.concatenate([s["cq"][0, rows, lanes], s["cq"][1, rows, lanes]], 0)
-            ds = softmax_back(probs.astype(f32), dot_nt(g_both, s["cv"][slots, lanes])).astype(bf16)
-            s["dcv"][slots, lanes] = dot_tn(probs, g_both).astype(bf16)
-            s["dck"][slots, lanes] = dot_tn(ds, q_both).astype(bf16)
-            s["dcq"][rows, lanes] = (join_halves(dot(ds, s["ck"][slots, lanes])) * SCALE).astype(bf16)
-        gm = gm + dot(s["dck"][slots, :], attn_t[5][...]) + dot(s["dcv"][slots, :], attn_t[6][...])
+        dcq, dck, dcv = attend_back(
+            s["cp"][seg], pair_queries(*head_halves(dot(gbl, attn_t[7][...]))),
+            pair_queries(s["cq"][0, rows, :], s["cq"][1, rows, :]),
+            pair_lanes(s["ck"][slots, :]), pair_lanes(s["cv"][slots, :]),
+        )
+        s["dcq"][rows, :] = dcq
+        s["dck"][slots, :] = dck
+        s["dcv"][slots, :] = dcv
+        gm = gm + dot(dck, attn_t[5][...]) + dot(dcv, attn_t[6][...])
         s["gain"][4:5, :] += jnp.sum(gm * xh4, 0, keepdims=True)
         gmem = gate * gz + norm_back(gm, gain[4], xh4, s["rs4"][slots, :])
         gmem = gmem.astype(bf16)
@@ -516,6 +531,7 @@
     for i in range(4):
         cut_i = pl.ds(pl.multiple_of(core * 4 * BLOCK + i * BLOCK, BLOCK), BLOCK)
         put(8 + i, dot_tn(s["hid"][:, cut_i], s["gyl"][...]))
+    put_products(12, [("n1", "dcq"), ("mlow", "dck"), ("mlow", "dcv"), ("co", "gbl")])
 
     def small_copies(axis):
         here = place[axis]
@@ -646,9 +662,79 @@
             one.wait()
         yield
 
+    def short_part_steps(chunk, part):
+        r = CHUNKS[chunk][part] * UNIT
+        base = 64 * UNIT * (sum(sum(c) for c in CHUNKS[:chunk]) + sum(CHUNKS[chunk][:part]))
+        axes = [(part + i) % 3 for i in range(3)]
+        i1, i2, i3 = (place[a] for a in axes)
+        sems = iter(range(40))
+        far, mid, last = (s[name][chunk][part] for name in ("far", "mid", "last"))
+        dw, mine = s["dw"], full_ref.at[core]
+
+        def copy(src, dst, device):
+            i = next(sems)
+            return remote(src, dst, s["send"].at[chunk, part, i], s["recv"].at[chunk, part, i], device)
+
+        def block(first, count):
+            return rows_at(base + first * r, count * r)
+
+        def add(refs):
+            total = refs[0][...].astype(f32)
+            for ref in refs[1:]:
+                total += ref[...].astype(f32)
+            return total.astype(bf16)
+
+        def others(axis, i):
+            return [((i + step) % 4, step - 1, along(axis, (i + step) % 4)) for step in range(1, 4)]
+
+        def all_do(copies, do):
+            for one in copies:
+                getattr(one, do)()
+
+        one = [copy(dw.at[block(b * 16, 16)], far.at[slot], to) for b, slot, to in others(axes[0], i1)]
+        all_do(one, "start")
+        yield
+        all_do(one, "wait")
+        far[0] = add([far.at[0], far.at[1], far.at[2], dw.at[block(i1 * 16, 16)]])
+        two = [
+            copy(far.at[0, rows_at(b * 4 * r, 4 * r)], mid.at[slot], to) for b, slot, to in others(axes[1], i2)
+        ]
+        all_do(two, "start")
+        yield
+        all_do(two, "wait")
+        mid[0] = add([mid.at[0], mid.at[1], mid.at[2], far.at[0, rows_at(i2 * 4 * r, 4 * r)]])
+        three = [copy(mid.at[0, rows_at(b * r, r)], last.at[slot], to) for b, slot, to in others(axes[2], i3)]
+        all_do(three, "start")
+        yield
+        all_do(three, "wait")
+        last[0] = add([last.at[0], last.at[1], last.at[2], mid.at[0, rows_at(i3 * r, r)]])
+        home = block(i1 * 16 + i2 * 4 + i3, 1)
+        keep = pltpu.make_async_copy(last.at[0], mine.at[home], s["own"].at[chunk, part])
+        back = [copy(last.at[0], mine.at[home], to) for _, _, to in others(axes[2], i3)]
+        all_do([keep] + back, "start")
+        yield
+        all_do([keep] + back, "wait")
+        home = block(i1 * 16 + i2 * 4, 4)
+        back = [copy(mine.at[home], mine.at[home], to) for _, _, to in others(axes[1], i2)]
+        all_do(back, "start")
+        yield
+        all_do(back, "wait")
+        home = block(i1 * 16, 16)
+        back = [copy(mine.at[home], mine.at[home], to) for _, _, to in others(axes[0], i1)]
+        over = [copy(mine.at[home], mine.at[home], sibling)]
+        all_do(back + over, "start")
+        yield
+        all_do(back, "wait")
+        for b, _, _ in others(axes[0], i1):
+            over.append(copy(mine.at[block(b * 16, 16)], mine.at[block(b * 16, 16)], sibling))
+            over[-1].start()
+        yield
+        all_do(over, "wait")
+        yield
+
     def chunk_steps(chunk):
-        parts = [part_steps(chunk, part) for part in range(3)]
-        for _ in range(10):
+        parts = [(part_steps if chunk == 0 else short_part_steps)(chunk, part) for part in range(3)]
+        for _ in range(10 if chunk == 0 else 8):
             for part in parts:
                 next(part)
             yield
@@ -669,50 +755,44 @@
 
     def self_backward(seg, carry):
         rows = pl.ds(pl.multiple_of(seg * SEG, SEG), SEG)
-        for pair in range(PAIRS):
-            lanes = slice(pair * PAIR, (pair + 1) * PAIR)
-            probs = s["p"][seg, pair]
-            g_both = jnp.concatenate([s["cq"][0, rows, lanes], s["cq"][1, rows, lanes]], 0)
-            q_both = jnp.concatenate([s["q"][0, rows, lanes], s["q"][1, rows, lanes]], 0)
-            ds = softmax_back(probs.astype(f32), dot_nt(g_both, s["v"][rows, lanes])).astype(bf16)
-            s["gyl"][rows, lanes] = dot_tn(probs, g_both).astype(bf16)
-            s["t"][rows, lanes] = dot_tn(ds, q_both).astype(bf16)
-            s["dq"][rows, lanes] = (join_halves(dot(ds, s["k"][rows, lanes])) * SCALE).astype(bf16)
+        s["dq"][rows, :], s["t"][rows, :], s["gyl"][rows, :] = attend_back(
+            s["p"][seg], pair_queries(s["cq"][0, rows, :], s["cq"][1, rows, :]),
+            pair_queries(s["q"][0, rows, :], s["q"][1, rows, :]),
+            pair_lanes(s["k"][rows, :]), pair_lanes(s["v"][rows, :]),
+        )
         return carry
 
-    lax.fori_loop(0, NSEG, self_backward, 0)
+    lax.fori_loop(0, NSEG - 1, self_backward, 0)
     next(first)
+    lax.fori_loop(NSEG - 1, NSEG, self_backward, 0)
     gh = dot_nt(s["dq"][...], attn[0]) + dot_nt(s["t"][...], attn[1]) + dot_nt(s["gyl"][...], attn[2])
     xhat = s["xh0"][...].astype(f32)
     s["gain"][0:1, :] = jnp.sum(gh * xhat, 0, keepdims=True)
     s["gtok"][...] = (s["res"][...] + norm_back(gh, gain[0], xhat, s["rs0"][...])).astype(bf16)
     s["gain"][6:7, 0:SLOTS] = jnp.sum(jnp.where(diagonal, s["bias"][:, 0:SLOTS], 0.0), 0, keepdims=True)
-    put_products(12, [("h", "dq"), ("h", "t"), ("h", "gyl"), ("o", "gal")])
-    put_products(16, [("n1", "dcq"), ("mlow", "dck"), ("mlow", "dcv"), ("co", "gbl")])
+    put_products(16, [("h", "dq"), ("h", "t"), ("h", "gyl"), ("o", "gal")])
 
     next(second)
     small_start(0, s["gain"][...])
+    results((2, 3), results_start)
     next(first)
-    results((2, 3), results_start)
     next(second)
-    next(first)
     total = small_finish(0)
     small_start(1, total)
+    next(first)
     next(second)
-    next(first)
     total = small_finish(1)
     small_start(2, total)
-    next(second)
-    next(first)
-    small_out[...] = small_finish(2)
-    next(second)
     next(first)
     next(second)
+    small_out[...] = small_finish(2)
+    next(first)
     next(second)
     next(first)
     next(second)
     next(first)
     next(second)
+    next(first)
     next(first)
     next(second)
     results((0, 1, 2, 3), results_finish)
@@ -756,7 +836,7 @@
             return in_ref.at[pl.ds(half * BLOCK, BLOCK), pl.ds((i - 4) * D, D)]
         if i < 12:
             return out_ref.at[pl.ds(half * 4 * BLOCK + (i - 8) * BLOCK, BLOCK), :]
-        return attn_ref.at[i - 12, pl.ds(half * BLOCK, BLOCK), :]
+        return attn_ref.at[i - 8 if i < 16 else i - 16, pl.ds(half * BLOCK, BLOCK), :]
 
     def store(i, half):
         return pltpu.make_async_copy(wide_s.at[i, half], target(i, half), store_sem.at[i, half])

time: 139 us -> 128 us (0.921)
  Pallas kernels: 138 us -> 127 us
    pallas_call x1, Pallas kernels: 125 us -> 115 us  [run_fused(): pl.pallas_call(fused_kernel, out_shape=(jax.ShapeDtypeStruct((2, FLAT, LA...]
where the time goes in v4:
time: 128 us
  Pallas kernels  127 us (99%)
    pallas_call x1, Pallas kernels, run_fused(): pl.pallas_call(fused_kernel, out_shape=(jax.ShapeDtypeStruct((2, FLAT, LA...  115 us
    pallas_call x1, Pallas kernels, run_widen(): pl.pallas_call(widen_kernel, out_shape=(jax.ShapeDtypeStruct((12, D, D),...  12.8 us

profile of v4, /device:TPU:1, one launch (start us, length us, event | category | flops | bytes accessed | tf_op | source)
XLA Modules:
  0.0 128.3 jit_solution(12006272986646956155)
XLA Ops:
  0.6 114.7 %layer_and_sums.1 = (bf16[2,20480,128]{2,1,0:T(8,128)(2,1)}, bf16[2,128,512]{2,1,0:T(8,128)(2,1)}, bf16[2,64,512]{2,1,0:T(8,128)(2,1)}, bf16[2,128,512]{2,1,0:T(...) custom-call(bf16[2,128,512]{2,1,0:T(8,128)(2,1)} %tok_ref.1, bf16[2,128,512]{2,1,0:T(8,128)(2,1)} %ocot_ref.1, ...), custom_call_target="tpu_custom_call" | custom-call | tf_op jit(solution)/shard_map/layer_and_sums/pallas_call | solution.py:804
  115.3 12.8 %widen_gradients.1 = (f32[12,512,512]{2,1,0:T(8,128)}, f32[512,2048]{1,0:T(8,128)}, f32[2048,512]{1,0:T(8,128)}, bf16[2,128,512]{2,1,0:T(8,128)(2,1)}, bf16[2,64...) custom-call(bf16[2,20,4,256,128]{4,3,2,1,0:T(8,128)(2,1)} %bitcast.7, ...), custom_call_target="tpu_custom_call" | custom-call | tf_op jit(solution)/shard_map/widen_gradients/pallas_call | solution.py:868

commit v5 on v4

--- a/solution.py
+++ b/solution.py
@@ -105,7 +105,7 @@
     return u * half, slope
 
 
-CHUNKS = ((5, 6, 5), (1, 1, 2))
+CHUNKS = ((2, 2, 2), (2, 2, 2), (1, 2, 2), (1, 1, 1))
 UNIT = 16
 
 TURNED = (5, 6, 7, 8, 9, 10, 11)
@@ -138,20 +138,20 @@
         n2=rows(), xh2=rows(), rs2=rows(f32, 1), hid=rows(bf16, FF), gd=rows(bf16, FF),
         t=rows(), xh3=rows(), rs3=rows(f32, 1),
         xh4=slots(f32), rs4=slots(f32, 1), mlow=slots(), gate=slots(f32, 1), upd=slots(f32),
-        mprev=pltpu.VMEM((SLOTS, D), f32),
         wq=two(MROWS), wk=rows(), wv=rows(), wp=pltpu.VMEM((NSEG, SEG, HEADS * SLOTS), bf16), wo=slots(),
         gup=slots(), dwq=slots(), dwk=rows(), dwv=rows(), gyl=rows(), gul=rows(bf16, FF), gbl=rows(),
         dcq=rows(), dck=slots(), dcv=slots(),
-        gal=rows(), dq=rows(),
-        gain=pltpu.VMEM((8, D), f32), gm=pltpu.VMEM((SLOTS, D), f32), bias=pltpu.VMEM((SLOTS, LANES), f32),
+        gal=rows(), dq=rows(), dk=rows(), dv=rows(),
+        gain=pltpu.VMEM((8, D), f32), bias=pltpu.VMEM((SLOTS, LANES), f32),
         dw=pltpu.VMEM((FLAT, LANES), bf16),
-        near=parts(lambda r: (2, 8 * r, LANES)), far=parts(lambda r: (3, 16 * r, LANES)),
-        mid=parts(lambda r: (3, 4 * r, LANES)), last=parts(lambda r: (3, r, LANES)),
+        near=parts(lambda r: (2, 8 * r, LANES)), far=parts(lambda r: (2, 16 * r, LANES)),
+        mid=parts(lambda r: (3, 4 * r, LANES)), quad=parts(lambda r: (4, 4 * r, LANES)), last=parts(lambda r: (4 * r, LANES)),
         small=pltpu.VMEM((3, 5, 8, D), f32),
-        in_send=dma((3, 2, 3)), in_recv=dma((5, 3)), pass_send=dma((4, 3)), pass_recv=dma((4, 3)), in_local=dma((8,)), load=dma((4,)),
-        send=dma((2, 3, 32)), recv=dma((2, 3, 32)), own=dma((2, 3)),
+        in_send=dma((2, 2, 3)), in_recv=dma((4, 3)), first_send=dma((2,)), first_recv=dma((2,)),
+        pass_send=dma((3, 3)), pass_recv=dma((3, 3)), in_local=dma((8,)), load=dma((4,)),
+        send=dma((len(CHUNKS),)), recv=dma((len(CHUNKS), 3, 10)), own=dma((len(CHUNKS), 3)),
         out_send=dma((2, 4)), out_recv=dma((2, 4)), out_local=dma((4,)),
-        small_send=dma((3, 3)), small_recv=dma((3, 3)),
+        small_send=dma((3,)), small_recv=dma((3,)),
     )
 
 
@@ -258,7 +258,7 @@
             remote(
                 part, part, s["in_send"].at[0, 0, i], s["in_recv"].at[seg, i], device_at(seg, y, z, owner)
             ).wait_recv()
-            copies.append(remote(part, part, s["pass_send"].at[step, i], s["pass_recv"].at[step, i], sibling))
+            copies.append(remote(part, part, s["pass_send"].at[step - 1, i], s["pass_recv"].at[step - 1, i], sibling))
             copies[-1].start()
         return copies
 
@@ -280,7 +280,7 @@
 
         @pl.when(mine_here)
         def _():
-            remote(src, dst, s["in_send"].at[2, 0, i], s["in_recv"].at[4, i], sibling).start()
+            remote(src, dst, s["first_send"].at[i], s["first_recv"].at[i], sibling).start()
             pltpu.make_async_copy(src, dst, s["in_local"].at[3 + i]).start()
 
     for load in loads[1:]:
@@ -296,12 +296,12 @@
 
         @pl.when(mine_here)
         def _():
-            remote(src, dst, s["in_send"].at[2, 0, i], s["in_recv"].at[4, i], sibling).wait_send()
+            remote(src, dst, s["first_send"].at[i], s["first_recv"].at[i], sibling).wait_send()
             pltpu.make_async_copy(src, dst, s["in_local"].at[3 + i]).wait()
 
         @pl.when(jnp.logical_not(mine_here))
         def _():
-            remote(src, dst, s["in_send"].at[2, 0, i], s["in_recv"].at[4, i], sibling).wait_recv()
+            remote(src, dst, s["first_send"].at[i], s["first_recv"].at[i], sibling).wait_recv()
 
     gather_finish(0, gather_forward(0))
     gather_sends(1, True)
@@ -324,96 +324,125 @@
         pos = lax.broadcasted_iota(jnp.int32, shape, dim) + base
         return sum((end <= pos).astype(jnp.int32) for end in ends)
 
-    xhat, rstd = norm_stats(s["tok"][...].astype(f32))
-    s["xh0"][...] = xhat.astype(bf16)
-    s["rs0"][...] = rstd
-    h = (xhat * gain[0]).astype(bf16)
-    s["h"][...] = h
-    s["q"][0], s["q"][1] = head_halves(dot(h, attn[0]) * SCALE)
-    s["k"][...] = dot(h, attn[1]).astype(bf16)
-    s["v"][...] = dot(h, attn[2]).astype(bf16)
-
-    def self_forward(seg, carry):
-        rows = pl.ds(pl.multiple_of(seg * SEG, SEG), SEG)
+    def row_cut(seg):
+        return slice(seg * SEG, (seg + 1) * SEG)
+
+    def slot_cut(seg):
+        return slice(seg * SLOTS, (seg + 1) * SLOTS)
+
+    def together(*works):
+        works = list(works)
+        while works:
+            for work in list(works):
+                try:
+                    next(work)
+                except StopIteration:
+                    works.remove(work)
+
+    def self_forward(seg):
+        rows = row_cut(seg)
+        tok = s["tok"][rows, :].astype(f32)
+        xhat, rstd = norm_stats(tok)
+        s["xh0"][rows, :] = xhat.astype(bf16)
+        s["rs0"][rows, :] = rstd
+        h = (xhat * gain[0]).astype(bf16)
+        s["h"][rows, :] = h
+        yield
+        q0, q1 = head_halves(dot(h, attn[0]) * SCALE)
+        s["q"][0, rows, :] = q0
+        s["q"][1, rows, :] = q1
+        yield
+        k = dot(h, attn[1]).astype(bf16)
+        v = dot(h, attn[2]).astype(bf16)
+        s["k"][rows, :] = k
+        s["v"][rows, :] = v
+        yield
         same = doc_ids((SEG, SEG), 0, seg * SEG) == doc_ids((SEG, SEG), 1, seg * SEG)
         bias = jnp.concatenate([jnp.where(same, 0.0, -1e30)] * HEADS, 1)
-        s["p"][seg], s["o"][rows, :] = attend(
-            pair_queries(s["q"][0, rows, :], s["q"][1, rows, :]), pair_lanes(s["k"][rows, :]), pair_lanes(s["v"][rows, :]), bias
-        )
-        return carry
-
-    lax.fori_loop(0, NSEG, self_forward, 0)
-    res = s["tok"][...].astype(f32) + dot(s["o"][...], attn[3])
-    s["res"][...] = res
-    xhat, rstd = norm_stats(res)
-    s["xh1"][...] = xhat.astype(bf16)
-    s["rs1"][...] = rstd
-    n1 = (xhat * gain[1]).astype(bf16)
-    s["n1"][...] = n1
-    s["cq"][0], s["cq"][1] = head_halves(dot(n1, attn[4]) * SCALE)
-
-    passed = [gather_forward(1), gather_forward(2)]
-
-    s["mprev"][...] = s["mem"][...].astype(f32)
-
-    def forward(seg, carry):
-        rows = pl.ds(pl.multiple_of(seg * SEG, SEG), SEG)
-        slots = pl.ds(pl.multiple_of(seg * SLOTS, SLOTS), SLOTS)
-        mem = s["mprev"][...]
+        s["p"][seg], o = attend(pair_queries(q0, q1), pair_lanes(k), pair_lanes(v), bias)
+        s["o"][rows, :] = o
+        yield
+        res = tok + dot(o, attn[3])
+        s["res"][rows, :] = res
+        xhat, rstd = norm_stats(res)
+        s["xh1"][rows, :] = xhat.astype(bf16)
+        s["rs1"][rows, :] = rstd
+        n1 = (xhat * gain[1]).astype(bf16)
+        s["n1"][rows, :] = n1
+        yield
+        s["cq"][0, rows, :], s["cq"][1, rows, :] = head_halves(dot(n1, attn[4]) * SCALE)
+        yield
+
+    def forward(seg, mem):
+        rows, slots = row_cut(seg), slot_cut(seg)
         xhat, rstd = norm_stats(mem)
         s["xh4"][slots, :] = xhat
         s["rs4"][slots, :] = rstd
         m = xhat * gain[4]
         mlow = m.astype(bf16)
         s["mlow"][slots, :] = mlow
-        gate = jax.nn.sigmoid(jnp.sum(m * forget_w, -1, keepdims=True) + forget_bias)
-        s["gate"][slots, :] = gate
         ck = dot(mlow, attn[5]).astype(bf16)
         cv = dot(mlow, attn[6]).astype(bf16)
         s["ck"][slots, :] = ck
         s["cv"][slots, :] = cv
-        wq0, wq1 = head_halves(dot(mlow, attn[8]) * SCALE)
-        s["wq"][0, slots, :] = wq0
-        s["wq"][1, slots, :] = wq1
+        yield
         s["cp"][seg], co = attend(
             pair_queries(s["cq"][0, rows, :], s["cq"][1, rows, :]), pair_lanes(ck), pair_lanes(cv), 0.0
         )
         s["co"][rows, :] = co
+        yield
         res = s["res"][rows, :] + dot(co, attn[7])
         xhat, rstd = norm_stats(res)
         s["xh2"][rows, :] = xhat.astype(bf16)
         s["rs2"][rows, :] = rstd
         n2 = (xhat * gain[2]).astype(bf16)
         s["n2"][rows, :] = n2
+        yield
         for c in range(0, FF, FCHUNK):
             hid, slope = gelu_both(dot(n2, win[:, c : c + FCHUNK]))
             hid = hid.astype(bf16)
             s["hid"][rows, c : c + FCHUNK] = hid
             s["gd"][rows, c : c + FCHUNK] = slope.astype(bf16)
             res = res + dot(hid, wout[c : c + FCHUNK, :])
+            yield
         s["act"][rows, :] = res.astype(bf16)
         xhat, rstd = norm_stats(res)
         s["xh3"][rows, :] = xhat.astype(bf16)
         s["rs3"][rows, :] = rstd
         t = (xhat * gain[3]).astype(bf16)
         s["t"][rows, :] = t
+        yield
+        gate = jax.nn.sigmoid(jnp.sum(m * forget_w, -1, keepdims=True) + forget_bias)
+        s["gate"][slots, :] = gate
+        wq0, wq1 = head_halves(dot(mlow, attn[8]) * SCALE)
+        s["wq"][0, slots, :] = wq0
+        s["wq"][1, slots, :] = wq1
         wk = dot(t, attn[9]).astype(bf16)
         wv = dot(t, attn[10]).astype(bf16)
         s["wk"][rows, :] = wk
         s["wv"][rows, :] = wv
+        yield
         pos = lax.broadcasted_iota(jnp.int32, (SEG, HEADS * SLOTS), 0) + seg * SEG
         s["wp"][seg], wo = attend(
             pair_queries(wq0, wq1), pair_lanes(wk), pair_lanes(wv), jnp.where(pos < ends[-1], 0.0, -1e30)
         )
         s["wo"][slots, :] = wo
+        yield
         update = dot(wo, attn[11])
         s["upd"][slots, :] = mem - update
-        fresh = (update + gate * (mem - update)).astype(bf16)
-        s["mout"][slots, :] = fresh
-        s["mprev"][...] = fresh.astype(f32)
-        return carry
-
-    lax.fori_loop(0, NSEG, forward, 0)
+        s["mout"][slots, :] = (update + gate * (mem - update)).astype(bf16)
+        yield
+
+    together(self_forward(0))
+    passed = []
+    for seg in range(NSEG):
+        mem = s["mem"][...] if seg == 0 else s["mout"][slot_cut(seg - 1), :]
+        works = [forward(seg, mem.astype(f32))]
+        if seg < NSEG - 1:
+            works.append(self_forward(seg + 1))
+        together(*works)
+        if seg in (1, 2):
+            passed.append(gather_forward(seg))
 
     def results(indices, do):
         for k in range(2):
@@ -452,67 +481,102 @@
     for i in (1, 2):
         gather_finish(i, passed[i - 1])
 
-    s["gm"][...] = jnp.zeros_like(s["gm"])
     s["gain"][...] = jnp.zeros_like(s["gain"])
     s["bias"][...] = jnp.zeros_like(s["bias"])
 
-    def backward(step, carry):
-        seg = NSEG - 1 - step
-        rows = pl.ds(pl.multiple_of(seg * SEG, SEG), SEG)
-        slots = pl.ds(pl.multiple_of(seg * SLOTS, SLOTS), SLOTS)
-        gz = (s["mcot"][slots, :].astype(f32) + s["gm"][...]).astype(bf16).astype(f32)
+    def backward(seg):
+        rows, slots = row_cut(seg), slot_cut(seg)
+        gz = s["mcot"][slots, :].astype(f32)
+        if seg < NSEG - 1:
+            gz = (gz + s["gmem"][slot_cut(seg + 1), :].astype(f32)).astype(bf16).astype(f32)
         gate = s["gate"][slots, :]
-        dgate = jnp.sum(gz * s["upd"][slots, :], -1, keepdims=True) * gate * (1.0 - gate)
         gup = ((1.0 - gate) * gz).astype(bf16)
         s["gup"][slots, :] = gup
-        xh4 = s["xh4"][slots, :]
-        s["gain"][5:6, :] += jnp.sum(dgate * (xh4 * gain[4]), 0, keepdims=True)
-        s["bias"][...] += jnp.broadcast_to(dgate, (SLOTS, LANES))
-        gm = dgate * forget_w
+        g_wo = head_halves(dot(gup, attn_t[11][...]))
+        yield
         dwq, dwk, dwv = attend_back(
-            s["wp"][seg], pair_queries(*head_halves(dot(gup, attn_t[11][...]))),
-            pair_queries(s["wq"][0, slots, :], s["wq"][1, slots, :]),
+            s["wp"][seg], pair_queries(*g_wo), pair_queries(s["wq"][0, slots, :], s["wq"][1, slots, :]),
             pair_lanes(s["wk"][rows, :]), pair_lanes(s["wv"][rows, :]),
         )
         s["dwq"][slots, :] = dwq
         s["dwk"][rows, :] = dwk
         s["dwv"][rows, :] = dwv
+        yield
         gt = dot(dwk, attn_t[9][...]) + dot(dwv, attn_t[10][...])
-        gm = gm + dot(dwq, attn_t[8][...])
         xhat = s["xh3"][rows, :].astype(f32)
         s["gain"][3:4, :] += jnp.sum(gt * xhat, 0, keepdims=True)
         gy = s["ocot"][rows, :].astype(f32) + norm_back(gt, gain[3], xhat, s["rs3"][rows, :])
         gyl = gy.astype(bf16)
         s["gyl"][rows, :] = gyl
+        yield
         gn2 = jnp.zeros((SEG, D), f32)
         for c in range(0, FF, FCHUNK):
             ghid = dot(gyl, wout_t[:, c : c + FCHUNK])
             gul = (ghid * s["gd"][rows, c : c + FCHUNK].astype(f32)).astype(bf16)
             s["gul"][rows, c : c + FCHUNK] = gul
             gn2 = gn2 + dot(gul, win_t[c : c + FCHUNK, :])
+            yield
         xhat = s["xh2"][rows, :].astype(f32)
         s["gain"][2:3, :] += jnp.sum(gn2 * xhat, 0, keepdims=True)
         gb = gy + norm_back(gn2, gain[2], xhat, s["rs2"][rows, :])
         s["res"][rows, :] = gb
         gbl = gb.astype(bf16)
         s["gbl"][rows, :] = gbl
+        yield
+        g_co = head_halves(dot(gbl, attn_t[7][...]))
+        dgate = jnp.sum(gz * s["upd"][slots, :], -1, keepdims=True) * gate * (1.0 - gate)
+        xh4 = s["xh4"][slots, :]
+        s["gain"][5:6, :] += jnp.sum(dgate * (xh4 * gain[4]), 0, keepdims=True)
+        s["bias"][...] += jnp.broadcast_to(dgate, (SLOTS, LANES))
+        gm = dgate * forget_w + dot(dwq, attn_t[8][...])
+        yield
         dcq, dck, dcv = attend_back(
-            s["cp"][seg], pair_queries(*head_halves(dot(gbl, attn_t[7][...]))),
-            pair_queries(s["cq"][0, rows, :], s["cq"][1, rows, :]),
+            s["cp"][seg], pair_queries(*g_co), pair_queries(s["cq"][0, rows, :], s["cq"][1, rows, :]),
             pair_lanes(s["ck"][slots, :]), pair_lanes(s["cv"][slots, :]),
         )
         s["dcq"][rows, :] = dcq
         s["dck"][slots, :] = dck
         s["dcv"][slots, :] = dcv
+        yield
         gm = gm + dot(dck, attn_t[5][...]) + dot(dcv, attn_t[6][...])
         s["gain"][4:5, :] += jnp.sum(gm * xh4, 0, keepdims=True)
-        gmem = gate * gz + norm_back(gm, gain[4], xh4, s["rs4"][slots, :])
-        gmem = gmem.astype(bf16)
-        s["gmem"][slots, :] = gmem
-        s["gm"][...] = gmem.astype(f32)
-        return carry
-
-    lax.fori_loop(0, NSEG, backward, 0)
+        s["gmem"][slots, :] = (gate * gz + norm_back(gm, gain[4], xh4, s["rs4"][slots, :])).astype(bf16)
+        yield
+
+    def self_backward(seg):
+        rows = row_cut(seg)
+        gn1 = dot_nt(s["dcq"][rows, :], attn[4])
+        yield
+        xhat = s["xh1"][rows, :].astype(f32)
+        s["gain"][1:2, :] += jnp.sum(gn1 * xhat, 0, keepdims=True)
+        ga = s["res"][rows, :] + norm_back(gn1, gain[1], xhat, s["rs1"][rows, :])
+        gal = ga.astype(bf16)
+        s["gal"][rows, :] = gal
+        yield
+        g_o = head_halves(dot_nt(gal, attn[3]))
+        yield
+        dq, dk, dv = attend_back(
+            s["p"][seg], pair_queries(*g_o), pair_queries(s["q"][0, rows, :], s["q"][1, rows, :]),
+            pair_lanes(s["k"][rows, :]), pair_lanes(s["v"][rows, :]),
+        )
+        s["dq"][rows, :] = dq
+        s["dk"][rows, :] = dk
+        s["dv"][rows, :] = dv
+        yield
+        gh = dot_nt(dq, attn[0]) + dot_nt(dk, attn[1])
+        yield
+        gh = gh + dot_nt(dv, attn[2])
+        xhat = s["xh0"][rows, :].astype(f32)
+        s["gain"][0:1, :] += jnp.sum(gh * xhat, 0, keepdims=True)
+        s["gtok"][rows, :] = (ga + norm_back(gh, gain[0], xhat, s["rs0"][rows, :])).astype(bf16)
+        yield
+
+    for seg in reversed(range(NSEG)):
+        works = [backward(seg)]
+        if seg < NSEG - 1:
+            works.append(self_backward(seg + 1))
+        together(*works)
+    results((3,), results_start)
 
     cut = pl.ds(pl.multiple_of(core * BLOCK, BLOCK), BLOCK)
 
@@ -525,276 +589,150 @@
         for i, (left, right) in enumerate(names):
             put(base + i, dot_tn(s[left][:, cut], s[right][...]))
 
-    put_products(0, [("mlow", "dwq"), ("t", "dwk"), ("t", "dwv"), ("wo", "gup")])
-    for i in range(4):
-        put(4 + i, dot_tn(s["n2"][:, cut], s["gul"][:, i * D : (i + 1) * D]))
-    for i in range(4):
-        cut_i = pl.ds(pl.multiple_of(core * 4 * BLOCK + i * BLOCK, BLOCK), BLOCK)
-        put(8 + i, dot_tn(s["hid"][:, cut_i], s["gyl"][...]))
-    put_products(12, [("n1", "dcq"), ("mlow", "dck"), ("mlow", "dcv"), ("co", "gbl")])
-
-    def small_copies(axis):
+    def small_start(axis, value):
         here = place[axis]
-        return [
-            remote(
-                s["small"].at[axis, here], s["small"].at[axis, here], s["small_send"].at[axis, step - 1],
-                s["small_recv"].at[axis, step - 1], along(axis, (here + step) % 4),
-            )
-            for step in range(1, 4)
-        ]
-
-    def small_start(axis, value):
-        s["small"][axis, place[axis]] = value
-        for copy in small_copies(axis):
-            copy.start()
+        s["small"][axis, here] = value
+        for step in range(1, 4):
+            own = s["small"].at[axis, here]
+            remote(own, own, s["small_send"].at[axis], s["small_recv"].at[axis], along(axis, (here + step) % 4)).start()
+
+    def all_moved(ref, send_sem, recv_sem):
+        copy = remote(ref, ref, send_sem, recv_sem, sibling)
+        copy.wait_send()
+        copy.wait_recv()
 
     def small_finish(axis):
-        for copy in small_copies(axis):
-            copy.wait()
+        all_moved(s["small"].at[axis, pl.ds(0, 3)], s["small_send"].at[axis], s["small_recv"].at[axis])
         return (s["small"][axis, 0] + s["small"][axis, 1]) + (s["small"][axis, 2] + s["small"][axis, 3])
 
-    def part_steps(chunk, part):
+    def others(axis, i):
+        return [((i + step) % 4, step - 1, along(axis, (i + step) % 4)) for step in range(1, 4)]
+
+    def add(refs):
+        total = refs[0][...].astype(f32)
+        for ref in refs[1:]:
+            total += ref[...].astype(f32)
+        return total.astype(bf16)
+
+    def part_place(chunk, part):
         r = CHUNKS[chunk][part] * UNIT
         base = 64 * UNIT * (sum(sum(c) for c in CHUNKS[:chunk]) + sum(CHUNKS[chunk][:part]))
         axes = [(part + i) % 3 for i in range(3)]
-        i1, i2, i3 = (place[a] for a in axes)
+        return r, base, axes, [place[a] for a in axes]
+
+    def part_steps(chunk, part):
+        r, base, axes, (i1, i2, i3) = part_place(chunk, part)
         right, left = along(axes[0], (i1 + 1) % 4), along(axes[0], (i1 + 3) % 4)
-        sems = iter(range(40))
-        near, far, mid, last = (s[name][chunk][part] for name in ("near", "far", "mid", "last"))
-        dw = s["dw"]
-
-        def copy(src, dst, device):
-            i = next(sems)
-            return remote(src, dst, s["send"].at[chunk, part, i], s["recv"].at[chunk, part, i], device)
+        near, far, mid, quad, last = (s[name][chunk][part] for name in ("near", "far", "mid", "quad", "last"))
+        dw, mine = s["dw"], full_ref.at[core]
+
+        def copy(src, dst, device, i):
+            remote(src, dst, s["send"].at[chunk], s["recv"].at[chunk, part, i], device).start()
+
+        def arrived(ref, i):
+            remote(ref, ref, s["send"].at[chunk], s["recv"].at[chunk, part, i], sibling).wait_recv()
 
         def block(b, first=0, count=16):
             return rows_at(base + (b % 4) * 16 * r + first * r, count * r)
 
-        def add(refs):
-            total = refs[0][...].astype(f32)
-            for ref in refs[1:]:
-                total += ref[...].astype(f32)
-            return total.astype(bf16)
+        def pass_on(rows, device, i):
+            copy(mine.at[rows], mine.at[rows], device, i)
 
         half0, half1 = pl.ds(0, 8 * r), pl.ds(8 * r, 8 * r)
-        a = copy(dw.at[block(i1 + 2, 0, 8)], near.at[0], right)
-        b = copy(dw.at[block(i1 + 2, 8, 8)], near.at[1], left)
-        c1 = copy(dw.at[block(i1 + 1, 8, 8)], far.at[0, half1], right)
-        d0 = copy(dw.at[block(i1 + 3, 0, 8)], far.at[1, half0], left)
-        for one in (a, b, c1, d0):
-            one.start()
-        yield
-        a.wait()
+        copy(dw.at[block(i1 + 2, 0, 8)], near.at[0], right, 0)
+        copy(dw.at[block(i1 + 2, 8, 8)], near.at[1], left, 1)
+        copy(dw.at[block(i1 + 1, 8, 8)], far.at[0, half1], right, 2)
+        copy(dw.at[block(i1 + 3, 0, 8)], far.at[1, half0], left, 2)
+        yield
+        arrived(near.at[0], 0)
         near[0] = add([near.at[0], dw.at[block(i1 + 1, 0, 8)]])
-        c0 = copy(near.at[0], far.at[0, half0], right)
-        c0.start()
-        b.wait()
+        copy(near.at[0], far.at[0, half0], right, 2)
+        arrived(near.at[1], 1)
         near[1] = add([near.at[1], dw.at[block(i1 + 3, 8, 8)]])
-        d1 = copy(near.at[1], far.at[1, half1], left)
-        d1.start()
-        yield
-        for one in (c1, d0, c0, d1):
-            one.wait()
+        copy(near.at[1], far.at[1, half1], left, 2)
+        yield
+        arrived(far, 2)
         far[0] = add([far.at[0], far.at[1], dw.at[block(i1)]])
-        two = [
-            copy(far.at[0, rows_at((i2 + step) % 4 * 4 * r, 4 * r)], mid.at[step - 1], along(axes[1], (i2 + step) % 4))
-            for step in range(1, 4)
-        ]
-        for one in two:
-            one.start()
-        yield
-        for one in two:
-            one.wait()
-        mid[0] = add([mid.at[0], mid.at[1], mid.at[2], far.at[0, rows_at(i2 * 4 * r, 4 * r)]])
-        three = [
-            copy(mid.at[0, rows_at((i3 + step) % 4 * r, r)], last.at[step - 1], along(axes[2], (i3 + step) % 4))
-            for step in range(1, 4)
-        ]
-        for one in three:
-            one.start()
-        yield
-        for one in three:
-            one.wait()
-        mine = full_ref.at[core]
-        home = block(i1, i2 * 4 + i3, 1)
-        last[0] = add([last.at[0], last.at[1], last.at[2], mid.at[0, rows_at(i3 * r, r)]])
-        keep = pltpu.make_async_copy(last.at[0], mine.at[home], s["own"].at[chunk, part])
-        back = [copy(last.at[0], mine.at[home], along(axes[2], (i3 + step) % 4)) for step in range(1, 4)]
-        for one in [keep] + back:
-            one.start()
-        yield
-        for one in [keep] + back:
-            one.wait()
-        home = block(i1, i2 * 4, 4)
-        back = [copy(mine.at[home], mine.at[home], along(axes[1], (i2 + step) % 4)) for step in range(1, 4)]
-        for one in back:
-            one.start()
-        yield
-        for one in back:
-            one.wait()
-        home = block(i1)
-        to_right = copy(mine.at[home], mine.at[home], right)
-        to_left = copy(mine.at[home], mine.at[home], left)
-        over = [copy(mine.at[home], mine.at[home], sibling)]
-        for one in (to_right, to_left, over[0]):
-            one.start()
-        yield
-        to_right.wait()
-        from_left = block(i1 + 3)
-        on_right = copy(mine.at[block(i1 + 3, 0, 8)], mine.at[block(i1 + 3, 0, 8)], right)
-        on_right.start()
-        over.append(copy(mine.at[from_left], mine.at[from_left], sibling))
-        over[-1].start()
-        to_left.wait()
-        from_right = block(i1 + 1)
-        on_left = copy(mine.at[block(i1 + 1, 8, 8)], mine.at[block(i1 + 1, 8, 8)], left)
-        on_left.start()
-        over.append(copy(mine.at[from_right], mine.at[from_right], sibling))
-        over[-1].start()
-        yield
-        on_right.wait()
-        on_left.wait()
-        opposite = block(i1 + 2)
-        over.append(copy(mine.at[opposite], mine.at[opposite], sibling))
-        over[-1].start()
-        yield
-        for one in over:
-            one.wait()
-        yield
-
-    def short_part_steps(chunk, part):
-        r = CHUNKS[chunk][part] * UNIT
-        base = 64 * UNIT * (sum(sum(c) for c in CHUNKS[:chunk]) + sum(CHUNKS[chunk][:part]))
-        axes = [(part + i) % 3 for i in range(3)]
-        i1, i2, i3 = (place[a] for a in axes)
-        sems = iter(range(40))
-        far, mid, last = (s[name][chunk][part] for name in ("far", "mid", "last"))
-        dw, mine = s["dw"], full_ref.at[core]
-
-        def copy(src, dst, device):
-            i = next(sems)
-            return remote(src, dst, s["send"].at[chunk, part, i], s["recv"].at[chunk, part, i], device)
-
-        def block(first, count):
-            return rows_at(base + first * r, count * r)
-
-        def add(refs):
-            total = refs[0][...].astype(f32)
-            for ref in refs[1:]:
-                total += ref[...].astype(f32)
-            return total.astype(bf16)
-
-        def others(axis, i):
-            return [((i + step) % 4, step - 1, along(axis, (i + step) % 4)) for step in range(1, 4)]
-
-        def all_do(copies, do):
-            for one in copies:
-                getattr(one, do)()
-
-        one = [copy(dw.at[block(b * 16, 16)], far.at[slot], to) for b, slot, to in others(axes[0], i1)]
-        all_do(one, "start")
-        yield
-        all_do(one, "wait")
-        far[0] = add([far.at[0], far.at[1], far.at[2], dw.at[block(i1 * 16, 16)]])
-        two = [
-            copy(far.at[0, rows_at(b * 4 * r, 4 * r)], mid.at[slot], to) for b, slot, to in others(axes[1], i2)
-        ]
-        all_do(two, "start")
-        yield
-        all_do(two, "wait")
-        mid[0] = add([mid.at[0], mid.at[1], mid.at[2], far.at[0, rows_at(i2 * 4 * r, 4 * r)]])
-        three = [copy(mid.at[0, rows_at(b * r, r)], last.at[slot], to) for b, slot, to in others(axes[2], i3)]
-        all_do(three, "start")
-        yield
-        all_do(three, "wait")
-        last[0] = add([last.at[0], last.at[1], last.at[2], mid.at[0, rows_at(i3 * r, r)]])
-        home = block(i1 * 16 + i2 * 4 + i3, 1)
-        keep = pltpu.make_async_copy(last.at[0], mine.at[home], s["own"].at[chunk, part])
-        back = [copy(last.at[0], mine.at[home], to) for _, _, to in others(axes[2], i3)]
-        all_do([keep] + back, "start")
-        yield
-        all_do([keep] + back, "wait")
-        home = block(i1 * 16 + i2 * 4, 4)
-        back = [copy(mine.at[home], mine.at[home], to) for _, _, to in others(axes[1], i2)]
-        all_do(back, "start")
-        yield
-        all_do(back, "wait")
-        home = block(i1 * 16, 16)
-        back = [copy(mine.at[home], mine.at[home], to) for _, _, to in others(axes[0], i1)]
-        over = [copy(mine.at[home], mine.at[home], sibling)]
-        all_do(back + over, "start")
-        yield
-        all_do(back, "wait")
-        for b, _, _ in others(axes[0], i1):
-            over.append(copy(mine.at[block(b * 16, 16)], mine.at[block(b * 16, 16)], sibling))
-            over[-1].start()
-        yield
-        all_do(over, "wait")
+        for b, slot, to in others(axes[1], i2):
+            copy(far.at[0, rows_at(b * 4 * r, 4 * r)], mid.at[slot], to, 3)
+        yield
+        arrived(mid, 3)
+        quad[i3] = add([mid.at[0], mid.at[1], mid.at[2], far.at[0, rows_at(i2 * 4 * r, 4 * r)]])
+        for _, _, to in others(axes[2], i3):
+            copy(quad.at[i3], quad.at[i3], to, 4)
+        yield
+        arrived(quad.at[pl.ds(0, 3)], 4)
+        last[...] = add([quad.at[i] for i in range(4)])
+        home = rows_at(base + (i1 * 16 + i2 * 4) * r, 4 * r)
+        keep = pltpu.make_async_copy(last, mine.at[home], s["own"].at[chunk, part])
+        keep.start()
+        for _, _, to in others(axes[1], i2):
+            copy(last, mine.at[home], to, 5)
+        yield
+        keep.wait()
+        arrived(mine.at[rows_at(base, 12 * r)], 5)
+        pass_on(block(i1), right, 6)
+        pass_on(block(i1), left, 7)
+        pass_on(block(i1), sibling, 9)
+        yield
+        arrived(mine.at[block(i1 + 3)], 6)
+        pass_on(block(i1 + 3, 0, 8), right, 8)
+        pass_on(block(i1 + 3), sibling, 9)
+        arrived(mine.at[block(i1 + 1)], 7)
+        pass_on(block(i1 + 1, 8, 8), left, 8)
+        pass_on(block(i1 + 1), sibling, 9)
+        yield
+        arrived(mine.at[block(i1 + 2)], 8)
+        pass_on(block(i1 + 2), sibling, 9)
+        yield
+        arrived(full_ref.at[1 - core, rows_at(base, 64 * r)], 9)
+        if part == 2:
+            sent = full_ref.at[core, rows_at(0, 196 * UNIT * sum(CHUNKS[chunk]))]
+            remote(sent, sent, s["send"].at[chunk], s["recv"].at[chunk, part, 0], sibling).wait_send()
         yield
 
     def chunk_steps(chunk):
-        parts = [(part_steps if chunk == 0 else short_part_steps)(chunk, part) for part in range(3)]
-        for _ in range(10 if chunk == 0 else 8):
+        parts = [part_steps(chunk, part) for part in range(3)]
+        while True:
             for part in parts:
                 next(part)
             yield
 
-    first, second = chunk_steps(0), chunk_steps(1)
-    next(first)
-
-    gn1 = dot_nt(s["dcq"][...], attn[4])
-    xhat = s["xh1"][...].astype(f32)
-    s["gain"][1:2, :] = jnp.sum(gn1 * xhat, 0, keepdims=True)
-    ga = s["res"][...] + norm_back(gn1, gain[1], xhat, s["rs1"][...])
-    s["res"][...] = ga
-    gal = ga.astype(bf16)
-    s["gal"][...] = gal
-    g0, g1 = head_halves(dot_nt(gal, attn[3]))
-    s["cq"][0] = g0
-    s["cq"][1] = g1
-
-    def self_backward(seg, carry):
-        rows = pl.ds(pl.multiple_of(seg * SEG, SEG), SEG)
-        s["dq"][rows, :], s["t"][rows, :], s["gyl"][rows, :] = attend_back(
-            s["p"][seg], pair_queries(s["cq"][0, rows, :], s["cq"][1, rows, :]),
-            pair_queries(s["q"][0, rows, :], s["q"][1, rows, :]),
-            pair_lanes(s["k"][rows, :]), pair_lanes(s["v"][rows, :]),
-        )
-        return carry
-
-    lax.fori_loop(0, NSEG - 1, self_backward, 0)
-    next(first)
-    lax.fori_loop(NSEG - 1, NSEG, self_backward, 0)
-    gh = dot_nt(s["dq"][...], attn[0]) + dot_nt(s["t"][...], attn[1]) + dot_nt(s["gyl"][...], attn[2])
-    xhat = s["xh0"][...].astype(f32)
-    s["gain"][0:1, :] = jnp.sum(gh * xhat, 0, keepdims=True)
-    s["gtok"][...] = (s["res"][...] + norm_back(gh, gain[0], xhat, s["rs0"][...])).astype(bf16)
+    chunks = [chunk_steps(chunk) for chunk in range(len(CHUNKS))]
+
+    def go(*order):
+        for chunk in order:
+            next(chunks[chunk])
+
+    for i in range(4):
+        put(i, dot_tn(s["n2"][:, cut], s["gul"][:, i * D : (i + 1) * D]))
+    for i in range(4):
+        if i == 2:
+            go(0)
+        cut_i = pl.ds(pl.multiple_of(core * 4 * BLOCK + i * BLOCK, BLOCK), BLOCK)
+        put(4 + i, dot_tn(s["hid"][:, cut_i], s["gyl"][...]))
+    put_products(8, [("mlow", "dwq"), ("t", "dwk"), ("t", "dwv"), ("wo", "gup")])
+    go(1)
+    put_products(12, [("n1", "dcq"), ("mlow", "dck"), ("mlow", "dcv"), ("co", "gbl")])
+    last_segment = self_backward(0)
+    for _ in range(3):
+        next(last_segment)
+    put_products(16, [("o", "gal")])
+    together(last_segment)
     s["gain"][6:7, 0:SLOTS] = jnp.sum(jnp.where(diagonal, s["bias"][:, 0:SLOTS], 0.0), 0, keepdims=True)
-    put_products(16, [("h", "dq"), ("h", "t"), ("h", "gyl"), ("o", "gal")])
-
-    next(second)
+    go(2, 0)
     small_start(0, s["gain"][...])
-    results((2, 3), results_start)
-    next(first)
-    next(second)
+    results((2,), results_start)
+    put_products(17, [("h", "dq"), ("h", "dk"), ("h", "dv")])
+    go(1, 3, 2, 0)
     total = small_finish(0)
     small_start(1, total)
-    next(first)
-    next(second)
+    go(3, 1, 2, 0)
     total = small_finish(1)
     small_start(2, total)
-    next(first)
-    next(second)
+    go(3, 1, 2, 3, 0, 1)
     small_out[...] = small_finish(2)
-    next(first)
-    next(second)
-    next(first)
-    next(second)
-    next(first)
-    next(second)
-    next(first)
-    next(first)
-    next(second)
+    go(2, 3, 0, 1, 3, 2, 0, 3, 1, 2, 3, 0, 1, 3, 2, 0, 1, 2)
     results((0, 1, 2, 3), results_finish)
 
 
@@ -814,7 +752,7 @@
         in_specs=[hbm] * 4 + [vmem] + [hbm] * 3 + [vmem] * 3,
         out_specs=[hbm] * 5 + [vmem],
         scratch_shapes=[scratch_buffers()],
-        compiler_params=pltpu.CompilerParams(collective_id=1, has_side_effects=True, vmem_limit_bytes=62 << 20),
+        compiler_params=pltpu.CompilerParams(collective_id=1, has_side_effects=True, vmem_limit_bytes=63 << 20),
         name="layer_and_sums",
     )(tok, ocot, mcot, mem, lens, attn, win, wout, gains, fw, fb)
 
@@ -831,12 +769,10 @@
 
     def target(i, half):
         if i < 4:
-            return attn_ref.at[8 + i, pl.ds(half * BLOCK, BLOCK), :]
+            return in_ref.at[pl.ds(half * BLOCK, BLOCK), pl.ds(i * D, D)]
         if i < 8:
-            return in_ref.at[pl.ds(half * BLOCK, BLOCK), pl.ds((i - 4) * D, D)]
-        if i < 12:
-            return out_ref.at[pl.ds(half * 4 * BLOCK + (i - 8) * BLOCK, BLOCK), :]
-        return attn_ref.at[i - 8 if i < 16 else i - 16, pl.ds(half * BLOCK, BLOCK), :]
+            return out_ref.at[pl.ds(half * 4 * BLOCK + (i - 4) * BLOCK, BLOCK), :]
+        return attn_ref.at[i if i < 12 else i - 8 if i < 16 else 3 if i == 16 else i - 17, pl.ds(half * BLOCK, BLOCK), :]
 
     def store(i, half):
         return pltpu.make_async_copy(wide_s.at[i, half], target(i, half), store_sem.at[i, half])

time: 128 us -> 117 us (0.914)
  Pallas kernels: 127 us -> 116 us
    pallas_call x1, Pallas kernels: 115 us -> 103 us  [run_fused(): pl.pallas_call(fused_kernel, out_shape=(jax.ShapeDtypeStruct((2, FLAT, LA...]
where the time goes in v5:
time: 117 us
  Pallas kernels  116 us (99%)
    pallas_call x1, Pallas kernels, run_fused(): pl.pallas_call(fused_kernel, out_shape=(jax.ShapeDtypeStruct((2, FLAT, LA...  103 us
    pallas_call x1, Pallas kernels, run_widen(): pl.pallas_call(widen_kernel, out_shape=(jax.ShapeDtypeStruct((12, D, D),...  12.8 us

profile of v5, /device:TPU:1, one launch (start us, length us, event | category | flops | bytes accessed | tf_op | source)
XLA Modules:
  0.0 116.6 jit_solution(7932845666394616196)
XLA Ops:
  0.6 102.9 %layer_and_sums.1 = (bf16[2,20480,128]{2,1,0:T(8,128)(2,1)}, bf16[2,128,512]{2,1,0:T(8,128)(2,1)}, bf16[2,64,512]{2,1,0:T(8,128)(2,1)}, bf16[2,128,512]{2,1,0:T(...) custom-call(bf16[2,128,512]{2,1,0:T(8,128)(2,1)} %tok_ref.1, bf16[2,128,512]{2,1,0:T(8,128)(2,1)} %ocot_ref.1, ...), custom_call_target="tpu_custom_call" | custom-call | tf_op jit(solution)/shard_map/layer_and_sums/pallas_call | solution.py:742
  103.6 12.8 %widen_gradients.1 = (f32[12,512,512]{2,1,0:T(8,128)}, f32[512,2048]{1,0:T(8,128)}, f32[2048,512]{1,0:T(8,128)}, bf16[2,128,512]{2,1,0:T(8,128)(2,1)}, bf16[2,64...) custom-call(bf16[2,20,4,256,128]{4,3,2,1,0:T(8,128)(2,1)} %bitcast.7, ...), custom_call_target="tpu_custom_call" | custom-call | tf_op jit(solution)/shard_map/widen_gradients/pallas_call | solution.py:804

commit v6 on v5

--- a/solution.py
+++ b/solution.py
@@ -18,7 +18,7 @@
 MROWS = NSEG * SLOTS
 PAIRS = 4
 PAIR = 128
-FCHUNK = 512
+FCHUNK = 2048
 BLOCK = 256
 NBLOCKS = 20
 LANES = 128
@@ -57,8 +57,11 @@
 
 
 def head_halves(values):
-    low_half = lax.broadcasted_iota(jnp.int32, values.shape, 1) % PAIR < PAIR // 2
-    return jnp.where(low_half, values, 0.0).astype(bf16), jnp.where(low_half, 0.0, values).astype(bf16)
+    low_half = lax.broadcasted_iota(jnp.int32, (16, values.shape[1]), 1) % PAIR < PAIR // 2
+    first = jnp.where(low_half, 1.0, 0.0).astype(bf16)[0:1, :]
+    second = jnp.where(low_half, 0.0, 1.0).astype(bf16)[0:1, :]
+    values = values.astype(bf16)
+    return values * first, values * second
 
 
 def join_halves(stacked):
@@ -101,8 +104,10 @@
     square = u * u
     tanh = jnp.tanh(0.7978845608028654 * u * (1.0 + 0.044715 * square))
     half = 0.5 + 0.5 * tanh
-    slope = half + u * half * (1.0 - tanh) * (0.7978845608028654 + 0.1070322243 * square)
-    return u * half, slope
+    hidden = u * half
+    rest, square = (1.0 - tanh).astype(bf16), square.astype(bf16)
+    slope = half.astype(bf16) + hidden.astype(bf16) * rest * (bf16(0.7978845608028654) + bf16(0.1070322243) * square)
+    return hidden, slope
 
 
 CHUNKS = ((2, 2, 2), (2, 2, 2), (1, 2, 2), (1, 1, 1))
@@ -135,11 +140,11 @@
         xh0=rows(), rs0=rows(f32, 1),
         res=rows(f32), n1=rows(), xh1=rows(), rs1=rows(f32, 1), cq=two(ROWS), ck=slots(), cv=slots(),
         cp=pltpu.VMEM((NSEG, SLOTS, HEADS * SEG), bf16), co=rows(),
-        n2=rows(), xh2=rows(), rs2=rows(f32, 1), hid=rows(bf16, FF), gd=rows(bf16, FF),
+        n2=rows(), xh2=rows(), rs2=rows(f32, 1), hid=rows(bf16, FF), gul=rows(bf16, FF),
         t=rows(), xh3=rows(), rs3=rows(f32, 1),
         xh4=slots(f32), rs4=slots(f32, 1), mlow=slots(), gate=slots(f32, 1), upd=slots(f32),
         wq=two(MROWS), wk=rows(), wv=rows(), wp=pltpu.VMEM((NSEG, SEG, HEADS * SLOTS), bf16), wo=slots(),
-        gup=slots(), dwq=slots(), dwk=rows(), dwv=rows(), gyl=rows(), gul=rows(bf16, FF), gbl=rows(),
+        gup=slots(), dwq=slots(), dwk=rows(), dwv=rows(), gyl=rows(), gbl=rows(),
         dcq=rows(), dck=slots(), dcv=slots(),
         gal=rows(), dq=rows(), dk=rows(), dv=rows(),
         gain=pltpu.VMEM((8, D), f32), bias=pltpu.VMEM((SLOTS, LANES), f32),
@@ -303,10 +308,6 @@
         def _():
             remote(src, dst, s["first_send"].at[i], s["first_recv"].at[i], sibling).wait_recv()
 
-    gather_finish(0, gather_forward(0))
-    gather_sends(1, True)
-    gather_sends(2, True)
-
     attn, win, wout = s["attn"], s["win"], s["wout"]
     attn_t = {index: s["attn_t"].at[i] for i, index in enumerate(TURNED)}
     win_t, wout_t = s["win_t"], s["wout_t"]
@@ -325,10 +326,10 @@
         return sum((end <= pos).astype(jnp.int32) for end in ends)
 
     def row_cut(seg):
-        return slice(seg * SEG, (seg + 1) * SEG)
+        return pl.ds(pl.multiple_of(seg * SEG, SEG), SEG)
 
     def slot_cut(seg):
-        return slice(seg * SLOTS, (seg + 1) * SLOTS)
+        return pl.ds(pl.multiple_of(seg * SLOTS, SLOTS), SLOTS)
 
     def together(*works):
         works = list(works)
@@ -402,7 +403,7 @@
             hid, slope = gelu_both(dot(n2, win[:, c : c + FCHUNK]))
             hid = hid.astype(bf16)
             s["hid"][rows, c : c + FCHUNK] = hid
-            s["gd"][rows, c : c + FCHUNK] = slope.astype(bf16)
+            s["gul"][rows, c : c + FCHUNK] = slope
             res = res + dot(hid, wout[c : c + FCHUNK, :])
             yield
         s["act"][rows, :] = res.astype(bf16)
@@ -430,19 +431,26 @@
         yield
         update = dot(wo, attn[11])
         s["upd"][slots, :] = mem - update
-        s["mout"][slots, :] = (update + gate * (mem - update)).astype(bf16)
-        yield
-
+        fresh = (update + gate * (mem - update)).astype(bf16)
+        s["mout"][slots, :] = fresh
+        s["mem"][...] = fresh
+        yield
+
+    first_step = forward(0, s["mem"][...].astype(f32))
+    next(first_step)
+    gather_finish(0, gather_forward(0))
+    gather_sends(1, True)
+    gather_sends(2, True)
     together(self_forward(0))
-    passed = []
-    for seg in range(NSEG):
-        mem = s["mem"][...] if seg == 0 else s["mout"][slot_cut(seg - 1), :]
-        works = [forward(seg, mem.astype(f32))]
-        if seg < NSEG - 1:
-            works.append(self_forward(seg + 1))
-        together(*works)
-        if seg in (1, 2):
-            passed.append(gather_forward(seg))
+    together(first_step, self_forward(1))
+
+    def forward_both(seg, carry):
+        together(forward(seg, s["mem"][...].astype(f32)), self_forward(seg + 1))
+        return carry
+
+    lax.fori_loop(1, NSEG - 1, forward_both, 0)
+    passed = [gather_forward(1), gather_forward(2)]
+    together(forward(NSEG - 1, s["mem"][...].astype(f32)))
 
     def results(indices, do):
         for k in range(2):
@@ -486,9 +494,7 @@
 
     def backward(seg):
         rows, slots = row_cut(seg), slot_cut(seg)
-        gz = s["mcot"][slots, :].astype(f32)
-        if seg < NSEG - 1:
-            gz = (gz + s["gmem"][slot_cut(seg + 1), :].astype(f32)).astype(bf16).astype(f32)
+        gz = (s["mcot"][slots, :].astype(f32) + s["mem"][...].astype(f32)).astype(bf16).astype(f32)
         gate = s["gate"][slots, :]
         gup = ((1.0 - gate) * gz).astype(bf16)
         s["gup"][slots, :] = gup
@@ -512,7 +518,7 @@
         gn2 = jnp.zeros((SEG, D), f32)
         for c in range(0, FF, FCHUNK):
             ghid = dot(gyl, wout_t[:, c : c + FCHUNK])
-            gul = (ghid * s["gd"][rows, c : c + FCHUNK].astype(f32)).astype(bf16)
+            gul = (ghid * s["gul"][rows, c : c + FCHUNK].astype(f32)).astype(bf16)
             s["gul"][rows, c : c + FCHUNK] = gul
             gn2 = gn2 + dot(gul, win_t[c : c + FCHUNK, :])
             yield
@@ -540,43 +546,21 @@
         yield
         gm = gm + dot(dck, attn_t[5][...]) + dot(dcv, attn_t[6][...])
         s["gain"][4:5, :] += jnp.sum(gm * xh4, 0, keepdims=True)
-        s["gmem"][slots, :] = (gate * gz + norm_back(gm, gain[4], xh4, s["rs4"][slots, :])).astype(bf16)
-        yield
-
-    def self_backward(seg):
-        rows = row_cut(seg)
-        gn1 = dot_nt(s["dcq"][rows, :], attn[4])
-        yield
-        xhat = s["xh1"][rows, :].astype(f32)
-        s["gain"][1:2, :] += jnp.sum(gn1 * xhat, 0, keepdims=True)
-        ga = s["res"][rows, :] + norm_back(gn1, gain[1], xhat, s["rs1"][rows, :])
-        gal = ga.astype(bf16)
-        s["gal"][rows, :] = gal
-        yield
-        g_o = head_halves(dot_nt(gal, attn[3]))
-        yield
-        dq, dk, dv = attend_back(
-            s["p"][seg], pair_queries(*g_o), pair_queries(s["q"][0, rows, :], s["q"][1, rows, :]),
-            pair_lanes(s["k"][rows, :]), pair_lanes(s["v"][rows, :]),
-        )
-        s["dq"][rows, :] = dq
-        s["dk"][rows, :] = dk
-        s["dv"][rows, :] = dv
-        yield
-        gh = dot_nt(dq, attn[0]) + dot_nt(dk, attn[1])
-        yield
-        gh = gh + dot_nt(dv, attn[2])
-        xhat = s["xh0"][rows, :].astype(f32)
-        s["gain"][0:1, :] += jnp.sum(gh * xhat, 0, keepdims=True)
-        s["gtok"][rows, :] = (ga + norm_back(gh, gain[0], xhat, s["rs0"][rows, :])).astype(bf16)
-        yield
-
-    for seg in reversed(range(NSEG)):
-        works = [backward(seg)]
-        if seg < NSEG - 1:
-            works.append(self_backward(seg + 1))
-        together(*works)
-    results((3,), results_start)
+        gmem = (gate * gz + norm_back(gm, gain[4], xh4, s["rs4"][slots, :])).astype(bf16)
+        s["gmem"][slots, :] = gmem
+        s["mem"][...] = gmem
+        yield
+
+    s["mem"][...] = jnp.zeros_like(s["mem"])
+
+    def backward_one(step, carry):
+        together(backward(NSEG - 1 - step))
+        return carry
+
+    lax.fori_loop(0, NSEG - 1, backward_one, 0)
+    last_step = backward(0)
+    for _ in range(3 + FF // FCHUNK):
+        next(last_step)
 
     cut = pl.ds(pl.multiple_of(core * BLOCK, BLOCK), BLOCK)
 
@@ -713,26 +697,52 @@
         put(4 + i, dot_tn(s["hid"][:, cut_i], s["gyl"][...]))
     put_products(8, [("mlow", "dwq"), ("t", "dwk"), ("t", "dwv"), ("wo", "gup")])
     go(1)
+    together(last_step)
+    results((3,), results_start)
     put_products(12, [("n1", "dcq"), ("mlow", "dck"), ("mlow", "dcv"), ("co", "gbl")])
-    last_segment = self_backward(0)
-    for _ in range(3):
-        next(last_segment)
+
+    gn1 = dot_nt(s["dcq"][...], attn[4])
+    xhat = s["xh1"][...].astype(f32)
+    s["gain"][1:2, :] = jnp.sum(gn1 * xhat, 0, keepdims=True)
+    ga = s["res"][...] + norm_back(gn1, gain[1], xhat, s["rs1"][...])
+    s["res"][...] = ga
+    gal = ga.astype(bf16)
+    s["gal"][...] = gal
+    s["cq"][0], s["cq"][1] = head_halves(dot_nt(gal, attn[3]))
     put_products(16, [("o", "gal")])
-    together(last_segment)
+    go(2)
+
+    def self_backward(seg):
+        rows = row_cut(seg)
+        s["dq"][rows, :], s["dk"][rows, :], s["dv"][rows, :] = attend_back(
+            s["p"][seg], pair_queries(s["cq"][0, rows, :], s["cq"][1, rows, :]),
+            pair_queries(s["q"][0, rows, :], s["q"][1, rows, :]),
+            pair_lanes(s["k"][rows, :]), pair_lanes(s["v"][rows, :]),
+        )
+
+    self_backward(0)
+    self_backward(1)
+    self_backward(2)
+    go(0)
+    self_backward(3)
+    gh = dot_nt(s["dq"][...], attn[0]) + dot_nt(s["dk"][...], attn[1]) + dot_nt(s["dv"][...], attn[2])
+    go(1)
+    xhat = s["xh0"][...].astype(f32)
+    s["gain"][0:1, :] = jnp.sum(gh * xhat, 0, keepdims=True)
+    s["gtok"][...] = (s["res"][...] + norm_back(gh, gain[0], xhat, s["rs0"][...])).astype(bf16)
     s["gain"][6:7, 0:SLOTS] = jnp.sum(jnp.where(diagonal, s["bias"][:, 0:SLOTS], 0.0), 0, keepdims=True)
-    go(2, 0)
     small_start(0, s["gain"][...])
     results((2,), results_start)
     put_products(17, [("h", "dq"), ("h", "dk"), ("h", "dv")])
-    go(1, 3, 2, 0)
+    go(3, 2, 0)
     total = small_finish(0)
     small_start(1, total)
-    go(3, 1, 2, 0)
+    go(1, 3, 2, 0)
     total = small_finish(1)
     small_start(2, total)
-    go(3, 1, 2, 3, 0, 1)
+    go(3, 1, 2, 0, 3)
     small_out[...] = small_finish(2)
-    go(2, 3, 0, 1, 3, 2, 0, 3, 1, 2, 3, 0, 1, 3, 2, 0, 1, 2)
+    go(1, 2, 3, 0, 1, 2, 3, 0, 3, 1, 2, 3, 0, 1, 3, 2, 0, 1, 2)
     results((0, 1, 2, 3), results_finish)
 
 
@@ -775,7 +785,7 @@
         return attn_ref.at[i if i < 12 else i - 8 if i < 16 else 3 if i == 16 else i - 17, pl.ds(half * BLOCK, BLOCK), :]
 
     def store(i, half):
-        return pltpu.make_async_copy(wide_s.at[i, half], target(i, half), store_sem.at[i, half])
+        return pltpu.make_async_copy(wide_s.at[i, half], target(i, half), store_sem)
 
     for i in range(NBLOCKS):
         for copy in load(i):
@@ -793,9 +803,7 @@
             for j in range(LANE_CUTS):
                 wide_s[i, half, :, j * LANES : (j + 1) * LANES] = full_s[i, half, j].astype(f32)
             store(i, half).start()
-    for i in range(NBLOCKS):
-        for half in range(2):
-            store(i, half).wait()
+    pltpu.make_async_copy(wide_s, wide_s, store_sem).wait()
 
 
 def run_widen(full, *others):
@@ -821,7 +829,7 @@
             pltpu.VMEM((NBLOCKS, 2, LANE_CUTS, BLOCK, LANES), bf16),
             pltpu.VMEM((NBLOCKS, 2, BLOCK, D), f32),
             pltpu.SemaphoreType.DMA((NBLOCKS, 2)),
-            pltpu.SemaphoreType.DMA((NBLOCKS, 2)),
+            pltpu.SemaphoreType.DMA,
         ],
         compiler_params=pltpu.CompilerParams(vmem_limit_bytes=60 << 20),
         name="widen_gradients",

time: 117 us -> 111 us (0.949)
  Pallas kernels: 116 us -> 110 us
    pallas_call x1, Pallas kernels: 103 us -> 97.1 us  [run_fused(): pl.pallas_call(fused_kernel, out_shape=(jax.ShapeDtypeStruct((2, FLAT, LA...]
where the time goes in v6:
time: 111 us; the launch traced here: 110 us
  Pallas kernels  110 us (99%)
    pallas_call x1, Pallas kernels, run_fused(): pl.pallas_call(fused_kernel, out_shape=(jax.ShapeDtypeStruct((2, FLAT, LA...  97.1 us
    pallas_call x1, Pallas kernels, run_widen(): pl.pallas_call(widen_kernel, out_shape=(jax.ShapeDtypeStruct((12, D, D),...  12.5 us

profile of v6, /device:TPU:1, one launch (start us, length us, event | category | flops | bytes accessed | tf_op | source)
XLA Modules:
  0.0 110.4 jit_solution(10157334457954938561)
XLA Ops:
  0.6 97.1 %layer_and_sums.1 = (bf16[2,20480,128]{2,1,0:T(8,128)(2,1)}, bf16[2,128,512]{2,1,0:T(8,128)(2,1)}, bf16[2,64,512]{2,1,0:T(8,128)(2,1)}, bf16[2,128,512]{2,1,0:T(...) custom-call(bf16[2,128,512]{2,1,0:T(8,128)(2,1)} %tok_ref.1, bf16[2,128,512]{2,1,0:T(8,128)(2,1)} %ocot_ref.1, ...), custom_call_target="tpu_custom_call" | custom-call | tf_op jit(solution)/shard_map/layer_and_sums/pallas_call | solution.py:752
  97.8 12.5 %widen_gradients.1 = (f32[12,512,512]{2,1,0:T(8,128)}, f32[512,2048]{1,0:T(8,128)}, f32[2048,512]{1,0:T(8,128)}, bf16[2,128,512]{2,1,0:T(8,128)(2,1)}, bf16[2,64...) custom-call(bf16[2,20,4,256,128]{4,3,2,1,0:T(8,128)(2,1)} %bitcast.7, ...), custom_call_target="tpu_custom_call" | custom-call | tf_op jit(solution)/shard_map/widen_gradients/pallas_call | solution.py:812

commit v7 on v6

--- a/solution.py
+++ b/solution.py
@@ -113,7 +113,7 @@
 CHUNKS = ((2, 2, 2), (2, 2, 2), (1, 2, 2), (1, 1, 1))
 UNIT = 16
 
-TURNED = (5, 6, 7, 8, 9, 10, 11)
+TURNED = (7, 11, 8, 5, 6, 9, 10)
 
 
 def scratch_buffers():
@@ -153,8 +153,10 @@
         mid=parts(lambda r: (3, 4 * r, LANES)), quad=parts(lambda r: (4, 4 * r, LANES)), last=parts(lambda r: (4 * r, LANES)),
         small=pltpu.VMEM((3, 5, 8, D), f32),
         in_send=dma((2, 2, 3)), in_recv=dma((4, 3)), first_send=dma((2,)), first_recv=dma((2,)),
-        pass_send=dma((3, 3)), pass_recv=dma((3, 3)), in_local=dma((8,)), load=dma((4,)),
-        send=dma((len(CHUNKS),)), recv=dma((len(CHUNKS), 3, 10)), own=dma((len(CHUNKS), 3)),
+        pass_send=dma((3,)), pass_recv=dma((3,)), in_local=dma((5,)), load=dma((8,)),
+        gains=pltpu.VMEM((5, D), f32), fw=pltpu.VMEM((1, D), f32), fb=pltpu.VMEM((1, SLOTS), f32),
+        lens_in=pltpu.VMEM((2, NDOC), jnp.int32),
+        send=dma((len(CHUNKS),)), recv=dma((len(CHUNKS), 3, 7)), over=dma((len(CHUNKS),)), own=dma((len(CHUNKS), 3)),
         out_send=dma((2, 4)), out_recv=dma((2, 4)), out_local=dma((4,)),
         small_send=dma((3,)), small_recv=dma((3,)),
     )
@@ -204,6 +206,12 @@
         pltpu.make_async_copy(win_ref, s["win"], s["load"].at[2]),
         pltpu.make_async_copy(wout_ref, s["wout"], s["load"].at[3]),
     ]
+    small_loads = [
+        pltpu.make_async_copy(src, s[name], s["load"].at[4 + i])
+        for i, (src, name) in enumerate([(len_ref, "lens_in"), (gains_ref, "gains"), (fw_ref, "fw"), (fb_ref, "fb")])
+    ]
+    for load in small_loads:
+        load.start()
     for i in (1, 2, 3, 0):
         loads[i].start()
 
@@ -220,8 +228,9 @@
         def _():
             signal(barrier, device_at(2 * core + k, y, z, owner))
 
+    small_loads[0].wait()
     s["lens_own"][...] = jnp.zeros_like(s["lens_own"])
-    s["lens_own"][0:2, 0:NDOC] = len_ref[...]
+    s["lens_own"][0:2, 0:NDOC] = s["lens_in"][...]
     pl.semaphore_wait(barrier, 16 - 3 * mine_here.astype(jnp.int32))
 
     arrays = [(tok_ref, s["tok"], SEG), (ocot_ref, s["ocot"], SEG), (mcot_ref, s["mcot"], SLOTS)]
@@ -244,39 +253,46 @@
             @pl.when(chip == x)
             def _():
                 target = dst.at[rows_at(x * count, count)]
-                local = pltpu.make_async_copy(src.at[st], target, s["in_local"].at[i])
                 copy = remote(src.at[st], target, s["in_send"].at[st, 0, i], s["in_recv"].at[x, i], sibling)
                 if start:
-                    local.start()
+                    pltpu.make_async_copy(src.at[st], target, s["in_local"].at[i]).start()
                     copy.start()
                 else:
-                    local.wait()
                     copy.wait_send()
+
+    def gather_own(i):
+        src, dst, count = arrays[i]
+        whole = dst.at[rows_at(x * count, count)]
+
+        @pl.when(mine_here)
+        def _():
+            pltpu.make_async_copy(src.at[stream], whole, s["in_local"].at[i]).wait()
+
+        @pl.when(jnp.logical_not(mine_here))
+        def _():
+            remote(whole, whole, s["in_send"].at[0, 0, i], s["in_recv"].at[x, i], sibling).wait_recv()
+
+    def all_moved(ref, send_sem, recv_sem):
+        copy = remote(ref, ref, send_sem, recv_sem, sibling)
+        copy.wait_send()
+        copy.wait_recv()
 
     def gather_forward(i):
         src, dst, count = arrays[i]
         half = count // 2
-        copies = []
         for step in (1, 3, 2):
             seg = (x + step) % 4
             part = dst.at[rows_at(seg * count + core * half, half)]
             remote(
                 part, part, s["in_send"].at[0, 0, i], s["in_recv"].at[seg, i], device_at(seg, y, z, owner)
             ).wait_recv()
-            copies.append(remote(part, part, s["pass_send"].at[step - 1, i], s["pass_recv"].at[step - 1, i], sibling))
-            copies[-1].start()
-        return copies
-
-    def gather_finish(i, copies):
+            remote(part, part, s["pass_send"].at[i], s["pass_recv"].at[i], sibling).start()
+
+    def gather_finish(i):
         src, dst, count = arrays[i]
         gather_sends(i, False)
-        for copy in copies:
-            copy.wait()
-
-        @pl.when(jnp.logical_not(mine_here))
-        def _():
-            whole = dst.at[rows_at(x * count, count)]
-            remote(whole, whole, s["in_send"].at[0, 0, i], s["in_recv"].at[x, i], sibling).wait_recv()
+        three_halves = dst.at[pl.ds(0, 3 * count // 2)]
+        all_moved(three_halves, s["pass_send"].at[i], s["pass_recv"].at[i])
 
     gather_sends(0, True)
 
@@ -288,12 +304,14 @@
             remote(src, dst, s["first_send"].at[i], s["first_recv"].at[i], sibling).start()
             pltpu.make_async_copy(src, dst, s["in_local"].at[3 + i]).start()
 
-    for load in loads[1:]:
-        load.wait()
+    loads[1].wait()
     for i, index in enumerate(TURNED):
         s["attn_t"][i] = jnp.transpose(s["attn"][index])
+    loads[2].wait()
     for c in range(0, FF, D):
         s["win_t"][c : c + D, :] = jnp.transpose(s["win"][:, c : c + D])
+    loads[3].wait()
+    for c in range(0, FF, D):
         s["wout_t"][:, c : c + D] = jnp.transpose(s["wout"][c : c + D, :])
     loads[0].wait()
 
@@ -311,11 +329,13 @@
     attn, win, wout = s["attn"], s["win"], s["wout"]
     attn_t = {index: s["attn_t"].at[i] for i, index in enumerate(TURNED)}
     win_t, wout_t = s["win_t"], s["wout_t"]
-    gain = [gains_ref[i : i + 1, :] for i in range(5)]
-    forget_w = fw_ref[...]
+    for load in small_loads[1:]:
+        load.wait()
+    gain = [s["gains"][i : i + 1, :] for i in range(5)]
+    forget_w = s["fw"][...]
     square = (SLOTS, SLOTS)
     diagonal = lax.broadcasted_iota(jnp.int32, square, 0) == lax.broadcasted_iota(jnp.int32, square, 1)
-    forget_bias = jnp.sum(jnp.where(diagonal, jnp.broadcast_to(fb_ref[...], square), 0.0), -1, keepdims=True)
+    forget_bias = jnp.sum(jnp.where(diagonal, jnp.broadcast_to(s["fb"][...], square), 0.0), -1, keepdims=True)
 
     ends = []
     for j in range(NDOC):
@@ -438,18 +458,19 @@
 
     first_step = forward(0, s["mem"][...].astype(f32))
     next(first_step)
-    gather_finish(0, gather_forward(0))
+    gather_forward(0)
+    gather_own(0)
+    together(self_forward(x))
+    gather_finish(0)
     gather_sends(1, True)
     gather_sends(2, True)
-    together(self_forward(0))
-    together(first_step, self_forward(1))
-
-    def forward_both(seg, carry):
-        together(forward(seg, s["mem"][...].astype(f32)), self_forward(seg + 1))
-        return carry
-
-    lax.fori_loop(1, NSEG - 1, forward_both, 0)
-    passed = [gather_forward(1), gather_forward(2)]
+    rest = [step + (x <= step).astype(jnp.int32) for step in range(NSEG - 1)]
+    together(self_forward(rest[0]))
+    together(first_step, self_forward(rest[1]))
+    together(forward(1, s["mem"][...].astype(f32)), self_forward(rest[2]))
+    together(forward(2, s["mem"][...].astype(f32)))
+    gather_forward(1)
+    gather_forward(2)
     together(forward(NSEG - 1, s["mem"][...].astype(f32)))
 
     def results(indices, do):
@@ -487,7 +508,8 @@
 
     results((0, 1), results_start)
     for i in (1, 2):
-        gather_finish(i, passed[i - 1])
+        gather_own(i)
+        gather_finish(i)
 
     s["gain"][...] = jnp.zeros_like(s["gain"])
     s["bias"][...] = jnp.zeros_like(s["bias"])
@@ -508,7 +530,7 @@
         s["dwk"][rows, :] = dwk
         s["dwv"][rows, :] = dwv
         yield
-        gt = dot(dwk, attn_t[9][...]) + dot(dwv, attn_t[10][...])
+        gt = dot(jnp.concatenate([dwk, dwv], 1), s["attn_t"][5:7].reshape(2 * D, D))
         xhat = s["xh3"][rows, :].astype(f32)
         s["gain"][3:4, :] += jnp.sum(gt * xhat, 0, keepdims=True)
         gy = s["ocot"][rows, :].astype(f32) + norm_back(gt, gain[3], xhat, s["rs3"][rows, :])
@@ -534,7 +556,7 @@
         xh4 = s["xh4"][slots, :]
         s["gain"][5:6, :] += jnp.sum(dgate * (xh4 * gain[4]), 0, keepdims=True)
         s["bias"][...] += jnp.broadcast_to(dgate, (SLOTS, LANES))
-        gm = dgate * forget_w + dot(dwq, attn_t[8][...])
+        gm = dgate * forget_w
         yield
         dcq, dck, dcv = attend_back(
             s["cp"][seg], pair_queries(*g_co), pair_queries(s["cq"][0, rows, :], s["cq"][1, rows, :]),
@@ -544,7 +566,7 @@
         s["dck"][slots, :] = dck
         s["dcv"][slots, :] = dcv
         yield
-        gm = gm + dot(dck, attn_t[5][...]) + dot(dcv, attn_t[6][...])
+        gm = gm + dot(jnp.concatenate([dwq, dck, dcv], 1), s["attn_t"][2:5].reshape(3 * D, D))
         s["gain"][4:5, :] += jnp.sum(gm * xh4, 0, keepdims=True)
         gmem = (gate * gz + norm_back(gm, gain[4], xh4, s["rs4"][slots, :])).astype(bf16)
         s["gmem"][slots, :] = gmem
@@ -559,7 +581,7 @@
 
     lax.fori_loop(0, NSEG - 1, backward_one, 0)
     last_step = backward(0)
-    for _ in range(3 + FF // FCHUNK):
+    for _ in range(3):
         next(last_step)
 
     cut = pl.ds(pl.multiple_of(core * BLOCK, BLOCK), BLOCK)
@@ -580,11 +602,6 @@
             own = s["small"].at[axis, here]
             remote(own, own, s["small_send"].at[axis], s["small_recv"].at[axis], along(axis, (here + step) % 4)).start()
 
-    def all_moved(ref, send_sem, recv_sem):
-        copy = remote(ref, ref, send_sem, recv_sem, sibling)
-        copy.wait_send()
-        copy.wait_recv()
-
     def small_finish(axis):
         all_moved(s["small"].at[axis, pl.ds(0, 3)], s["small_send"].at[axis], s["small_recv"].at[axis])
         return (s["small"][axis, 0] + s["small"][axis, 1]) + (s["small"][axis, 2] + s["small"][axis, 3])
@@ -622,80 +639,83 @@
         def pass_on(rows, device, i):
             copy(mine.at[rows], mine.at[rows], device, i)
 
+        def pass_over(rows):
+            remote(mine.at[rows], mine.at[rows], s["send"].at[chunk], s["over"].at[chunk], sibling).start()
+
         half0, half1 = pl.ds(0, 8 * r), pl.ds(8 * r, 8 * r)
         copy(dw.at[block(i1 + 2, 0, 8)], near.at[0], right, 0)
-        copy(dw.at[block(i1 + 2, 8, 8)], near.at[1], left, 1)
-        copy(dw.at[block(i1 + 1, 8, 8)], far.at[0, half1], right, 2)
-        copy(dw.at[block(i1 + 3, 0, 8)], far.at[1, half0], left, 2)
-        yield
-        arrived(near.at[0], 0)
+        copy(dw.at[block(i1 + 2, 8, 8)], near.at[1], left, 0)
+        copy(dw.at[block(i1 + 1, 8, 8)], far.at[0, half1], right, 1)
+        copy(dw.at[block(i1 + 3, 0, 8)], far.at[1, half0], left, 1)
+        yield
+        arrived(near, 0)
         near[0] = add([near.at[0], dw.at[block(i1 + 1, 0, 8)]])
-        copy(near.at[0], far.at[0, half0], right, 2)
-        arrived(near.at[1], 1)
+        copy(near.at[0], far.at[0, half0], right, 1)
         near[1] = add([near.at[1], dw.at[block(i1 + 3, 8, 8)]])
-        copy(near.at[1], far.at[1, half1], left, 2)
-        yield
-        arrived(far, 2)
+        copy(near.at[1], far.at[1, half1], left, 1)
+        yield
+        arrived(far, 1)
         far[0] = add([far.at[0], far.at[1], dw.at[block(i1)]])
         for b, slot, to in others(axes[1], i2):
-            copy(far.at[0, rows_at(b * 4 * r, 4 * r)], mid.at[slot], to, 3)
-        yield
-        arrived(mid, 3)
-        quad[i3] = add([mid.at[0], mid.at[1], mid.at[2], far.at[0, rows_at(i2 * 4 * r, 4 * r)]])
+            copy(far.at[0, rows_at(b * 4 * r, 4 * r)], mid.at[slot], to, 2)
+        yield
+        arrived(mid, 2)
+        middle = [mid.at[0], mid.at[1], mid.at[2], far.at[0, rows_at(i2 * 4 * r, 4 * r)]]
+        home = rows_at(base + (i1 * 16 + i2 * 4) * r, 4 * r)
+        quad[i3] = add(middle)
         for _, _, to in others(axes[2], i3):
-            copy(quad.at[i3], quad.at[i3], to, 4)
-        yield
-        arrived(quad.at[pl.ds(0, 3)], 4)
+            copy(quad.at[i3], quad.at[i3], to, 3)
+        yield
+        arrived(quad.at[pl.ds(0, 3)], 3)
         last[...] = add([quad.at[i] for i in range(4)])
-        home = rows_at(base + (i1 * 16 + i2 * 4) * r, 4 * r)
         keep = pltpu.make_async_copy(last, mine.at[home], s["own"].at[chunk, part])
         keep.start()
         for _, _, to in others(axes[1], i2):
-            copy(last, mine.at[home], to, 5)
+            copy(last, mine.at[home], to, 4)
         yield
         keep.wait()
-        arrived(mine.at[rows_at(base, 12 * r)], 5)
-        pass_on(block(i1), right, 6)
-        pass_on(block(i1), left, 7)
-        pass_on(block(i1), sibling, 9)
-        yield
-        arrived(mine.at[block(i1 + 3)], 6)
-        pass_on(block(i1 + 3, 0, 8), right, 8)
-        pass_on(block(i1 + 3), sibling, 9)
-        arrived(mine.at[block(i1 + 1)], 7)
-        pass_on(block(i1 + 1, 8, 8), left, 8)
-        pass_on(block(i1 + 1), sibling, 9)
-        yield
-        arrived(mine.at[block(i1 + 2)], 8)
-        pass_on(block(i1 + 2), sibling, 9)
-        yield
-        arrived(full_ref.at[1 - core, rows_at(base, 64 * r)], 9)
+        arrived(mine.at[rows_at(base, 12 * r)], 4)
+        pass_on(block(i1), right, 5)
+        pass_on(block(i1), left, 5)
+        pass_over(block(i1))
+        yield
+        arrived(mine.at[rows_at(base, 32 * r)], 5)
+        pass_on(block(i1 + 3, 0, 8), right, 6)
+        pass_on(block(i1 + 1, 8, 8), left, 6)
+        pass_over(block(i1 + 3))
+        pass_over(block(i1 + 1))
+        yield
+        arrived(mine.at[block(i1 + 2)], 6)
+        pass_over(block(i1 + 2))
+        yield
         if part == 2:
-            sent = full_ref.at[core, rows_at(0, 196 * UNIT * sum(CHUNKS[chunk]))]
-            remote(sent, sent, s["send"].at[chunk], s["recv"].at[chunk, part, 0], sibling).wait_send()
-        yield
-
-    def chunk_steps(chunk):
-        parts = [part_steps(chunk, part) for part in range(3)]
-        while True:
-            for part in parts:
-                next(part)
-            yield
-
-    chunks = [chunk_steps(chunk) for chunk in range(len(CHUNKS))]
+            units = sum(CHUNKS[chunk]) * UNIT
+            start = base + 64 * r - 64 * units
+            got = full_ref.at[1 - core, rows_at(start, 64 * units)]
+            remote(got, got, s["send"].at[chunk], s["over"].at[chunk], sibling).wait_recv()
+            sent = full_ref.at[core, rows_at(0, 196 * units)]
+            remote(sent, sent, s["send"].at[chunk], s["over"].at[chunk], sibling).wait_send()
+        yield
+
+    chunks = [[part_steps(chunk, part) for part in range(3)] for chunk in range(len(CHUNKS))]
 
     def go(*order):
         for chunk in order:
-            next(chunks[chunk])
+            for part in chunks[chunk]:
+                next(part)
 
     for i in range(4):
-        put(i, dot_tn(s["n2"][:, cut], s["gul"][:, i * D : (i + 1) * D]))
+        cut_i = pl.ds(pl.multiple_of(core * 4 * BLOCK + i * BLOCK, BLOCK), BLOCK)
+        put(i, dot_tn(s["hid"][:, cut_i], s["gyl"][...]))
+        if i % 2:
+            next(chunks[0][i // 2])
+    put_products(4, [("mlow", "dwq"), ("t", "dwk")])
+    next(chunks[0][2])
+    for _ in range(FF // FCHUNK):
+        next(last_step)
+    put_products(6, [("t", "dwv"), ("wo", "gup")])
     for i in range(4):
-        if i == 2:
-            go(0)
-        cut_i = pl.ds(pl.multiple_of(core * 4 * BLOCK + i * BLOCK, BLOCK), BLOCK)
-        put(4 + i, dot_tn(s["hid"][:, cut_i], s["gyl"][...]))
-    put_products(8, [("mlow", "dwq"), ("t", "dwk"), ("t", "dwv"), ("wo", "gup")])
+        put(8 + i, dot_tn(s["n2"][:, cut], s["gul"][:, i * D : (i + 1) * D]))
     go(1)
     together(last_step)
     results((3,), results_start)
@@ -759,7 +779,7 @@
             jax.ShapeDtypeStruct((2, SLOTS, D), bf16),
             jax.ShapeDtypeStruct((8, D), f32),
         ),
-        in_specs=[hbm] * 4 + [vmem] + [hbm] * 3 + [vmem] * 3,
+        in_specs=[hbm] * 11,
         out_specs=[hbm] * 5 + [vmem],
         scratch_shapes=[scratch_buffers()],
         compiler_params=pltpu.CompilerParams(collective_id=1, has_side_effects=True, vmem_limit_bytes=63 << 20),
@@ -779,10 +799,11 @@
 
     def target(i, half):
         if i < 4:
-            return in_ref.at[pl.ds(half * BLOCK, BLOCK), pl.ds(i * D, D)]
-        if i < 8:
-            return out_ref.at[pl.ds(half * 4 * BLOCK + (i - 4) * BLOCK, BLOCK), :]
-        return attn_ref.at[i if i < 12 else i - 8 if i < 16 else 3 if i == 16 else i - 17, pl.ds(half * BLOCK, BLOCK), :]
+            return out_ref.at[pl.ds(half * 4 * BLOCK + i * BLOCK, BLOCK), :]
+        if 8 <= i < 12:
+            return in_ref.at[pl.ds(half * BLOCK, BLOCK), pl.ds((i - 8) * D, D)]
+        index = i + 4 if i < 8 else i - 8 if i < 16 else 3 if i == 16 else i - 17
+        return attn_ref.at[index, pl.ds(half * BLOCK, BLOCK), :]
 
     def store(i, half):
         return pltpu.make_async_copy(wide_s.at[i, half], target(i, half), store_sem)

time: 111 us -> 109 us (0.982)
  Pallas kernels: 110 us -> 108 us
    pallas_call x1, Pallas kernels: 97.1 us -> 95.7 us  [run_fused(): pl.pallas_call(fused_kernel, out_shape=(jax.ShapeDtypeStruct((2, FLAT, LA...]
where the time goes in v7:
time: 109 us
  Pallas kernels  108 us (99%)
    pallas_call x1, Pallas kernels, run_fused(): pl.pallas_call(fused_kernel, out_shape=(jax.ShapeDtypeStruct((2, FLAT, LA...  95.7 us
    pallas_call x1, Pallas kernels, run_widen(): pl.pallas_call(widen_kernel, out_shape=(jax.ShapeDtypeStruct((12, D, D),...  12.5 us

profile of v7, /device:TPU:1, one launch (start us, length us, event | category | flops | bytes accessed | tf_op | source)
XLA Modules:
  0.0 109.0 jit_solution(13293358690837111705)
XLA Ops:
  0.6 95.7 %layer_and_sums.1 = (bf16[2,20480,128]{2,1,0:T(8,128)(2,1)}, bf16[2,128,512]{2,1,0:T(8,128)(2,1)}, bf16[2,64,512]{2,1,0:T(8,128)(2,1)}, bf16[2,128,512]{2,1,0:T(...) custom-call(bf16[2,128,512]{2,1,0:T(8,128)(2,1)} %tok_ref.1, bf16[2,128,512]{2,1,0:T(8,128)(2,1)} %ocot_ref.1, ...), custom_call_target="tpu_custom_call" | custom-call | tf_op jit(solution)/shard_map/layer_and_sums/pallas_call | solution.py:772
  96.4 12.5 %widen_gradients.1 = (f32[12,512,512]{2,1,0:T(8,128)}, f32[512,2048]{1,0:T(8,128)}, f32[2048,512]{1,0:T(8,128)}, bf16[2,128,512]{2,1,0:T(8,128)(2,1)}, bf16[2,64...) custom-call(bf16[2,20,4,256,128]{4,3,2,1,0:T(8,128)(2,1)} %bitcast.7, ...), custom_call_target="tpu_custom_call" | custom-call | tf_op jit(solution)/shard_map/widen_gradients/pallas_call | solution.py:833

commit v8 on v7

--- a/solution.py
+++ b/solution.py
@@ -1,4 +1,4 @@
-import functools
+from types import SimpleNamespace
 
 import jax
 import jax.numpy as jnp
@@ -184,8 +184,9 @@
 def fused_kernel(
     tok_ref, ocot_ref, mcot_ref, mem_ref, len_ref, attn_ref, win_ref, wout_ref, gains_ref, fw_ref, fb_ref,
     full_ref, act_out, mout_out, gtok_out, gmem_out, small_out,
-    s,
+    scratch,
 ):
+    s = SimpleNamespace(**scratch)
     place = my_place()
     x, y, z, core = place
     owner, stream = x // 2, x % 2
@@ -201,14 +202,14 @@
         return pl.ds(pl.multiple_of(first, UNIT), count)
 
     loads = [
-        pltpu.make_async_copy(attn_ref.at[pl.ds(0, 4)], s["attn"].at[pl.ds(0, 4)], s["load"].at[0]),
-        pltpu.make_async_copy(attn_ref.at[pl.ds(4, 8)], s["attn"].at[pl.ds(4, 8)], s["load"].at[1]),
-        pltpu.make_async_copy(win_ref, s["win"], s["load"].at[2]),
-        pltpu.make_async_copy(wout_ref, s["wout"], s["load"].at[3]),
+        pltpu.make_async_copy(attn_ref.at[pl.ds(0, 4)], s.attn.at[pl.ds(0, 4)], s.load.at[0]),
+        pltpu.make_async_copy(attn_ref.at[pl.ds(4, 8)], s.attn.at[pl.ds(4, 8)], s.load.at[1]),
+        pltpu.make_async_copy(win_ref, s.win, s.load.at[2]),
+        pltpu.make_async_copy(wout_ref, s.wout, s.load.at[3]),
     ]
     small_loads = [
-        pltpu.make_async_copy(src, s[name], s["load"].at[4 + i])
-        for i, (src, name) in enumerate([(len_ref, "lens_in"), (gains_ref, "gains"), (fw_ref, "fw"), (fb_ref, "fb")])
+        pltpu.make_async_copy(src, dst, s.load.at[4 + i])
+        for i, (src, dst) in enumerate([(len_ref, s.lens_in), (gains_ref, s.gains), (fw_ref, s.fw), (fb_ref, s.fb)])
     ]
     for load in small_loads:
         load.start()
@@ -229,11 +230,11 @@
             signal(barrier, device_at(2 * core + k, y, z, owner))
 
     small_loads[0].wait()
-    s["lens_own"][...] = jnp.zeros_like(s["lens_own"])
-    s["lens_own"][0:2, 0:NDOC] = s["lens_in"][...]
+    s.lens_own[...] = jnp.zeros_like(s.lens_own)
+    s.lens_own[0:2, 0:NDOC] = s.lens_in[...]
     pl.semaphore_wait(barrier, 16 - 3 * mine_here.astype(jnp.int32))
 
-    arrays = [(tok_ref, s["tok"], SEG), (ocot_ref, s["ocot"], SEG), (mcot_ref, s["mcot"], SLOTS)]
+    arrays = [(tok_ref, s.tok, SEG), (ocot_ref, s.ocot, SEG), (mcot_ref, s.mcot, SLOTS)]
 
     def gather_sends(i, start):
         src, dst, count = arrays[i]
@@ -246,16 +247,16 @@
                 for to_core in range(2):
                     copy = remote(
                         src.at[st, pl.ds(to_core * half, half)], dst.at[rows_at(x * count + to_core * half, half)],
-                        s["in_send"].at[st, to_core, i], s["in_recv"].at[x, i], device_at(chip, y, z, to_core),
+                        s.in_send.at[st, to_core, i], s.in_recv.at[x, i], device_at(chip, y, z, to_core),
                     )
                     copy.start() if start else copy.wait_send()
 
             @pl.when(chip == x)
             def _():
                 target = dst.at[rows_at(x * count, count)]
-                copy = remote(src.at[st], target, s["in_send"].at[st, 0, i], s["in_recv"].at[x, i], sibling)
+                copy = remote(src.at[st], target, s.in_send.at[st, 0, i], s.in_recv.at[x, i], sibling)
                 if start:
-                    pltpu.make_async_copy(src.at[st], target, s["in_local"].at[i]).start()
+                    pltpu.make_async_copy(src.at[st], target, s.in_local.at[i]).start()
                     copy.start()
                 else:
                     copy.wait_send()
@@ -266,11 +267,11 @@
 
         @pl.when(mine_here)
         def _():
-            pltpu.make_async_copy(src.at[stream], whole, s["in_local"].at[i]).wait()
+            pltpu.make_async_copy(src.at[stream], whole, s.in_local.at[i]).wait()
 
         @pl.when(jnp.logical_not(mine_here))
         def _():
-            remote(whole, whole, s["in_send"].at[0, 0, i], s["in_recv"].at[x, i], sibling).wait_recv()
+            remote(whole, whole, s.in_send.at[0, 0, i], s.in_recv.at[x, i], sibling).wait_recv()
 
     def all_moved(ref, send_sem, recv_sem):
         copy = remote(ref, ref, send_sem, recv_sem, sibling)
@@ -284,62 +285,62 @@
             seg = (x + step) % 4
             part = dst.at[rows_at(seg * count + core * half, half)]
             remote(
-                part, part, s["in_send"].at[0, 0, i], s["in_recv"].at[seg, i], device_at(seg, y, z, owner)
+                part, part, s.in_send.at[0, 0, i], s.in_recv.at[seg, i], device_at(seg, y, z, owner)
             ).wait_recv()
-            remote(part, part, s["pass_send"].at[i], s["pass_recv"].at[i], sibling).start()
+            remote(part, part, s.pass_send.at[i], s.pass_recv.at[i], sibling).start()
 
     def gather_finish(i):
         src, dst, count = arrays[i]
         gather_sends(i, False)
         three_halves = dst.at[pl.ds(0, 3 * count // 2)]
-        all_moved(three_halves, s["pass_send"].at[i], s["pass_recv"].at[i])
+        all_moved(three_halves, s.pass_send.at[i], s.pass_recv.at[i])
 
     gather_sends(0, True)
 
-    firsts = [(mem_ref.at[stream], s["mem"]), (s["lens_own"], s["lens"])]
+    firsts = [(mem_ref.at[stream], s.mem), (s.lens_own, s.lens)]
     for i, (src, dst) in enumerate(firsts):
 
         @pl.when(mine_here)
         def _():
-            remote(src, dst, s["first_send"].at[i], s["first_recv"].at[i], sibling).start()
-            pltpu.make_async_copy(src, dst, s["in_local"].at[3 + i]).start()
+            remote(src, dst, s.first_send.at[i], s.first_recv.at[i], sibling).start()
+            pltpu.make_async_copy(src, dst, s.in_local.at[3 + i]).start()
 
     loads[1].wait()
     for i, index in enumerate(TURNED):
-        s["attn_t"][i] = jnp.transpose(s["attn"][index])
+        s.attn_t[i] = jnp.transpose(s.attn[index])
     loads[2].wait()
     for c in range(0, FF, D):
-        s["win_t"][c : c + D, :] = jnp.transpose(s["win"][:, c : c + D])
+        s.win_t[c : c + D, :] = jnp.transpose(s.win[:, c : c + D])
     loads[3].wait()
     for c in range(0, FF, D):
-        s["wout_t"][:, c : c + D] = jnp.transpose(s["wout"][c : c + D, :])
+        s.wout_t[:, c : c + D] = jnp.transpose(s.wout[c : c + D, :])
     loads[0].wait()
 
     for i, (src, dst) in enumerate(firsts):
 
         @pl.when(mine_here)
         def _():
-            remote(src, dst, s["first_send"].at[i], s["first_recv"].at[i], sibling).wait_send()
-            pltpu.make_async_copy(src, dst, s["in_local"].at[3 + i]).wait()
+            remote(src, dst, s.first_send.at[i], s.first_recv.at[i], sibling).wait_send()
+            pltpu.make_async_copy(src, dst, s.in_local.at[3 + i]).wait()
 
         @pl.when(jnp.logical_not(mine_here))
         def _():
-            remote(src, dst, s["first_send"].at[i], s["first_recv"].at[i], sibling).wait_recv()
-
-    attn, win, wout = s["attn"], s["win"], s["wout"]
-    attn_t = {index: s["attn_t"].at[i] for i, index in enumerate(TURNED)}
-    win_t, wout_t = s["win_t"], s["wout_t"]
+            remote(src, dst, s.first_send.at[i], s.first_recv.at[i], sibling).wait_recv()
+
+    attn, win, wout = s.attn, s.win, s.wout
+    attn_t = {index: s.attn_t.at[i] for i, index in enumerate(TURNED)}
+    win_t, wout_t = s.win_t, s.wout_t
     for load in small_loads[1:]:
         load.wait()
-    gain = [s["gains"][i : i + 1, :] for i in range(5)]
-    forget_w = s["fw"][...]
+    gain = [s.gains[i : i + 1, :] for i in range(5)]
+    forget_w = s.fw[...]
     square = (SLOTS, SLOTS)
     diagonal = lax.broadcasted_iota(jnp.int32, square, 0) == lax.broadcasted_iota(jnp.int32, square, 1)
-    forget_bias = jnp.sum(jnp.where(diagonal, jnp.broadcast_to(s["fb"][...], square), 0.0), -1, keepdims=True)
+    forget_bias = jnp.sum(jnp.where(diagonal, jnp.broadcast_to(s.fb[...], square), 0.0), -1, keepdims=True)
 
     ends = []
     for j in range(NDOC):
-        ends.append(s["lens"][pl.ds(stream, 1), j : j + 1] + (ends[-1] if ends else 0))
+        ends.append(s.lens[pl.ds(stream, 1), j : j + 1] + (ends[-1] if ends else 0))
 
     def doc_ids(shape, dim, base):
         pos = lax.broadcasted_iota(jnp.int32, shape, dim) + base
@@ -362,101 +363,101 @@
 
     def self_forward(seg):
         rows = row_cut(seg)
-        tok = s["tok"][rows, :].astype(f32)
+        tok = s.tok[rows, :].astype(f32)
         xhat, rstd = norm_stats(tok)
-        s["xh0"][rows, :] = xhat.astype(bf16)
-        s["rs0"][rows, :] = rstd
+        s.xh0[rows, :] = xhat.astype(bf16)
+        s.rs0[rows, :] = rstd
         h = (xhat * gain[0]).astype(bf16)
-        s["h"][rows, :] = h
+        s.h[rows, :] = h
         yield
         q0, q1 = head_halves(dot(h, attn[0]) * SCALE)
-        s["q"][0, rows, :] = q0
-        s["q"][1, rows, :] = q1
+        s.q[0, rows, :] = q0
+        s.q[1, rows, :] = q1
         yield
         k = dot(h, attn[1]).astype(bf16)
         v = dot(h, attn[2]).astype(bf16)
-        s["k"][rows, :] = k
-        s["v"][rows, :] = v
+        s.k[rows, :] = k
+        s.v[rows, :] = v
         yield
         same = doc_ids((SEG, SEG), 0, seg * SEG) == doc_ids((SEG, SEG), 1, seg * SEG)
         bias = jnp.concatenate([jnp.where(same, 0.0, -1e30)] * HEADS, 1)
-        s["p"][seg], o = attend(pair_queries(q0, q1), pair_lanes(k), pair_lanes(v), bias)
-        s["o"][rows, :] = o
+        s.p[seg], o = attend(pair_queries(q0, q1), pair_lanes(k), pair_lanes(v), bias)
+        s.o[rows, :] = o
         yield
         res = tok + dot(o, attn[3])
-        s["res"][rows, :] = res
+        s.res[rows, :] = res
         xhat, rstd = norm_stats(res)
-        s["xh1"][rows, :] = xhat.astype(bf16)
-        s["rs1"][rows, :] = rstd
+        s.xh1[rows, :] = xhat.astype(bf16)
+        s.rs1[rows, :] = rstd
         n1 = (xhat * gain[1]).astype(bf16)
-        s["n1"][rows, :] = n1
-        yield
-        s["cq"][0, rows, :], s["cq"][1, rows, :] = head_halves(dot(n1, attn[4]) * SCALE)
+        s.n1[rows, :] = n1
+        yield
+        s.cq[0, rows, :], s.cq[1, rows, :] = head_halves(dot(n1, attn[4]) * SCALE)
         yield
 
     def forward(seg, mem):
         rows, slots = row_cut(seg), slot_cut(seg)
         xhat, rstd = norm_stats(mem)
-        s["xh4"][slots, :] = xhat
-        s["rs4"][slots, :] = rstd
+        s.xh4[slots, :] = xhat
+        s.rs4[slots, :] = rstd
         m = xhat * gain[4]
         mlow = m.astype(bf16)
-        s["mlow"][slots, :] = mlow
+        s.mlow[slots, :] = mlow
         ck = dot(mlow, attn[5]).astype(bf16)
         cv = dot(mlow, attn[6]).astype(bf16)
-        s["ck"][slots, :] = ck
-        s["cv"][slots, :] = cv
-        yield
-        s["cp"][seg], co = attend(
-            pair_queries(s["cq"][0, rows, :], s["cq"][1, rows, :]), pair_lanes(ck), pair_lanes(cv), 0.0
+        s.ck[slots, :] = ck
+        s.cv[slots, :] = cv
+        yield
+        s.cp[seg], co = attend(
+            pair_queries(s.cq[0, rows, :], s.cq[1, rows, :]), pair_lanes(ck), pair_lanes(cv), 0.0
         )
-        s["co"][rows, :] = co
-        yield
-        res = s["res"][rows, :] + dot(co, attn[7])
+        s.co[rows, :] = co
+        yield
+        res = s.res[rows, :] + dot(co, attn[7])
         xhat, rstd = norm_stats(res)
-        s["xh2"][rows, :] = xhat.astype(bf16)
-        s["rs2"][rows, :] = rstd
+        s.xh2[rows, :] = xhat.astype(bf16)
+        s.rs2[rows, :] = rstd
         n2 = (xhat * gain[2]).astype(bf16)
-        s["n2"][rows, :] = n2
+        s.n2[rows, :] = n2
         yield
         for c in range(0, FF, FCHUNK):
             hid, slope = gelu_both(dot(n2, win[:, c : c + FCHUNK]))
             hid = hid.astype(bf16)
-            s["hid"][rows, c : c + FCHUNK] = hid
-            s["gul"][rows, c : c + FCHUNK] = slope
+            s.hid[rows, c : c + FCHUNK] = hid
+            s.gul[rows, c : c + FCHUNK] = slope
             res = res + dot(hid, wout[c : c + FCHUNK, :])
             yield
-        s["act"][rows, :] = res.astype(bf16)
+        s.act[rows, :] = res.astype(bf16)
         xhat, rstd = norm_stats(res)
-        s["xh3"][rows, :] = xhat.astype(bf16)
-        s["rs3"][rows, :] = rstd
+        s.xh3[rows, :] = xhat.astype(bf16)
+        s.rs3[rows, :] = rstd
         t = (xhat * gain[3]).astype(bf16)
-        s["t"][rows, :] = t
+        s.t[rows, :] = t
         yield
         gate = jax.nn.sigmoid(jnp.sum(m * forget_w, -1, keepdims=True) + forget_bias)
-        s["gate"][slots, :] = gate
+        s.gate[slots, :] = gate
         wq0, wq1 = head_halves(dot(mlow, attn[8]) * SCALE)
-        s["wq"][0, slots, :] = wq0
-        s["wq"][1, slots, :] = wq1
+        s.wq[0, slots, :] = wq0
+        s.wq[1, slots, :] = wq1
         wk = dot(t, attn[9]).astype(bf16)
         wv = dot(t, attn[10]).astype(bf16)
-        s["wk"][rows, :] = wk
-        s["wv"][rows, :] = wv
+        s.wk[rows, :] = wk
+        s.wv[rows, :] = wv
         yield
         pos = lax.broadcasted_iota(jnp.int32, (SEG, HEADS * SLOTS), 0) + seg * SEG
-        s["wp"][seg], wo = attend(
+        s.wp[seg], wo = attend(
             pair_queries(wq0, wq1), pair_lanes(wk), pair_lanes(wv), jnp.where(pos < ends[-1], 0.0, -1e30)
         )
-        s["wo"][slots, :] = wo
+        s.wo[slots, :] = wo
         yield
         update = dot(wo, attn[11])
-        s["upd"][slots, :] = mem - update
+        s.upd[slots, :] = mem - update
         fresh = (update + gate * (mem - update)).astype(bf16)
-        s["mout"][slots, :] = fresh
-        s["mem"][...] = fresh
-        yield
-
-    first_step = forward(0, s["mem"][...].astype(f32))
+        s.mout[slots, :] = fresh
+        s.mem[...] = fresh
+        yield
+
+    first_step = forward(0, s.mem[...].astype(f32))
     next(first_step)
     gather_forward(0)
     gather_own(0)
@@ -467,11 +468,11 @@
     rest = [step + (x <= step).astype(jnp.int32) for step in range(NSEG - 1)]
     together(self_forward(rest[0]))
     together(first_step, self_forward(rest[1]))
-    together(forward(1, s["mem"][...].astype(f32)), self_forward(rest[2]))
-    together(forward(2, s["mem"][...].astype(f32)))
+    together(forward(1, s.mem[...].astype(f32)), self_forward(rest[2]))
+    together(forward(2, s.mem[...].astype(f32)))
     gather_forward(1)
     gather_forward(2)
-    together(forward(NSEG - 1, s["mem"][...].astype(f32)))
+    together(forward(NSEG - 1, s.mem[...].astype(f32)))
 
     def results(indices, do):
         for k in range(2):
@@ -479,8 +480,8 @@
             here = jnp.logical_and(seg == x, mine_here)
             peer = device_at(seg, y, z, owner)
             sources = [
-                (s["act"].at[rows_at(seg * SEG, SEG)], act_out), (s["mout"].at[rows_at(seg * SLOTS, SLOTS)], mout_out),
-                (s["gtok"].at[rows_at(seg * SEG, SEG)], gtok_out), (s["gmem"].at[rows_at(seg * SLOTS, SLOTS)], gmem_out),
+                (s.act.at[rows_at(seg * SEG, SEG)], act_out), (s.mout.at[rows_at(seg * SLOTS, SLOTS)], mout_out),
+                (s.gtok.at[rows_at(seg * SEG, SEG)], gtok_out), (s.gmem.at[rows_at(seg * SLOTS, SLOTS)], gmem_out),
             ]
             for i in indices:
                 src, dst = sources[i]
@@ -488,13 +489,13 @@
                 @pl.when(jnp.logical_not(here))
                 def _():
                     do(
-                        remote(src, dst.at[stream], s["out_send"].at[k, i], s["out_recv"].at[stream, i], peer),
-                        remote(src, dst.at[k], s["out_send"].at[k, i], s["out_recv"].at[k, i], peer),
+                        remote(src, dst.at[stream], s.out_send.at[k, i], s.out_recv.at[stream, i], peer),
+                        remote(src, dst.at[k], s.out_send.at[k, i], s.out_recv.at[k, i], peer),
                     )
 
                 @pl.when(here)
                 def _():
-                    do(pltpu.make_async_copy(src, dst.at[stream], s["out_local"].at[i]), None)
+                    do(pltpu.make_async_copy(src, dst.at[stream], s.out_local.at[i]), None)
 
     def results_start(copy, back):
         copy.start()
@@ -511,69 +512,69 @@
         gather_own(i)
         gather_finish(i)
 
-    s["gain"][...] = jnp.zeros_like(s["gain"])
-    s["bias"][...] = jnp.zeros_like(s["bias"])
+    s.gain[...] = jnp.zeros_like(s.gain)
+    s.bias[...] = jnp.zeros_like(s.bias)
 
     def backward(seg):
         rows, slots = row_cut(seg), slot_cut(seg)
-        gz = (s["mcot"][slots, :].astype(f32) + s["mem"][...].astype(f32)).astype(bf16).astype(f32)
-        gate = s["gate"][slots, :]
+        gz = (s.mcot[slots, :].astype(f32) + s.mem[...].astype(f32)).astype(bf16).astype(f32)
+        gate = s.gate[slots, :]
         gup = ((1.0 - gate) * gz).astype(bf16)
-        s["gup"][slots, :] = gup
+        s.gup[slots, :] = gup
         g_wo = head_halves(dot(gup, attn_t[11][...]))
         yield
         dwq, dwk, dwv = attend_back(
-            s["wp"][seg], pair_queries(*g_wo), pair_queries(s["wq"][0, slots, :], s["wq"][1, slots, :]),
-            pair_lanes(s["wk"][rows, :]), pair_lanes(s["wv"][rows, :]),
+            s.wp[seg], pair_queries(*g_wo), pair_queries(s.wq[0, slots, :], s.wq[1, slots, :]),
+            pair_lanes(s.wk[rows, :]), pair_lanes(s.wv[rows, :]),
         )
-        s["dwq"][slots, :] = dwq
-        s["dwk"][rows, :] = dwk
-        s["dwv"][rows, :] = dwv
-        yield
-        gt = dot(jnp.concatenate([dwk, dwv], 1), s["attn_t"][5:7].reshape(2 * D, D))
-        xhat = s["xh3"][rows, :].astype(f32)
-        s["gain"][3:4, :] += jnp.sum(gt * xhat, 0, keepdims=True)
-        gy = s["ocot"][rows, :].astype(f32) + norm_back(gt, gain[3], xhat, s["rs3"][rows, :])
+        s.dwq[slots, :] = dwq
+        s.dwk[rows, :] = dwk
+        s.dwv[rows, :] = dwv
+        yield
+        gt = dot(jnp.concatenate([dwk, dwv], 1), s.attn_t[5:7].reshape(2 * D, D))
+        xhat = s.xh3[rows, :].astype(f32)
+        s.gain[3:4, :] += jnp.sum(gt * xhat, 0, keepdims=True)
+        gy = s.ocot[rows, :].astype(f32) + norm_back(gt, gain[3], xhat, s.rs3[rows, :])
         gyl = gy.astype(bf16)
-        s["gyl"][rows, :] = gyl
+        s.gyl[rows, :] = gyl
         yield
         gn2 = jnp.zeros((SEG, D), f32)
         for c in range(0, FF, FCHUNK):
             ghid = dot(gyl, wout_t[:, c : c + FCHUNK])
-            gul = (ghid * s["gul"][rows, c : c + FCHUNK].astype(f32)).astype(bf16)
-            s["gul"][rows, c : c + FCHUNK] = gul
+            gul = (ghid * s.gul[rows, c : c + FCHUNK].astype(f32)).astype(bf16)
+            s.gul[rows, c : c + FCHUNK] = gul
             gn2 = gn2 + dot(gul, win_t[c : c + FCHUNK, :])
             yield
-        xhat = s["xh2"][rows, :].astype(f32)
-        s["gain"][2:3, :] += jnp.sum(gn2 * xhat, 0, keepdims=True)
-        gb = gy + norm_back(gn2, gain[2], xhat, s["rs2"][rows, :])
-        s["res"][rows, :] = gb
+        xhat = s.xh2[rows, :].astype(f32)
+        s.gain[2:3, :] += jnp.sum(gn2 * xhat, 0, keepdims=True)
+        gb = gy + norm_back(gn2, gain[2], xhat, s.rs2[rows, :])
+        s.res[rows, :] = gb
         gbl = gb.astype(bf16)
-        s["gbl"][rows, :] = gbl
+        s.gbl[rows, :] = gbl
         yield
         g_co = head_halves(dot(gbl, attn_t[7][...]))
-        dgate = jnp.sum(gz * s["upd"][slots, :], -1, keepdims=True) * gate * (1.0 - gate)
-        xh4 = s["xh4"][slots, :]
-        s["gain"][5:6, :] += jnp.sum(dgate * (xh4 * gain[4]), 0, keepdims=True)
-        s["bias"][...] += jnp.broadcast_to(dgate, (SLOTS, LANES))
+        dgate = jnp.sum(gz * s.upd[slots, :], -1, keepdims=True) * gate * (1.0 - gate)
+        xh4 = s.xh4[slots, :]
+        s.gain[5:6, :] += jnp.sum(dgate * (xh4 * gain[4]), 0, keepdims=True)
+        s.bias[...] += jnp.broadcast_to(dgate, (SLOTS, LANES))
         gm = dgate * forget_w
         yield
         dcq, dck, dcv = attend_back(
-            s["cp"][seg], pair_queries(*g_co), pair_queries(s["cq"][0, rows, :], s["cq"][1, rows, :]),
-            pair_lanes(s["ck"][slots, :]), pair_lanes(s["cv"][slots, :]),
+            s.cp[seg], pair_queries(*g_co), pair_queries(s.cq[0, rows, :], s.cq[1, rows, :]),
+            pair_lanes(s.ck[slots, :]), pair_lanes(s.cv[slots, :]),
         )
-        s["dcq"][rows, :] = dcq
-        s["dck"][slots, :] = dck
-        s["dcv"][slots, :] = dcv
-        yield
-        gm = gm + dot(jnp.concatenate([dwq, dck, dcv], 1), s["attn_t"][2:5].reshape(3 * D, D))
-        s["gain"][4:5, :] += jnp.sum(gm * xh4, 0, keepdims=True)
-        gmem = (gate * gz + norm_back(gm, gain[4], xh4, s["rs4"][slots, :])).astype(bf16)
-        s["gmem"][slots, :] = gmem
-        s["mem"][...] = gmem
-        yield
-
-    s["mem"][...] = jnp.zeros_like(s["mem"])
+        s.dcq[rows, :] = dcq
+        s.dck[slots, :] = dck
+        s.dcv[slots, :] = dcv
+        yield
+        gm = gm + dot(jnp.concatenate([dwq, dck, dcv], 1), s.attn_t[2:5].reshape(3 * D, D))
+        s.gain[4:5, :] += jnp.sum(gm * xh4, 0, keepdims=True)
+        gmem = (gate * gz + norm_back(gm, gain[4], xh4, s.rs4[slots, :])).astype(bf16)
+        s.gmem[slots, :] = gmem
+        s.mem[...] = gmem
+        yield
+
+    s.mem[...] = jnp.zeros_like(s.mem)
 
     def backward_one(step, carry):
         together(backward(NSEG - 1 - step))
@@ -589,22 +590,22 @@
     def put(i, value):
         value = value.astype(bf16)
         for j in range(LANE_CUTS):
-            s["dw"][(i * LANE_CUTS + j) * BLOCK : (i * LANE_CUTS + j + 1) * BLOCK, :] = value[:, j * LANES : (j + 1) * LANES]
+            s.dw[(i * LANE_CUTS + j) * BLOCK : (i * LANE_CUTS + j + 1) * BLOCK, :] = value[:, j * LANES : (j + 1) * LANES]
 
     def put_products(base, names):
         for i, (left, right) in enumerate(names):
-            put(base + i, dot_tn(s[left][:, cut], s[right][...]))
+            put(base + i, dot_tn(left[:, cut], right[...]))
 
     def small_start(axis, value):
         here = place[axis]
-        s["small"][axis, here] = value
+        s.small[axis, here] = value
         for step in range(1, 4):
-            own = s["small"].at[axis, here]
-            remote(own, own, s["small_send"].at[axis], s["small_recv"].at[axis], along(axis, (here + step) % 4)).start()
+            own = s.small.at[axis, here]
+            remote(own, own, s.small_send.at[axis], s.small_recv.at[axis], along(axis, (here + step) % 4)).start()
 
     def small_finish(axis):
-        all_moved(s["small"].at[axis, pl.ds(0, 3)], s["small_send"].at[axis], s["small_recv"].at[axis])
-        return (s["small"][axis, 0] + s["small"][axis, 1]) + (s["small"][axis, 2] + s["small"][axis, 3])
+        all_moved(s.small.at[axis, pl.ds(0, 3)], s.small_send.at[axis], s.small_recv.at[axis])
+        return (s.small[axis, 0] + s.small[axis, 1]) + (s.small[axis, 2] + s.small[axis, 3])
 
     def others(axis, i):
         return [((i + step) % 4, step - 1, along(axis, (i + step) % 4)) for step in range(1, 4)]
@@ -624,14 +625,14 @@
     def part_steps(chunk, part):
         r, base, axes, (i1, i2, i3) = part_place(chunk, part)
         right, left = along(axes[0], (i1 + 1) % 4), along(axes[0], (i1 + 3) % 4)
-        near, far, mid, quad, last = (s[name][chunk][part] for name in ("near", "far", "mid", "quad", "last"))
-        dw, mine = s["dw"], full_ref.at[core]
+        near, far, mid, quad, last = (refs[chunk][part] for refs in (s.near, s.far, s.mid, s.quad, s.last))
+        dw, mine = s.dw, full_ref.at[core]
 
         def copy(src, dst, device, i):
-            remote(src, dst, s["send"].at[chunk], s["recv"].at[chunk, part, i], device).start()
+            remote(src, dst, s.send.at[chunk], s.recv.at[chunk, part, i], device).start()
 
         def arrived(ref, i):
-            remote(ref, ref, s["send"].at[chunk], s["recv"].at[chunk, part, i], sibling).wait_recv()
+            remote(ref, ref, s.send.at[chunk], s.recv.at[chunk, part, i], sibling).wait_recv()
 
         def block(b, first=0, count=16):
             return rows_at(base + (b % 4) * 16 * r + first * r, count * r)
@@ -640,7 +641,7 @@
             copy(mine.at[rows], mine.at[rows], device, i)
 
         def pass_over(rows):
-            remote(mine.at[rows], mine.at[rows], s["send"].at[chunk], s["over"].at[chunk], sibling).start()
+            remote(mine.at[rows], mine.at[rows], s.send.at[chunk], s.over.at[chunk], sibling).start()
 
         half0, half1 = pl.ds(0, 8 * r), pl.ds(8 * r, 8 * r)
         copy(dw.at[block(i1 + 2, 0, 8)], near.at[0], right, 0)
@@ -668,7 +669,7 @@
         yield
         arrived(quad.at[pl.ds(0, 3)], 3)
         last[...] = add([quad.at[i] for i in range(4)])
-        keep = pltpu.make_async_copy(last, mine.at[home], s["own"].at[chunk, part])
+        keep = pltpu.make_async_copy(last, mine.at[home], s.own.at[chunk, part])
         keep.start()
         for _, _, to in others(axes[1], i2):
             copy(last, mine.at[home], to, 4)
@@ -692,9 +693,9 @@
             units = sum(CHUNKS[chunk]) * UNIT
             start = base + 64 * r - 64 * units
             got = full_ref.at[1 - core, rows_at(start, 64 * units)]
-            remote(got, got, s["send"].at[chunk], s["over"].at[chunk], sibling).wait_recv()
+            remote(got, got, s.send.at[chunk], s.over.at[chunk], sibling).wait_recv()
             sent = full_ref.at[core, rows_at(0, 196 * units)]
-            remote(sent, sent, s["send"].at[chunk], s["over"].at[chunk], sibling).wait_send()
+            remote(sent, sent, s.send.at[chunk], s.over.at[chunk], sibling).wait_send()
         yield
 
     chunks = [[part_steps(chunk, part) for part in range(3)] for chunk in range(len(CHUNKS))]
@@ -706,38 +707,38 @@
 
     for i in range(4):
         cut_i = pl.ds(pl.multiple_of(core * 4 * BLOCK + i * BLOCK, BLOCK), BLOCK)
-        put(i, dot_tn(s["hid"][:, cut_i], s["gyl"][...]))
+        put(i, dot_tn(s.hid[:, cut_i], s.gyl[...]))
         if i % 2:
             next(chunks[0][i // 2])
-    put_products(4, [("mlow", "dwq"), ("t", "dwk")])
+    put_products(4, [(s.mlow, s.dwq), (s.t, s.dwk)])
     next(chunks[0][2])
     for _ in range(FF // FCHUNK):
         next(last_step)
-    put_products(6, [("t", "dwv"), ("wo", "gup")])
+    put_products(6, [(s.t, s.dwv), (s.wo, s.gup)])
     for i in range(4):
-        put(8 + i, dot_tn(s["n2"][:, cut], s["gul"][:, i * D : (i + 1) * D]))
+        put(8 + i, dot_tn(s.n2[:, cut], s.gul[:, i * D : (i + 1) * D]))
     go(1)
     together(last_step)
     results((3,), results_start)
-    put_products(12, [("n1", "dcq"), ("mlow", "dck"), ("mlow", "dcv"), ("co", "gbl")])
-
-    gn1 = dot_nt(s["dcq"][...], attn[4])
-    xhat = s["xh1"][...].astype(f32)
-    s["gain"][1:2, :] = jnp.sum(gn1 * xhat, 0, keepdims=True)
-    ga = s["res"][...] + norm_back(gn1, gain[1], xhat, s["rs1"][...])
-    s["res"][...] = ga
+    put_products(12, [(s.n1, s.dcq), (s.mlow, s.dck), (s.mlow, s.dcv), (s.co, s.gbl)])
+
+    gn1 = dot_nt(s.dcq[...], attn[4])
+    xhat = s.xh1[...].astype(f32)
+    s.gain[1:2, :] = jnp.sum(gn1 * xhat, 0, keepdims=True)
+    ga = s.res[...] + norm_back(gn1, gain[1], xhat, s.rs1[...])
+    s.res[...] = ga
     gal = ga.astype(bf16)
-    s["gal"][...] = gal
-    s["cq"][0], s["cq"][1] = head_halves(dot_nt(gal, attn[3]))
-    put_products(16, [("o", "gal")])
+    s.gal[...] = gal
+    s.cq[0], s.cq[1] = head_halves(dot_nt(gal, attn[3]))
+    put_products(16, [(s.o, s.gal)])
     go(2)
 
     def self_backward(seg):
         rows = row_cut(seg)
-        s["dq"][rows, :], s["dk"][rows, :], s["dv"][rows, :] = attend_back(
-            s["p"][seg], pair_queries(s["cq"][0, rows, :], s["cq"][1, rows, :]),
-            pair_queries(s["q"][0, rows, :], s["q"][1, rows, :]),
-            pair_lanes(s["k"][rows, :]), pair_lanes(s["v"][rows, :]),
+        s.dq[rows, :], s.dk[rows, :], s.dv[rows, :] = attend_back(
+            s.p[seg], pair_queries(s.cq[0, rows, :], s.cq[1, rows, :]),
+            pair_queries(s.q[0, rows, :], s.q[1, rows, :]),
+            pair_lanes(s.k[rows, :]), pair_lanes(s.v[rows, :]),
         )
 
     self_backward(0)
@@ -745,15 +746,15 @@
     self_backward(2)
     go(0)
     self_backward(3)
-    gh = dot_nt(s["dq"][...], attn[0]) + dot_nt(s["dk"][...], attn[1]) + dot_nt(s["dv"][...], attn[2])
+    gh = dot_nt(s.dq[...], attn[0]) + dot_nt(s.dk[...], attn[1]) + dot_nt(s.dv[...], attn[2])
     go(1)
-    xhat = s["xh0"][...].astype(f32)
-    s["gain"][0:1, :] = jnp.sum(gh * xhat, 0, keepdims=True)
-    s["gtok"][...] = (s["res"][...] + norm_back(gh, gain[0], xhat, s["rs0"][...])).astype(bf16)
-    s["gain"][6:7, 0:SLOTS] = jnp.sum(jnp.where(diagonal, s["bias"][:, 0:SLOTS], 0.0), 0, keepdims=True)
-    small_start(0, s["gain"][...])
+    xhat = s.xh0[...].astype(f32)
+    s.gain[0:1, :] = jnp.sum(gh * xhat, 0, keepdims=True)
+    s.gtok[...] = (s.res[...] + norm_back(gh, gain[0], xhat, s.rs0[...])).astype(bf16)
+    s.gain[6:7, 0:SLOTS] = jnp.sum(jnp.where(diagonal, s.bias[:, 0:SLOTS], 0.0), 0, keepdims=True)
+    small_start(0, s.gain[...])
     results((2,), results_start)
-    put_products(17, [("h", "dq"), ("h", "dk"), ("h", "dv")])
+    put_products(17, [(s.h, s.dq), (s.h, s.dk), (s.h, s.dv)])
     go(3, 2, 0)
     total = small_finish(0)
     small_start(1, total)

time: 109 us -> 109 us (level)
  no operation moved by 1% of the time
where the time goes in v8:
time: 109 us
  Pallas kernels  108 us (99%)
    pallas_call x1, Pallas kernels, run_fused(): pl.pallas_call(fused_kernel, out_shape=(jax.ShapeDtypeStruct((2, FLAT, LA...  95.7 us
    pallas_call x1, Pallas kernels, run_widen(): pl.pallas_call(widen_kernel, out_shape=(jax.ShapeDtypeStruct((12, D, D),...  12.5 us

profile of v8, /device:TPU:1, one launch (start us, length us, event | category | flops | bytes accessed | tf_op | source)
XLA Modules:
  0.0 109.0 jit_solution(13293358690837111705)
XLA Ops:
  0.6 95.7 %layer_and_sums.1 = (bf16[2,20480,128]{2,1,0:T(8,128)(2,1)}, bf16[2,128,512]{2,1,0:T(8,128)(2,1)}, bf16[2,64,512]{2,1,0:T(8,128)(2,1)}, bf16[2,128,512]{2,1,0:T(...) custom-call(bf16[2,128,512]{2,1,0:T(8,128)(2,1)} %tok_ref.1, bf16[2,128,512]{2,1,0:T(8,128)(2,1)} %ocot_ref.1, ...), custom_call_target="tpu_custom_call" | custom-call | tf_op jit(solution)/shard_map/layer_and_sums/pallas_call | solution.py:773
  96.4 12.5 %widen_gradients.1 = (f32[12,512,512]{2,1,0:T(8,128)}, f32[512,2048]{1,0:T(8,128)}, f32[2048,512]{1,0:T(8,128)}, bf16[2,128,512]{2,1,0:T(8,128)(2,1)}, bf16[2,64...) custom-call(bf16[2,20,4,256,128]{4,3,2,1,0:T(8,128)(2,1)} %bitcast.7, ...), custom_call_target="tpu_custom_call" | custom-call | tf_op jit(solution)/shard_map/widen_gradients/pallas_call | solution.py:834

commit v9 on v8

--- a/solution.py
+++ b/solution.py
@@ -712,12 +712,14 @@
             next(chunks[0][i // 2])
     put_products(4, [(s.mlow, s.dwq), (s.t, s.dwk)])
     next(chunks[0][2])
+    put_products(6, [(s.t, s.dwv), (s.wo, s.gup)])
+    next(chunks[1][0])
     for _ in range(FF // FCHUNK):
         next(last_step)
-    put_products(6, [(s.t, s.dwv), (s.wo, s.gup)])
     for i in range(4):
         put(8 + i, dot_tn(s.n2[:, cut], s.gul[:, i * D : (i + 1) * D]))
-    go(1)
+        if i % 2:
+            next(chunks[1][1 + i // 2])
     together(last_step)
     results((3,), results_start)
     put_products(12, [(s.n1, s.dcq), (s.mlow, s.dck), (s.mlow, s.dcv), (s.co, s.gbl)])

time: 109 us -> 109 us (level)
  no operation moved by 1% of the time
where the time goes in v9:
time: 109 us
  Pallas kernels  108 us (99%)
    pallas_call x1, Pallas kernels, run_fused(): pl.pallas_call(fused_kernel, out_shape=(jax.ShapeDtypeStruct((2, FLAT, LA...  95.5 us
    pallas_call x1, Pallas kernels, run_widen(): pl.pallas_call(widen_kernel, out_shape=(jax.ShapeDtypeStruct((12, D, D),...  12.5 us

profile of v9, /device:TPU:1, one launch (start us, length us, event | category | flops | bytes accessed | tf_op | source)
XLA Modules:
  0.0 108.8 jit_solution(16228285682334372449)
XLA Ops:
  0.6 95.5 %layer_and_sums.1 = (bf16[2,20480,128]{2,1,0:T(8,128)(2,1)}, bf16[2,128,512]{2,1,0:T(8,128)(2,1)}, bf16[2,64,512]{2,1,0:T(8,128)(2,1)}, bf16[2,128,512]{2,1,0:T(...) custom-call(bf16[2,128,512]{2,1,0:T(8,128)(2,1)} %tok_ref.1, bf16[2,128,512]{2,1,0:T(8,128)(2,1)} %ocot_ref.1, ...), custom_call_target="tpu_custom_call" | custom-call | tf_op jit(solution)/shard_map/layer_and_sums/pallas_call | solution.py:775
  96.2 12.5 %widen_gradients.1 = (f32[12,512,512]{2,1,0:T(8,128)}, f32[512,2048]{1,0:T(8,128)}, f32[2048,512]{1,0:T(8,128)}, bf16[2,128,512]{2,1,0:T(8,128)(2,1)}, bf16[2,64...) custom-call(bf16[2,20,4,256,128]{4,3,2,1,0:T(8,128)(2,1)} %bitcast.7, ...), custom_call_target="tpu_custom_call" | custom-call | tf_op jit(solution)/shard_map/widen_gradients/pallas_call | solution.py:836
